TPU v7x, 128 devices: a whole 4x4x4 slice. The times are simulated.
128 devices in a mesh: dom: 16 (over y_lo, z, core), side: 4 (over x), rep: 2 (over y_hi).
Axes of the slice: x: 4, y: 4 (y_hi: 2, y_lo: 2; y = y_hi * 2 + y_lo), z: 4, core: 2. Of those that a mesh axis runs over, the one named last changes fastest.
Arguments:
- embeddings: bfloat16 [65536, 400], P('dom')
- relation: float32 [1345, 400], replicated, may hold values from 0.5 to 1.5
- source_ids: int32 [16, 4, 2, 8192], P('dom', 'side', 'rep'), may hold values from 0 to 4095
- relation_ids: int32 [16, 4, 2, 8192], P('dom', 'side', 'rep'), may hold values from 0 to 1344
- target_ids: int32 [16, 4, 2, 8192], P('dom', 'side', 'rep'), may hold values from 0 to 4095
- negative_ids: int32 [16, 4, 2, 8, 1000], P('dom', 'side', 'rep'), may hold values from 0 to 4095
- edge_counts: int32 [16, 4, 2], P('dom', 'side', 'rep'), may hold values from 1024 to 8192, as said below
- dirty: int32 [65536], P('dom'), may hold values 0 or 1
Outputs:
- updated: bfloat16 [65536, 400], P('dom')
- relation_grad: float32 [1345, 400], replicated
- checkpoint: bfloat16 [65536, 400], P('dom')
Inputs may be any that keep to these rules, and one draw needn't show every extreme that they name: `edge_counts`: some list has exactly 8192 live slots in every draw.
All inputs are finite; a program needn't handle non-finite values. No bound on the sum of `dirty` on one device may be relied on, other than what follows from the above.
Results may differ from a plain program's by a relative error of at most 0.0077.
Values may be sent and summed in bfloat16 or wider, within the bound.
No kernel may reach another device: no remote copies, remote signals or barrier semaphores. Data moves between devices by JAX's collectives and lax.ppermute only.
A program may use at most 128 MiB of HBM per device.

v0:
```python
import jax
import jax.numpy as jnp
from jax import lax
from jax.sharding import PartitionSpec as P

SPAN = 1024


def from_behind(shard, axis, by):
    count = lax.axis_size(axis)
    return lax.ppermute(shard, axis, [(i, (i + by) % count) for i in range(count)])


def block_grads(slab, dst_slab, relation, src, rel_ids, dst, negs, live, acc):
    gsrc, gdst, grel = acc
    erows = slab[src]
    rrows = relation[rel_ids]
    left = (erows.astype(jnp.float32) * rrows).astype(jnp.bfloat16)
    drows = dst_slab[dst].astype(jnp.float32)
    nrows = dst_slab[negs]
    positive = jnp.sum(left.astype(jnp.float32) * drows, axis=1)
    negative = lax.dot_general(
        left, nrows, (((1,), (1,)), ((), ())), preferred_element_type=jnp.float32
    )
    top = jnp.maximum(positive, jnp.max(negative, axis=1))
    e_pos = jnp.exp(positive - top)
    e_neg = jnp.exp(negative - top[:, None])
    total = e_pos + jnp.sum(e_neg, axis=1)
    d_pos = live * (e_pos / total - 1.0)
    d_neg = (live[:, None] * e_neg / total[:, None]).astype(jnp.bfloat16)
    d_left = d_pos[:, None] * drows + jnp.dot(d_neg, nrows, preferred_element_type=jnp.float32)
    gsrc = gsrc.at[src].add(d_left * rrows)
    grel = grel.at[rel_ids].add(d_left * erows.astype(jnp.float32))
    gdst = gdst.at[dst].add(d_pos[:, None] * left.astype(jnp.float32))
    neg_part = lax.dot_general(
        d_neg, left, (((0,), (0,)), ((), ())), preferred_element_type=jnp.float32
    )
    gdst = gdst.at[negs].add(neg_part)
    return (gsrc, gdst, grel)


def run_block(slab, dst_slab, relation, src_all, rid_all, dst_all, neg_all, count, blk, acc):
    first = blk * SPAN
    src = lax.dynamic_slice_in_dim(src_all, first, SPAN, 0)
    rid = lax.dynamic_slice_in_dim(rid_all, first, SPAN, 0)
    dst = lax.dynamic_slice_in_dim(dst_all, first, SPAN, 0)
    negs = lax.dynamic_index_in_dim(neg_all, blk, 0, keepdims=False)
    live = (first + jnp.arange(SPAN, dtype=jnp.int32) < count).astype(jnp.float32)
    return block_grads(slab, dst_slab, relation, src, rid, dst, negs, live, acc)


def local(
    embeddings, relation, source_ids, relation_ids, target_ids, negative_ids, edge_counts, dirty
):
    rows, width = embeddings.shape
    dst_slab = from_behind(embeddings, "dom", -1)
    init = (
        jnp.zeros((rows, width), jnp.float32),
        jnp.zeros((rows, width), jnp.float32),
        jnp.zeros(relation.shape, jnp.float32),
    )
    count = edge_counts[0, 0, 0]
    nblocks = (count + SPAN - 1) // SPAN

    def own_step(blk, acc):
        return run_block(
            embeddings,
            dst_slab,
            relation,
            source_ids[0, 0, 0],
            relation_ids[0, 0, 0],
            target_ids[0, 0, 0],
            negative_ids[0, 0, 0],
            count,
            blk,
            acc,
        )

    gsrc, gdst, grel = lax.fori_loop(0, nblocks, own_step, init)
    relation_grad = lax.psum(grel, ("dom", "side", "rep"))
    returned = from_behind(gdst, "dom", 1)
    row_grad = lax.psum(gsrc + returned, ("side", "rep"))
    updated = (embeddings.astype(jnp.float32) - 0.5 * row_grad).astype(jnp.bfloat16)
    checkpoint = jnp.where(dirty[:, None] == 1, updated, jnp.zeros_like(updated))
    return (updated, relation_grad, checkpoint)


def solution(mesh):
    placed = (
        P("dom", None),
        P(),
        P("dom", "side", "rep", None),
        P("dom", "side", "rep", None),
        P("dom", "side", "rep", None),
        P("dom", "side", "rep", None, None),
        P("dom", "side", "rep"),
        P("dom"),
    )
    return jax.shard_map(
        local,
        mesh=mesh,
        in_specs=placed,
        out_specs=(P("dom", None), P(), P("dom", None)),
        check_vma=False,
    )
```

profile of v0, /device:TPU:96, one launch (start us, length us, event | category | flops | bytes accessed | tf_op | source)
XLA Modules:
  0.0 1501.8 jit_solution(2388914290056405518)
XLA Ops:
  7.9 6.0 copy.43
  13.9 3.3 copy.44
  17.2 26.5 %collective-permute-done = bf16[4096,400]{0,1:T(8,128)(2,1)S(1)} collective-permute-done((bf16[4096,400]{0,1:T(8,128)(2,1)}, bf16[4096,400]{0,1:T(8,128)(2,1)S(1)}, u32[]{:S(2)}, u32[]{:S(2)}) %collective-permute-start) | collective-permute-done | bytes 3276832 | tf_op jit(solution)/shard_map/ppermute | solution.py:11
  43.8 4.9 copy.45
  49.1 4.3 broadcast.148.clone
  53.4 4.3 broadcast.148
  57.6 567.7 %while.16 = (s32[]{:T(128)}, f32[4096,400]{1,0:T(8,128)}, f32[4096,400]{1,0:T(8,128)}, f32[1345,400]{1,0:T(8,128)S(1)}, s32[]{:T(128)}, /*index=5*/s32[1,1,1,819...) while((s32[]{:T(128)}, f32[4096,400]{1,0:T(8,128)}, ...), condition=%wide.region_8.9_spmd, body=%wide.region_0.8_spmd.sunk | while | flops 2472565248 | bytes 100216768 | solution.py:79
  60.5 7.8 gather_fusion.3
  68.4 7.8 gather_fusion.2
  78.4 7.8 gather_fusion
  88.5 7.0 gather_fusion.1
  118.7 2.9 copy.61
  121.6 8.2 scatter_fusion.3
  129.8 13.8 scatter_fusion.1
  143.6 13.8 scatter_fusion.2
  157.4 13.8 scatter_fusion
  174.1 7.8 gather_fusion.3
  181.9 7.8 gather_fusion.2
  192.0 7.8 gather_fusion
  202.0 7.0 gather_fusion.1
  218.6 2.9 convert_multiply_fusion.7
  232.2 2.9 copy.61
  235.1 8.2 scatter_fusion.3
  243.3 13.8 scatter_fusion.1
  257.1 13.8 scatter_fusion.2
  270.9 13.8 scatter_fusion
  287.6 7.8 gather_fusion.3
  295.4 7.8 gather_fusion.2
  305.5 7.8 gather_fusion
  315.5 7.0 gather_fusion.1
  332.1 2.9 convert_multiply_fusion.7
  345.7 2.9 copy.61
  348.6 8.2 scatter_fusion.3
  356.9 13.8 scatter_fusion.1
  370.6 13.8 scatter_fusion.2
  384.4 13.8 scatter_fusion
  401.1 7.8 gather_fusion.3
  409.0 7.8 gather_fusion.2
  419.0 7.8 gather_fusion
  429.1 7.0 gather_fusion.1
  459.3 2.9 copy.61
  462.2 8.2 scatter_fusion.3
  470.4 13.8 scatter_fusion.1
  484.2 13.8 scatter_fusion.2
  498.0 13.8 scatter_fusion
  514.7 7.8 gather_fusion.3
  522.5 7.8 gather_fusion.2
  532.5 7.8 gather_fusion
  542.6 7.0 gather_fusion.1
  559.2 2.9 convert_multiply_fusion.7
  572.8 2.9 copy.61
  575.7 8.2 scatter_fusion.3
  583.9 13.8 scatter_fusion.1
  597.7 13.8 scatter_fusion.2
  611.5 13.8 scatter_fusion
  625.3 8.6 copy.46
  633.9 117.3 %collective-permute-start.1 = (f32[4096,400]{0,1:T(8,128)}, f32[4096,400]{0,1:T(8,128)}, u32[]{:S(2)}, u32[]{:S(2)}) collective-permute-start(f32[4096,400]{0,1:T(8,128)} %copy.46), channel_id=1, source_target_pairs={{0,8},{8,16},{16,24},{24,32},{32,40},{40,48},{48,56},{56,64},{64,7... | collective-permute-start | bytes 19660808 | tf_op jit(solution)/shard_map/ppermute | solution.py:11
  751.2 8.6 copy.47
  759.8 288.3 %collective-permute-done.1 = f32[4096,400]{0,1:T(8,128)} collective-permute-done((f32[4096,400]{0,1:T(8,128)}, f32[4096,400]{0,1:T(8,128)}, u32[]{:S(2)}, u32[]{:S(2)}) %collective-permute-start.1) | collective-permute-done | bytes 6553632 | tf_op jit(solution)/shard_map/ppermute | solution.py:11
  1048.1 8.9 add.146
  1059.8 272.5 %all-reduce.3.cloned.1.call-done = f32[4096,400]{0,1:T(8,128)} async-done(((f32[4096,400]{0,1:T(8,128)}), f32[4096,400]{0,1:T(8,128)}) %all-reduce.3.cloned.1.call-update) | async-done | bytes 6553616 | tf_op jit(solution)/shard_map/psum | solution.py:82
  1332.3 8.2 broadcast_select_fusion
  1340.6 151.3 %all-reduce.5.cloned.1.call-done = f32[1345,400]{0,1:T(8,128)} async-done(((f32[1345,400]{0,1:T(8,128)}), f32[1345,400]{0,1:T(8,128)}) %all-reduce.5.cloned.1.call-update) | async-done | bytes 2152016 | tf_op jit(solution)/shard_map/psum | solution.py:80
  1491.8 3.1 copy.81
  (167 shorter events, 146.5 us)
Async XLA Ops:
  7.2 1325.2 %all-reduce.3.cloned.1.call-start = ((), (), s32[]{:S(2)}) async-start(), calls=%async_computation | async-start | bytes 13107200 | tf_op jit(solution)/shard_map/psum | solution.py:82
  7.2 36.6 %collective-permute-start = (bf16[4096,400]{0,1:T(8,128)(2,1)}, bf16[4096,400]{0,1:T(8,128)(2,1)S(1)}, u32[]{:S(2)}, u32[]{:S(2)}) collective-permute-start(bf16[4096,400]{0,1:T(8,128)(2,1)} %param.10), channel_id=1, source_target_pairs={{0,120},{8,0},{16,8},{24,16},{32,24},{40,32},{48,40},{56,48},{64,5... | collective-permute-start | bytes 9830408 | tf_op jit(solution)/shard_map/ppermute | solution.py:11
  98.3 2.4 copy-start.3
  100.6 7.3 copy-start.4
  103.2 1.4 copy-start
  103.2 1.6 copy-start.1
  103.2 1.9 copy-start.2
  211.8 2.4 copy-start.3
  214.2 7.3 copy-start.4
  216.7 1.4 copy-start
  216.7 1.6 copy-start.1
  216.7 1.9 copy-start.2
  325.3 2.4 copy-start.3
  327.7 7.3 copy-start.4
  330.2 1.4 copy-start
  330.3 1.6 copy-start.1
  330.3 1.9 copy-start.2
  438.9 2.4 copy-start.3
  441.2 7.3 copy-start.4
  443.8 1.4 copy-start
  443.8 1.6 copy-start.1
  443.8 1.9 copy-start.2
  552.4 2.4 copy-start.3
  554.8 7.3 copy-start.4
  557.3 1.4 copy-start
  557.3 1.6 copy-start.1
  557.3 1.9 copy-start.2
  633.9 414.2 %collective-permute-start.1 = (f32[4096,400]{0,1:T(8,128)}, f32[4096,400]{0,1:T(8,128)}, u32[]{:S(2)}, u32[]{:S(2)}) collective-permute-start(f32[4096,400]{0,1:T(8,128)} %copy.46), channel_id=1, source_target_pairs={{0,8},{8,16},{16,24},{24,32},{32,40},{40,48},{48,56},{56,64},{64,7... | collective-permute-start | bytes 19660808 | tf_op jit(solution)/shard_map/ppermute | solution.py:11
  1057.0 0.7 copy-start.5
  1057.0 434.9 %all-reduce.5.cloned.1.call-start = ((), (), s32[]{:S(2)}) async-start(), calls=%async_computation.1 | async-start | bytes 4505600 | tf_op jit(solution)/shard_map/psum | solution.py:80
Sparse Core Ops, SparseCore 0:
  1057.1 275.1 all-reduce.2
  1337.7 154.0 all-reduce.4
where the time goes:
time: 1510 us; the launch traced here: 1500 us
  waiting for transfers between devices  739 us (49%)
  other arithmetic  315 us (21%)
  local copies, waits for them, and re-layouts  283 us (19%)
  starting transfers between devices  117 us (8%)
  matrix products  33.1 us (2%)
    ppermute x2, waiting for transfers between devices, from_behind(): lax.ppermute(shard, axis, [(i, (i + by) % count) for i in range(count)])  315 us
    psum x1, waiting for transfers between devices, local(): row_grad = lax.psum(gsrc + returned, ('side', 'rep'))  273 us
    psum x1, waiting for transfers between devices, local(): relation_grad = lax.psum(grel, ('dom', 'side', 'rep'))  151 us
    ppermute x2, starting transfers between devices, from_behind(): lax.ppermute(shard, axis, [(i, (i + by) % count) for i in range(count)])  117 us
    scatter-add x5, other arithmetic, block_grads(): gsrc = gsrc.at[src].add(d_left * rrows)  69 us
    scatter-add x5, other arithmetic, block_grads(): gdst = gdst.at[dst].add(d_pos[:, None] * left.astype(jnp.float32))  69 us
    scatter-add x5, other arithmetic, block_grads(): gdst = gdst.at[negs].add(neg_part)  69 us
    gather x10, local copies, waits for them, and re-layouts, block_grads(): drows = dst_slab[dst].astype(jnp.float32)  50.2 us
  transfers between devices with their start and end apart: 4, of which 4 were waited for; matrix products, arithmetic and copies ran while one was open for 2% of the time, Pallas kernels for 0%

commit v1 on v0

v1 whole, which is shorter than its diff:
```python
import functools

import jax
import jax.numpy as jnp
from jax import lax
from jax.experimental import pallas as pl
from jax.experimental.pallas import tpu as pltpu
from jax.sharding import PartitionSpec as P

SPAN = 1024
LANES = 128
GROUPS = 4
REST = 16
FLAT = SPAN * GROUPS
CHUNK = 256
PIECES = 8
VMEM = 61 * 2**20

f32 = jnp.float32
bf16 = jnp.bfloat16


def shifted(x, axis, by):
    count = lax.axis_size(axis)
    return lax.ppermute(x, axis, [(i, (i + by) % count) for i in range(count)])


def row_of(index):
    return pl.ds(pl.multiple_of(index, GROUPS), GROUPS)


def slot_of(base, k):
    return pl.ds(base + (k // 8) * 8 * GROUPS + k % 8, GROUPS, stride=8)


def tiles(x):
    n = x.shape[0] // GROUPS
    x = x.reshape(n // 8, GROUPS, 8, LANES)
    return [x[:, c].reshape(n, LANES) for c in range(GROUPS)]


def untiles(cols):
    n = cols[0].shape[0]
    x = jnp.concatenate([c.reshape(n // 8, 1, 8, LANES) for c in cols], axis=1)
    return x.reshape(n * GROUPS, LANES)


def fill_rows(x, table, first, n):
    x = x.astype(f32)
    for c in range(GROUPS):
        part = x[:, c * LANES : min((c + 1) * LANES, x.shape[1])]
        if part.shape[1] < LANES:
            part = jnp.concatenate(
                [part, jnp.zeros((n, LANES - part.shape[1]), f32)], axis=1
            )
        table[pl.ds(first * GROUPS + c, n, stride=GROUPS), :] = part


def load_table(src_hbm, raw, sems, table):
    rows = src_hbm.shape[0]
    part = rows // 4
    copies = [
        pltpu.make_async_copy(
            src_hbm.at[pl.ds(i * part, part)], raw.at[pl.ds(i * part, part)], sems.at[i]
        )
        for i in range(4)
    ]
    for c in copies:
        c.start()
    for i in range(4):
        copies[i].wait()

        @pl.loop(0, part // 64)
        def _(q):
            first = pl.multiple_of(i * part + q * 64, 64)
            fill_rows(raw[pl.ds(first, 64), :], table, first, 64)


def edge_rows_kernel(count, src_i, rid_i, emb_hbm, rel_ref, e_out, r_out, ts, tr, raw, eb, rb, lsem, sems):
    load_table(emb_hbm, raw, lsem, ts)
    nrel = rel_ref.shape[0]
    whole = nrel // 64

    @pl.loop(0, whole)
    def _(q):
        first = pl.multiple_of(q * 64, 64)
        fill_rows(rel_ref[pl.ds(first, 64), :], tr, first, 64)

    for i in range(whole * 64, nrel):
        fill_rows(rel_ref[i : i + 1, :], tr, i, 1)

    nblocks = (count[0] + SPAN - 1) // SPAN

    def copies(blk, slot):
        return (
            pltpu.make_async_copy(eb.at[slot], e_out.at[blk], sems.at[slot, 0]),
            pltpu.make_async_copy(rb.at[slot], r_out.at[blk], sems.at[slot, 1]),
        )

    def step(blk, _):
        slot = lax.rem(blk, 2)

        @pl.when(blk >= 2)
        def _():
            for c in copies(blk - 2, slot):
                c.wait()

        es, rs = eb.at[slot], rb.at[slot]

        @pl.loop(0, SPAN // 16)
        def _(q):
            base = pl.multiple_of(q * 16 * GROUPS, 64)
            for k in range(16):
                j = blk * SPAN + q * 16 + k
                es[slot_of(base, k), :] = ts[row_of(src_i[j]), :]
                rs[slot_of(base, k), :] = tr[row_of(rid_i[j]), :]

        for c in copies(blk, slot):
            c.start()
        return 0

    lax.fori_loop(0, nblocks, step, 0)

    @pl.when(nblocks >= 2)
    def _():
        for c in copies(nblocks - 2, lax.rem(nblocks, 2)):
            c.wait()

    for c in copies(nblocks - 1, lax.rem(nblocks + 1, 2)):
        c.wait()


def write_piece(first, n, load, stage):
    for c in range(GROUPS - 1):
        stage[c * n : (c + 1) * n, :] = load(c, first, n).astype(stage.dtype)
    part = n // 8
    rest = load(GROUPS - 1, first, part)
    for k in range(1, 8):
        rest = rest + pltpu.roll(load(GROUPS - 1, first + k * part, part), k * REST, 1)
    stage[3 * n : 3 * n + part, :] = rest.astype(stage.dtype)


def block_kernel(
    nneg, count, src_i, rid_i, dst_i, neg_i, dst_hbm, e_hbm, r_hbm,
    gdst_out, gsrc_out, grel_out,
    td, asrc, adst, aneg, arel, raw, eb, rb, db, nb, lb, nbb, dn, stage, rstage, lsem, sems, osem,
):
    total = count[0]
    nblocks = (total + SPAN - 1) // SPAN

    def fetches(blk, slot):
        return (
            pltpu.make_async_copy(e_hbm.at[blk], eb.at[slot], sems.at[slot, 0]),
            pltpu.make_async_copy(r_hbm.at[blk], rb.at[slot], sems.at[slot, 1]),
        )

    for c in fetches(0, 0):
        c.start()
    load_table(dst_hbm, raw, lsem, td)
    for acc in (asrc, adst, aneg, arel):
        n = acc.shape[0] // 8

        @pl.loop(0, n // 16)
        def _(q):
            acc[pl.ds(pl.multiple_of(q * LANES, LANES), LANES), :] = jnp.zeros((LANES, LANES), f32)

        if n % 16:
            acc[(n // 16) * LANES :, :] = jnp.zeros((acc.shape[0] - (n // 16) * LANES, LANES), f32)

    def step(blk, _):
        slot = lax.rem(blk, 2)

        @pl.when(blk + 1 < nblocks)
        def _():
            for c in fetches(blk + 1, 1 - slot):
                c.start()

        first = blk * SPAN
        es, rs = eb.at[slot], rb.at[slot]

        @pl.loop(0, SPAN // 16)
        def _(q):
            base = pl.multiple_of(q * 16 * GROUPS, 64)
            for k in range(16):
                j = first + q * 16 + k
                db[slot_of(base, k), :] = td[row_of(dst_i[j]), :]
                nb[slot_of(base, k), :] = td[row_of(neg_i[j]), :]

        for ch in range(SPAN // CHUNK):
            cols = tiles(nb[ch * CHUNK * GROUPS : (ch + 1) * CHUNK * GROUPS, :])
            for c in range(GROUPS):
                nbb[ch * CHUNK : (ch + 1) * CHUNK, c * LANES : (c + 1) * LANES] = cols[c].astype(bf16)

        for c in fetches(blk, slot):
            c.wait()

        @pl.loop(0, SPAN // CHUNK)
        def _(ch):
            r0 = pl.multiple_of(ch * CHUNK, CHUNK)
            flat = pl.ds(pl.multiple_of(ch * CHUNK * GROUPS, CHUNK * GROUPS), CHUNK * GROUPS)
            e = tiles(es[flat, :])
            r = tiles(rs[flat, :])
            d = tiles(db[flat, :])
            left = [(e[c] * r[c]).astype(bf16) for c in range(GROUPS)]
            leftf = [x.astype(f32) for x in left]
            prod = leftf[0] * d[0]
            for c in range(1, GROUPS):
                prod = prod + leftf[c] * d[c]
            positive = jnp.sum(prod, axis=1, keepdims=True)
            lc = jnp.concatenate(left, axis=1)
            lb[pl.ds(r0, CHUNK), :] = lc
            negative = lax.dot_general(
                lc, nbb[...], (((1,), (1,)), ((), ())), preferred_element_type=f32
            )
            lane = lax.broadcasted_iota(jnp.int32, negative.shape, 1)
            negative = jnp.where(lane < nneg, negative, -jnp.inf)
            top = jnp.maximum(positive, jnp.max(negative, axis=1, keepdims=True))
            e_pos = jnp.exp(positive - top)
            e_neg = jnp.exp(negative - top)
            z = e_pos + jnp.sum(e_neg, axis=1, keepdims=True)
            row = lax.broadcasted_iota(jnp.int32, (CHUNK, 1), 0) + (first + r0)
            live = jnp.where(row < total, 1.0, 0.0).astype(f32)
            inv = 1.0 / z
            d_pos = live * (e_pos * inv - 1.0)
            d_neg = (e_neg * (live * inv)).astype(bf16)
            dn[pl.ds(r0, CHUNK), :] = d_neg
            dl = jnp.dot(d_neg, nbb[...], preferred_element_type=f32)
            x = [d_pos * d[c] + dl[:, c * LANES : (c + 1) * LANES] for c in range(GROUPS)]
            db[flat, :] = untiles([d_pos * leftf[c] for c in range(GROUPS)])
            es[flat, :] = untiles([x[c] * e[c] for c in range(GROUPS)])
            rs[flat, :] = untiles([x[c] * r[c] for c in range(GROUPS)])

        for ch in range(SPAN // CHUNK):
            part = lax.dot_general(
                dn[:, ch * CHUNK : (ch + 1) * CHUNK], lb[...], (((0,), (0,)), ((), ())),
                preferred_element_type=f32,
            )
            nb[ch * CHUNK * GROUPS : (ch + 1) * CHUNK * GROUPS, :] = untiles(
                [part[:, c * LANES : (c + 1) * LANES] for c in range(GROUPS)]
            )

        @pl.loop(0, SPAN // 16)
        def _(q):
            base = pl.multiple_of(q * 16 * GROUPS, 64)
            for k in range(16):
                j = first + q * 16 + k
                at = slot_of(base, k)
                for acc, idx, val in ((asrc, src_i, rs), (adst, dst_i, db), (aneg, neg_i, nb), (arel, rid_i, es)):
                    row = row_of(idx[j])
                    acc[row, :] = acc[row, :] + val[at, :]

        return 0

    lax.fori_loop(0, nblocks, step, 0)

    def emit(load, out, npieces, n, st):
        def copy(j, slot):
            return pltpu.make_async_copy(st.at[slot], out.at[j], osem.at[slot])

        @pl.loop(0, npieces)
        def _(j):
            slot = lax.rem(j, 2)

            @pl.when(j >= 2)
            def _():
                copy(j - 2, slot).wait()

            write_piece(j * n, n, load, st.at[slot])
            copy(j, slot).start()

        for j in (npieces - 2, npieces - 1):
            copy(j, j % 2).wait()

    def rows(acc):
        return lambda c, first, n: acc[pl.ds(first * GROUPS + c, n, stride=GROUPS), :]

    n = asrc.shape[0] // GROUPS // PIECES
    emit(lambda c, f, m: rows(adst)(c, f, m) + rows(aneg)(c, f, m), gdst_out, PIECES, n, stage)
    emit(rows(asrc), gsrc_out, PIECES, n, stage)
    emit(rows(arel), grel_out, grel_out.shape[0], LANES, rstage)


def smem():
    return pl.BlockSpec(memory_space=pltpu.SMEM)


def hbm():
    return pl.BlockSpec(memory_space=pl.ANY)


def edge_rows(count, src, rid, emb, relation):
    nb = src.shape[0] // SPAN
    rows = emb.shape[0]
    nrel = relation.shape[0]
    shape = jax.ShapeDtypeStruct((nb, FLAT, LANES), f32)
    return pl.pallas_call(
        edge_rows_kernel,
        out_shape=(shape, shape),
        in_specs=[smem()] * 3 + [hbm(), pl.BlockSpec(memory_space=pltpu.VMEM)],
        out_specs=(hbm(), hbm()),
        scratch_shapes=[
            pltpu.VMEM((rows * GROUPS, LANES), f32),
            pltpu.VMEM((-(-nrel // 8) * 8 * GROUPS, LANES), f32),
            pltpu.VMEM(emb.shape, bf16),
            pltpu.VMEM((2, FLAT, LANES), f32),
            pltpu.VMEM((2, FLAT, LANES), f32),
            pltpu.SemaphoreType.DMA((4,)),
            pltpu.SemaphoreType.DMA((2, 2)),
        ],
        compiler_params=pltpu.CompilerParams(vmem_limit_bytes=VMEM),
        cost_estimate=pl.CostEstimate(flops=0, bytes_accessed=60_000_000, transcendentals=0),
        name="edge_rows",
    )(count, src, rid, emb, relation)


def edge_blocks(nneg, count, src, rid, dst, neg, dst_slab, e_rows, r_rows, nrel):
    rows = dst_slab.shape[0]
    packed = rows // PIECES * 25 // 8
    relp = -(-nrel // LANES)
    arel = relp * LANES * GROUPS
    grad = jax.ShapeDtypeStruct((PIECES, packed, LANES), bf16)
    return pl.pallas_call(
        functools.partial(block_kernel, nneg),
        out_shape=(grad, grad, jax.ShapeDtypeStruct((relp, LANES * 25 // 8, LANES), f32)),
        in_specs=[smem()] * 5 + [hbm()] * 3,
        out_specs=(hbm(), hbm(), hbm()),
        scratch_shapes=[
            pltpu.VMEM((rows * GROUPS, LANES), f32),
            pltpu.VMEM((rows * GROUPS, LANES), f32),
            pltpu.VMEM((rows * GROUPS, LANES), f32),
            pltpu.VMEM((rows * GROUPS, LANES), f32),
            pltpu.VMEM((arel, LANES), f32),
            pltpu.VMEM(dst_slab.shape, bf16),
            pltpu.VMEM((2, FLAT, LANES), f32),
            pltpu.VMEM((2, FLAT, LANES), f32),
            pltpu.VMEM((FLAT, LANES), f32),
            pltpu.VMEM((FLAT, LANES), f32),
            pltpu.VMEM((SPAN, LANES * GROUPS), bf16),
            pltpu.VMEM((SPAN, LANES * GROUPS), bf16),
            pltpu.VMEM((SPAN, SPAN), bf16),
            pltpu.VMEM((2, packed, LANES), bf16),
            pltpu.VMEM((2, LANES * 25 // 8, LANES), f32),
            pltpu.SemaphoreType.DMA((4,)),
            pltpu.SemaphoreType.DMA((2, 2)),
            pltpu.SemaphoreType.DMA((2,)),
        ],
        compiler_params=pltpu.CompilerParams(vmem_limit_bytes=VMEM),
        name="edge_blocks",
    )(count, src, rid, dst, neg, dst_slab, e_rows, r_rows)


def unpack(x, n):
    part = n // 8
    rest = x[3 * n :]
    cols = jnp.concatenate(
        [rest if k == 0 else pltpu.roll(rest, LANES - k * REST, 1) for k in range(8)], axis=0
    )
    return jnp.concatenate([x[:n], x[n : 2 * n], x[2 * n : 3 * n], cols[:, :REST]], axis=1)


def update_kernel(a_ref, b_ref, emb_ref, out_ref):
    n = emb_ref.shape[0]
    part = n // 8
    g = jnp.sum(a_ref[...].astype(f32), axis=0) + jnp.sum(b_ref[...].astype(f32), axis=0)
    e = emb_ref[...].astype(f32)
    for c in range(GROUPS - 1):
        out_ref[c * n : (c + 1) * n, :] = (
            e[:, c * LANES : (c + 1) * LANES] - 0.5 * g[c * n : (c + 1) * n]
        ).astype(bf16)
    rest = -0.5 * g[3 * n :]
    last = jnp.concatenate([e[:, 3 * LANES :], jnp.zeros((n, LANES - REST), f32)], axis=1)
    for k in range(8):
        x = last[k * part : (k + 1) * part]
        rest = rest + (x if k == 0 else pltpu.roll(x, k * REST, 1))
    out_ref[3 * n :, :] = rest.astype(bf16)


def update(a, b, emb):
    n = emb.shape[0]
    return pl.pallas_call(
        update_kernel,
        out_shape=jax.ShapeDtypeStruct((n * 25 // 8, LANES), bf16),
        compiler_params=pltpu.CompilerParams(vmem_limit_bytes=VMEM),
        name="update",
    )(a, b, emb)


def finish_kernel(x_ref, dirty_ref, up_ref, check_ref):
    n = up_ref.shape[0]
    rows = unpack(x_ref[0].astype(f32), n)
    up_ref[...] = rows.astype(bf16)
    check_ref[...] = jnp.where(dirty_ref[...] == 1, rows, 0.0).astype(bf16)


def finish(x, dirty, width):
    pieces, packed, _ = x.shape
    n = packed * 8 // 25
    out = jax.ShapeDtypeStruct((pieces * n, width), bf16)
    return pl.pallas_call(
        finish_kernel,
        grid=(pieces,),
        in_specs=[
            pl.BlockSpec((1, packed, LANES), lambda i: (i, 0, 0)),
            pl.BlockSpec((n, 1), lambda i: (i, 0)),
        ],
        out_specs=[pl.BlockSpec((n, width), lambda i: (i, 0))] * 2,
        out_shape=(out, out),
        compiler_params=pltpu.CompilerParams(vmem_limit_bytes=VMEM),
        name="finish",
    )(x, dirty)


def relation_kernel(x_ref, out_ref):
    for i in range(x_ref.shape[0]):
        rows = unpack(x_ref[i], LANES)
        n = min(LANES, out_ref.shape[0] - i * LANES)
        out_ref[i * LANES : i * LANES + n, :] = rows[:n]


def relation_out(x, shape):
    return pl.pallas_call(
        relation_kernel,
        out_shape=jax.ShapeDtypeStruct(shape, f32),
        compiler_params=pltpu.CompilerParams(vmem_limit_bytes=VMEM),
        name="relation_out",
    )(x)


def local(
    embeddings, relation, source_ids, relation_ids, target_ids, negative_ids, edge_counts, dirty
):
    rows, width = embeddings.shape
    count = edge_counts.reshape(1)
    nneg = negative_ids.shape[-1]
    src = source_ids.reshape(-1) * GROUPS
    rid = relation_ids.reshape(-1) * GROUPS
    dst = target_ids.reshape(-1) * GROUPS
    neg = (jnp.pad(negative_ids[0, 0, 0], ((0, 0), (0, SPAN - nneg))) * GROUPS).reshape(-1)

    dst_slab = shifted(embeddings, "dom", -1)
    e_rows, r_rows = edge_rows(count, src, rid, embeddings, relation)
    gdst, gsrc, grel = edge_blocks(
        nneg, count, src, rid, dst, neg, dst_slab, e_rows, r_rows, relation.shape[0]
    )

    returned = shifted(gdst, "dom", 1)
    a = lax.all_to_all(gsrc, ("side", "rep"), 0, 0, tiled=True)
    b = lax.all_to_all(returned, ("side", "rep"), 0, 0, tiled=True)
    me = lax.axis_index("side") * lax.axis_size("rep") + lax.axis_index("rep")
    piece = rows // PIECES
    own = lax.dynamic_slice_in_dim(embeddings, me * piece, piece, 0)
    mine = update(a, b, own)
    both = lax.all_gather(mine, "rep")
    gathered = lax.all_gather(both, "side").reshape(PIECES, -1, LANES)
    updated, checkpoint = finish(gathered, dirty[:, None], width)
    relation_grad = relation_out(lax.psum(grel, ("dom", "side", "rep")), relation.shape)
    return (updated, relation_grad, checkpoint)


def solution(mesh):
    placed = (
        P("dom", None),
        P(),
        P("dom", "side", "rep", None),
        P("dom", "side", "rep", None),
        P("dom", "side", "rep", None),
        P("dom", "side", "rep", None, None),
        P("dom", "side", "rep"),
        P("dom"),
    )
    return jax.shard_map(
        local,
        mesh=mesh,
        in_specs=placed,
        out_specs=(P("dom", None), P(), P("dom", None)),
        check_vma=False,
    )
```

time: 1510 us -> 503 us (0.33)
  waiting for transfers between devices: 739 us -> 221 us
  other arithmetic: 315 us -> 1.93 us
  local copies, waits for them, and re-layouts: 283 us -> 34 us
  blocking collectives: 0 us -> 114 us
  starting transfers between devices: 117 us -> 35.2 us
  Pallas kernels: 0 us -> 75.6 us
  matrix products: 33.1 us -> 0 us
    ppermute x2, waiting for transfers between devices: 315 us -> 14.2 us  [shifted(): return lax.ppermute(x, axis, [(i, (i + by) % count) for i in range(count)])]
    scatter-add x20 -> x0, other arithmetic: 248 us -> none  [the longest x5 69 us: block_grads(): gsrc = gsrc.at[src].add(d_left * rrows)]
    psum x2 -> x1, waiting for transfers between devices: 424 us -> 182 us  [local(): lax.psum(grel, ('dom', 'side', 'rep'))]
    gather x35 -> x0, local copies, waits for them, and re-layouts: 189 us -> none  [the longest x10 50.2 us: block_grads(): drows = dst_slab[dst].astype(jnp.float32)]
    all_to_all x0 -> x1, blocking collectives: none -> 102 us  [local(): a = lax.all_to_all(gsrc, ('side', 'rep'), 0, 0, tiled=True)]
    ppermute x2, starting transfers between devices: 117 us -> 30.7 us  [shifted(): return lax.ppermute(x, axis, [(i, (i + by) % count) for i in range(count)])]
    pallas_call x0 -> x5, Pallas kernels: none -> 75.6 us  [the longest x1 48.2 us: edge_blocks(): pl.pallas_call(functools.partial(block_kernel, nneg), out_shape=(grad, gr...]
    mul x15 -> x0, local copies, waits for them, and re-layouts: 42.4 us -> none  [the longest x5 14.4 us: block_grads(): grel = grel.at[rel_ids].add(d_left * erows.astype(jnp.float32))]
  transfers between devices with their start and end apart: 4 -> 5, of which waited for: 4 -> 3; matrix products, arithmetic and copies ran while one was open for 2% -> 4% of each run, Pallas kernels for 0% -> 4%
where the time goes in v1:
time: 503 us; the launch traced here: 498 us
  waiting for transfers between devices  221 us (44%)
  blocking collectives  114 us (23%)
  Pallas kernels  75.6 us (15%)
  starting transfers between devices  35.2 us (7%)
  local copies, waits for them, and re-layouts  34 us (7%)
  between operations  16.2 us (3%)
    psum x1, waiting for transfers between devices, local(): lax.psum(grel, ('dom', 'side', 'rep'))  182 us
    all_to_all x1, blocking collectives, local(): a = lax.all_to_all(gsrc, ('side', 'rep'), 0, 0, tiled=True)  102 us
    pallas_call x1, Pallas kernels, edge_blocks(): pl.pallas_call(functools.partial(block_kernel, nneg), out_shape=(grad, gr...  48.2 us
    ppermute x2, starting transfers between devices, shifted(): return lax.ppermute(x, axis, [(i, (i + by) % count) for i in range(count)])  30.7 us
    unnamed x18, local copies, waits for them, and re-layouts  24.2 us
    all_to_all x1, waiting for transfers between devices, local(): b = lax.all_to_all(returned, ('side', 'rep'), 0, 0, tiled=True)  23.8 us
    ppermute x2, waiting for transfers between devices, shifted(): return lax.ppermute(x, axis, [(i, (i + by) % count) for i in range(count)])  14.2 us
    all_gather x1, blocking collectives, local(): both = lax.all_gather(mine, 'rep')  12.1 us
  transfers between devices with their start and end apart: 5, of which 3 were waited for; matrix products, arithmetic and copies ran while one was open for 4% of the time, Pallas kernels for 4%

profile of v1, /device:TPU:96, one launch (start us, length us, event | category | flops | bytes accessed | tf_op | source)
XLA Modules:
  0.0 497.7 jit_solution(7471957176497872726)
XLA Ops:
  8.0 0.0 copy-start.1
  8.0 0.0 copy-start.2
  8.0 0.0 copy-start
  8.0 0.1 collective-permute-start
  8.1 6.2 %copy.26.emb_hbm = bf16[4096,400]{1,0:T(8,128)(2,1)} copy(bf16[4096,400]{0,1:T(8,128)(2,1)} %param.8) | data formatting | bytes 6553600 | tf_op args[0]
  14.3 0.0 copy-start.3
  15.0 0.0 copy-done.1
  15.0 0.6 broadcast_multiply_fusion.2
  15.6 0.0 copy-done.2
  15.6 0.6 copy.36
  16.2 0.0 copy-done
  16.2 2.2 copy.27.rel_ref
  18.4 0.0 copy-done.3
  18.4 0.6 broadcast_multiply_fusion.1
  19.1 0.0 copy-start.4
  19.1 10.7 %edge_rows.1 = (f32[8,4096,128]{2,1,0:T(8,128)}, f32[8,4096,128]{2,1,0:T(8,128)}) custom-call(s32[1]{0:T(128)} %bitcast.12.count, s32[8192]{0:T(1024)} %bitcast.15, s32[8192]{0:T(1024)} %bitcast.17, bf16[4096,400]{1,0:T(8,128)(2,1)} %copy.26.emb_hbm, f32[1345,400]{1,0:T(8,128)} %copy.27.rel_ref), custom_call_target="tpu_custom_call" | custom-call | bytes 60000000 | tf_op jit(solution)/shard_map/edge_rows/pallas_call | solution.py:296
  29.8 0.0 copy-done.4
  29.8 0.6 broadcast_multiply_fusion
  30.5 14.2 %collective-permute-done = bf16[4096,400]{0,1:T(8,128)(2,1)} collective-permute-done((bf16[4096,400]{0,1:T(8,128)(2,1)}, bf16[4096,400]{0,1:T(8,128)(2,1)}, u32[]{:S(2)}, u32[]{:S(2)}) %collective-permute-start) | collective-permute-done | bytes 3276832 | tf_op jit(solution)/shard_map/ppermute | solution.py:25
  44.6 6.0 %copy.28.dst_hbm = bf16[4096,400]{1,0:T(8,128)(2,1)} copy(bf16[4096,400]{0,1:T(8,128)(2,1)} %collective-permute-done) | data formatting | bytes 6553600 | tf_op jit(solution)/shard_map/ppermute | solution.py:25
  50.6 48.2 %edge_blocks.1 = (bf16[8,1600,128]{2,1,0:T(8,128)(2,1)}, bf16[8,1600,128]{2,1,0:T(8,128)(2,1)}, f32[11,400,128]{2,1,0:T(8,128)}) custom-call(s32[1]{0:T(128)} %bitcast.13.count, s32[8192]{0:T(1024)} %bitcast.16, s32[8192]{0:T(1024)} %bitcast.18, s32[8192]{0:T(1024)} %bitcast.20, s32[8192]{0:T(1024)} %bitcast.19, bf16[4096,400]{1,0:T(8,128)(2,1)} %copy.28.dst_hbm, ...), custom_call_target="tpu_custom_call" | custom-call | tf_op jit(solution)/shard_map/edge_blocks/pallas_call | solution.py:322
  98.8 30.6 %collective-permute-start.1 = (bf16[8,1600,128]{2,1,0:T(8,128)(2,1)}, bf16[8,1600,128]{2,1,0:T(8,128)(2,1)}, u32[]{:S(2)}, u32[]{:S(2)}) collective-permute-start(bf16[8,1600,128]{2,1,0:T(8,128)(2,1)} %get-tuple-element.13), channel_id=1, source_target_pairs={{0,8},{8,16},{16,24},{24,32},{32,40},{40,48},{48,56},{56,64},{64,7... | collective-permute-start | bytes 9830408 | tf_op jit(solution)/shard_map/ppermute | solution.py:25
  129.5 102.0 %all_to_all.10.a_ref = bf16[8,1600,128]{2,1,0:T(8,128)(2,1)} all-to-all(bf16[8,1600,128]{2,1,0:T(8,128)(2,1)} %get-tuple-element.12), channel_id=1, replica_groups=mesh['dom'=16,'side'=4,'rep'=2] {'side','rep'}, dimensions={0} | all-to-all | bytes 6553600 | tf_op jit(solution)/shard_map/all_to_all | solution.py:447
  231.4 0.0 collective-permute-done.1
  231.5 4.5 all-to-all-start.1
  235.9 0.0 all-reduce.3.cloned.1.call-start
  236.0 0.7 all-reduce.3.cloned.1.call-update
  236.7 0.0 all-gather.4.cloned.1.call-start
  236.7 1.9 constant_dynamic-slice_fusion.emb_ref
  238.6 0.0 copy-start.5
  238.6 23.8 %all-to-all-done.1.b_ref = bf16[8,1600,128]{2,1,0:T(8,128)(2,1)} async-done(((bf16[8,1600,128]{2,1,0:T(8,128)(2,1)}), bf16[8,1600,128]{2,1,0:T(8,128)(2,1)}, u32[]{:S(2)}, u32[]{:S(2)}) %all-to-all-start.1) | async-done | bytes 3276832 | tf_op jit(solution)/shard_map/all_to_all | solution.py:448
  262.4 5.0 %update.1 = bf16[1600,128]{1,0:T(8,128)(2,1)} custom-call(bf16[8,1600,128]{2,1,0:T(8,128)(2,1)} %all_to_all.10.a_ref, bf16[8,1600,128]{2,1,0:T(8,128)(2,1)} %all-to-all-done.1.b_ref, bf16[512,400]{1,0:T(8,128)(2,1)} %constant_dynamic-slice_fusion.emb_ref), custom_call_target="tpu_custom_call" | custom-call | tf_op jit(solution)/shard_map/update/pallas_call | solution.py:380
  267.4 12.1 %all-gather = bf16[3200,128]{1,0:T(8,128)(2,1)} all-gather(bf16[1600,128]{1,0:T(8,128)(2,1)} %update.1), channel_id=2, replica_groups=mesh['dom'=16,'side'=4,'rep'=2] {'rep'}, dimensions={0}, use_global_device_ids=true | all-gather | bytes 1228800 | tf_op jit(solution)/shard_map/all_gather | solution.py:453
  279.5 0.0 all-gather.4.cloned.1.call-update
  279.5 0.0 copy-done.5
  279.5 2.0 copy.30.dirty_ref
  281.5 181.9 %all-reduce.3.cloned.1.call-done.x_ref = f32[11,400,128]{2,1,0:T(8,128)} async-done(((f32[11,400,128]{2,1,0:T(8,128)}), f32[11,400,128]{2,1,0:T(8,128)}) %all-reduce.3.cloned.1.call-update) | async-done | bytes 2252816 | tf_op jit(solution)/shard_map/psum | solution.py:456
  463.4 3.5 relation_out.1
  466.9 3.3 copy.32
  470.1 0.0 all-gather.4.cloned.1.call-done.x_ref
  470.1 8.2 %finish.1 = (bf16[4096,400]{1,0:T(8,128)(2,1)}, bf16[4096,400]{1,0:T(8,128)(2,1)}) custom-call(bf16[8,1600,128]{2,1,0:T(8,128)(2,1)} %all-gather.4.cloned.1.call-done.x_ref, s32[4096,1]{1,0:T(8,128)} %copy.30.dirty_ref), custom_call_target="tpu_custom_call" | custom-call | tf_op jit(solution)/shard_map/finish/pallas_call | solution.py:399
  478.3 6.0 %copy.31 = bf16[4096,400]{0,1:T(8,128)(2,1)} copy(bf16[4096,400]{1,0:T(8,128)(2,1)} %get-tuple-element.23) | data formatting | bytes 6553600
  484.2 6.0 %copy.33 = bf16[4096,400]{0,1:T(8,128)(2,1)} copy(bf16[4096,400]{1,0:T(8,128)(2,1)} %get-tuple-element.25) | data formatting | bytes 6553600
  (1 shorter events, 0.0 us)
Async XLA Ops:
  8.0 7.0 %copy-start.1 = (s32[1,1,1,8192]{3,2,1,0:T(1,128)S(1)}, s32[1,1,1,8192]{3,2,1,0:T(1,128)}, u32[]{:S(2)}) copy-start(s32[1,1,1,8192]{3,2,1,0:T(1,128)} %param.10) | copy-start | bytes 98308
  8.0 7.6 %copy-start.2 = (s32[1,1,1,8,1000]{4,3,2,1,0:T(8,128)S(1)}, s32[1,1,1,8,1000]{4,3,2,1,0:T(8,128)}, u32[]{:S(2)}) copy-start(s32[1,1,1,8,1000]{4,3,2,1,0:T(8,128)} %param.13) | copy-start | bytes 96004
  8.0 8.2 %copy-start = (f32[1345,400]{0,1:T(8,128)S(1)}, f32[1345,400]{0,1:T(8,128)}, u32[]{:S(2)}) copy-start(f32[1345,400]{0,1:T(8,128)} %param.9) | copy-start | bytes 6456004
  8.0 36.6 %collective-permute-start = (bf16[4096,400]{0,1:T(8,128)(2,1)}, bf16[4096,400]{0,1:T(8,128)(2,1)}, u32[]{:S(2)}, u32[]{:S(2)}) collective-permute-start(bf16[4096,400]{0,1:T(8,128)(2,1)} %param.8), channel_id=1, source_target_pairs={{0,120},{8,0},{16,8},{24,16},{32,24},{40,32},{48,40},{56,48},{64,5... | collective-permute-start | bytes 9830408 | tf_op jit(solution)/shard_map/ppermute | solution.py:25
  14.3 4.1 copy-start.3
  19.1 10.8 %copy-start.4 = (s32[1,1,1,8192]{3,2,1,0:T(1,128)S(1)}, s32[1,1,1,8192]{3,2,1,0:T(1,128)}, u32[]{:S(2)}) copy-start(s32[1,1,1,8192]{3,2,1,0:T(1,128)} %param.12) | copy-start | bytes 98308
  98.8 132.6 %collective-permute-start.1 = (bf16[8,1600,128]{2,1,0:T(8,128)(2,1)}, bf16[8,1600,128]{2,1,0:T(8,128)(2,1)}, u32[]{:S(2)}, u32[]{:S(2)}) collective-permute-start(bf16[8,1600,128]{2,1,0:T(8,128)(2,1)} %get-tuple-element.13), channel_id=1, source_target_pairs={{0,8},{8,16},{16,24},{24,32},{32,40},{40,48},{48,56},{56,64},{64,7... | collective-permute-start | bytes 9830408 | tf_op jit(solution)/shard_map/ppermute | solution.py:25
  231.5 30.9 %all-to-all-start.1 = ((bf16[8,1600,128]{2,1,0:T(8,128)(2,1)}), bf16[8,1600,128]{2,1,0:T(8,128)(2,1)}, u32[]{:S(2)}, u32[]{:S(2)}) async-start(bf16[8,1600,128]{2,1,0:T(8,128)(2,1)} %collective-permute-done.1), calls=%async_computation.1 | async-start | bytes 6553600 | tf_op jit(solution)/shard_map/all_to_all | solution.py:448
  235.9 227.5 %all-reduce.3.cloned.1.call-start = ((), (), s32[]{:S(2)}) async-start(), calls=%async_computation.2 | async-start | bytes 4505600 | tf_op jit(solution)/shard_map/psum | solution.py:456
  236.7 233.5 %all-gather.4.cloned.1.call-start = ((), (), s32[]{:S(2)}) async-start(), calls=%async_computation.3 | async-start | bytes 4096000 | tf_op jit(solution)/shard_map/all_gather | solution.py:454
  238.6 40.9 %copy-start.5 = (s32[4096]{0:T(1024)S(1)}, s32[4096]{0:T(1024)}, u32[]{:S(2)}) copy-start(s32[4096]{0:T(1024)} %param.15) | copy-start | bytes 49156
Sparse Core Ops, SparseCore 0:
  242.2 221.1 all-reduce.2
Sparse Core Ops, SparseCore 1:
  279.6 85.0 all-gather.3

commit v2 on v1

--- a/solution.py
+++ b/solution.py
@@ -57,23 +57,30 @@
 
 
 def load_table(src_hbm, raw, sems, table):
-    rows = src_hbm.shape[0]
-    part = rows // 4
-    copies = [
-        pltpu.make_async_copy(
-            src_hbm.at[pl.ds(i * part, part)], raw.at[pl.ds(i * part, part)], sems.at[i]
+    part = raw.shape[1]
+    count = src_hbm.shape[0] // part
+
+    def copy(i, slot):
+        return pltpu.make_async_copy(
+            src_hbm.at[pl.ds(pl.multiple_of(i * part, part), part)], raw.at[slot], sems.at[slot]
         )
-        for i in range(4)
-    ]
-    for c in copies:
-        c.start()
-    for i in range(4):
-        copies[i].wait()
+
+    for i in range(2):
+        copy(i, i).start()
+
+    @pl.loop(0, count)
+    def _(i):
+        slot = lax.rem(i, 2)
+        copy(i, slot).wait()
 
         @pl.loop(0, part // 64)
         def _(q):
-            first = pl.multiple_of(i * part + q * 64, 64)
-            fill_rows(raw[pl.ds(first, 64), :], table, first, 64)
+            at = pl.multiple_of(q * 64, 64)
+            fill_rows(raw[slot, pl.ds(at, 64), :], table, i * part + at, 64)
+
+        @pl.when(i + 2 < count)
+        def _():
+            copy(i + 2, slot).start()
 
 
 def edge_rows_kernel(count, src_i, rid_i, emb_hbm, rel_ref, e_out, r_out, ts, tr, raw, eb, rb, lsem, sems):
@@ -140,10 +147,40 @@
     stage[3 * n : 3 * n + part, :] = rest.astype(stage.dtype)
 
 
+def zero(acc):
+    n = acc.shape[0]
+    whole = n // 256
+
+    @pl.loop(0, whole)
+    def _(q):
+        acc[pl.ds(pl.multiple_of(q * 256, 256), 256), :] = jnp.zeros((256, LANES), f32)
+
+    if n % 256:
+        acc[whole * 256 :, :] = jnp.zeros((n - whole * 256, LANES), f32)
+
+
+def add_rows(ops):
+    values = [val[at, :] for _, _, val, at in ops]
+    held = [acc[row, :] for acc, row, _, _ in ops]
+    for (acc, row, _, _), v, h in zip(ops, values, held):
+        acc[row, :] = h + v
+
+
+def plane(accs):
+    def load(c, first, n):
+        at = pl.ds(first * GROUPS + c, n, stride=GROUPS)
+        x = accs[0][at, :]
+        for acc in accs[1:]:
+            x = x + acc[at, :]
+        return x
+
+    return load
+
+
 def block_kernel(
-    nneg, count, src_i, rid_i, dst_i, neg_i, dst_hbm, e_hbm, r_hbm,
-    gdst_out, gsrc_out, grel_out,
-    td, asrc, adst, aneg, arel, raw, eb, rb, db, nb, lb, nbb, dn, stage, rstage, lsem, sems, osem,
+    nneg, count, rid_i, dst_i, neg_i, dst_hbm, e_hbm, r_hbm,
+    grad_out, v_out,
+    td, a0, a1, a2, r0_acc, r1_acc, raw, eb, rb, db, nb, lb, nbb, dn, stage, lsem, sems, vsem, osem,
 ):
     total = count[0]
     nblocks = (total + SPAN - 1) // SPAN
@@ -154,21 +191,21 @@
             pltpu.make_async_copy(r_hbm.at[blk], rb.at[slot], sems.at[slot, 1]),
         )
 
+    def put(blk, slot):
+        return pltpu.make_async_copy(rb.at[slot], v_out.at[blk], vsem.at[slot])
+
     for c in fetches(0, 0):
         c.start()
     load_table(dst_hbm, raw, lsem, td)
-    for acc in (asrc, adst, aneg, arel):
-        n = acc.shape[0] // 8
-
-        @pl.loop(0, n // 16)
-        def _(q):
-            acc[pl.ds(pl.multiple_of(q * LANES, LANES), LANES), :] = jnp.zeros((LANES, LANES), f32)
-
-        if n % 16:
-            acc[(n // 16) * LANES :, :] = jnp.zeros((acc.shape[0] - (n // 16) * LANES, LANES), f32)
+    for acc in (a0, a1, a2, r0_acc, r1_acc):
+        zero(acc)
 
     def step(blk, _):
         slot = lax.rem(blk, 2)
+
+        @pl.when(blk >= 1)
+        def _():
+            put(blk - 1, 1 - slot).wait()
 
         @pl.when(blk + 1 < nblocks)
         def _():
@@ -230,6 +267,8 @@
             es[flat, :] = untiles([x[c] * e[c] for c in range(GROUPS)])
             rs[flat, :] = untiles([x[c] * r[c] for c in range(GROUPS)])
 
+        put(blk, slot).start()
+
         for ch in range(SPAN // CHUNK):
             part = lax.dot_general(
                 dn[:, ch * CHUNK : (ch + 1) * CHUNK], lb[...], (((0,), (0,)), ((), ())),
@@ -239,45 +278,105 @@
                 [part[:, c * LANES : (c + 1) * LANES] for c in range(GROUPS)]
             )
 
+        def scatter(j0, base, n):
+            for t in range(0, n, 3):
+                ks = list(range(t, min(t + 3, n)))
+                at = [slot_of(base, k) for k in ks]
+                copies = (a0, a1, a2)
+                dst = [(copies[i], row_of(dst_i[j0 + k]), db, at[i]) for i, k in enumerate(ks)]
+                neg = [(copies[i], row_of(neg_i[j0 + k]), nb, at[i]) for i, k in enumerate(ks)]
+                rel = [
+                    ((r0_acc, r1_acc)[i % 2], row_of(rid_i[j0 + k]), es, at[i])
+                    for i, k in enumerate(ks)
+                ]
+                add_rows(dst + rel[:2])
+                add_rows(neg + rel[2:])
+
+        @pl.loop(0, SPAN // 24)
+        def _(q):
+            scatter(first + q * 24, pl.multiple_of(q * 24 * GROUPS, 32), 24)
+
+        done = SPAN // 24 * 24
+        scatter(first + done, done * GROUPS, SPAN - done)
+        return 0
+
+    lax.fori_loop(0, nblocks, step, 0)
+    last = nblocks - 1
+    put(last, lax.rem(last, 2)).wait()
+
+    n = td.shape[0] // GROUPS // PIECES
+    m = r0_acc.shape[0] // GROUPS // PIECES
+    packed = n * 25 // 8
+    relp = m * 25 // 8
+    pad = grad_out.shape[1] - packed - relp
+    grad, rel = plane((a0, a1, a2)), plane((r0_acc, r1_acc))
+
+    def fill(j, st):
+        write_piece(j * n, n, grad, st)
+        write_piece(j * m, m, rel, st.at[pl.ds(packed, relp)])
+        if pad:
+            st[packed + relp :, :] = jnp.zeros((pad, LANES), st.dtype)
+
+    emit(fill, grad_out, stage, osem)
+
+
+def emit(fill, out, stage, sem):
+    def copy(j, slot):
+        return pltpu.make_async_copy(stage.at[slot], out.at[j], sem.at[slot])
+
+    @pl.loop(0, PIECES)
+    def _(j):
+        slot = lax.rem(j, 2)
+
+        @pl.when(j >= 2)
+        def _():
+            copy(j - 2, slot).wait()
+
+        fill(j, stage.at[slot])
+        copy(j, slot).start()
+
+    for j in (PIECES - 2, PIECES - 1):
+        copy(j, j % 2).wait()
+
+
+def source_kernel(count, src_i, v_hbm, grad_out, a0, a1, a2, a3, vb, stage, sems, osem):
+    nblocks = (count[0] + SPAN - 1) // SPAN
+    accs = (a0, a1, a2, a3)
+
+    def fetch(blk, slot):
+        return pltpu.make_async_copy(v_hbm.at[blk], vb.at[slot], sems.at[slot])
+
+    fetch(0, 0).start()
+    for acc in accs:
+        zero(acc)
+
+    def step(blk, _):
+        slot = lax.rem(blk, 2)
+
+        @pl.when(blk + 1 < nblocks)
+        def _():
+            fetch(blk + 1, 1 - slot).start()
+
+        fetch(blk, slot).wait()
+        vs = vb.at[slot]
+
         @pl.loop(0, SPAN // 16)
         def _(q):
             base = pl.multiple_of(q * 16 * GROUPS, 64)
-            for k in range(16):
-                j = first + q * 16 + k
-                at = slot_of(base, k)
-                for acc, idx, val in ((asrc, src_i, rs), (adst, dst_i, db), (aneg, neg_i, nb), (arel, rid_i, es)):
-                    row = row_of(idx[j])
-                    acc[row, :] = acc[row, :] + val[at, :]
+            for t in range(0, 16, 4):
+                add_rows(
+                    [
+                        (accs[i], row_of(src_i[blk * SPAN + q * 16 + t + i]), vs, slot_of(base, t + i))
+                        for i in range(4)
+                    ]
+                )
 
         return 0
 
     lax.fori_loop(0, nblocks, step, 0)
-
-    def emit(load, out, npieces, n, st):
-        def copy(j, slot):
-            return pltpu.make_async_copy(st.at[slot], out.at[j], osem.at[slot])
-
-        @pl.loop(0, npieces)
-        def _(j):
-            slot = lax.rem(j, 2)
-
-            @pl.when(j >= 2)
-            def _():
-                copy(j - 2, slot).wait()
-
-            write_piece(j * n, n, load, st.at[slot])
-            copy(j, slot).start()
-
-        for j in (npieces - 2, npieces - 1):
-            copy(j, j % 2).wait()
-
-    def rows(acc):
-        return lambda c, first, n: acc[pl.ds(first * GROUPS + c, n, stride=GROUPS), :]
-
-    n = asrc.shape[0] // GROUPS // PIECES
-    emit(lambda c, f, m: rows(adst)(c, f, m) + rows(aneg)(c, f, m), gdst_out, PIECES, n, stage)
-    emit(rows(asrc), gsrc_out, PIECES, n, stage)
-    emit(rows(arel), grel_out, grel_out.shape[0], LANES, rstage)
+    n = a0.shape[0] // GROUPS // PIECES
+    load = plane(accs)
+    emit(lambda j, st: write_piece(j * n, n, load, st), grad_out, stage, osem)
 
 
 def smem():
@@ -301,10 +400,10 @@
         scratch_shapes=[
             pltpu.VMEM((rows * GROUPS, LANES), f32),
             pltpu.VMEM((-(-nrel // 8) * 8 * GROUPS, LANES), f32),
-            pltpu.VMEM(emb.shape, bf16),
+            pltpu.VMEM((2, 512, emb.shape[1]), bf16),
             pltpu.VMEM((2, FLAT, LANES), f32),
             pltpu.VMEM((2, FLAT, LANES), f32),
-            pltpu.SemaphoreType.DMA((4,)),
+            pltpu.SemaphoreType.DMA((2,)),
             pltpu.SemaphoreType.DMA((2, 2)),
         ],
         compiler_params=pltpu.CompilerParams(vmem_limit_bytes=VMEM),
@@ -313,24 +412,24 @@
     )(count, src, rid, emb, relation)
 
 
-def edge_blocks(nneg, count, src, rid, dst, neg, dst_slab, e_rows, r_rows, nrel):
+def edge_blocks(nneg, count, rid, dst, neg, dst_slab, e_rows, r_rows, nrel):
     rows = dst_slab.shape[0]
     packed = rows // PIECES * 25 // 8
-    relp = -(-nrel // LANES)
-    arel = relp * LANES * GROUPS
-    grad = jax.ShapeDtypeStruct((PIECES, packed, LANES), bf16)
+    relm = -(-nrel // (PIECES * 64)) * 64
+    wire = -(-(packed + relm * 25 // 8) // 16) * 16
+    table = pltpu.VMEM((rows * GROUPS, LANES), f32)
+    rel = pltpu.VMEM((relm * PIECES * GROUPS, LANES), f32)
     return pl.pallas_call(
         functools.partial(block_kernel, nneg),
-        out_shape=(grad, grad, jax.ShapeDtypeStruct((relp, LANES * 25 // 8, LANES), f32)),
-        in_specs=[smem()] * 5 + [hbm()] * 3,
-        out_specs=(hbm(), hbm(), hbm()),
+        out_shape=(
+            jax.ShapeDtypeStruct((PIECES, wire, LANES), bf16),
+            jax.ShapeDtypeStruct(r_rows.shape, f32),
+        ),
+        in_specs=[smem()] * 4 + [hbm()] * 3,
+        out_specs=(hbm(), hbm()),
         scratch_shapes=[
-            pltpu.VMEM((rows * GROUPS, LANES), f32),
-            pltpu.VMEM((rows * GROUPS, LANES), f32),
-            pltpu.VMEM((rows * GROUPS, LANES), f32),
-            pltpu.VMEM((rows * GROUPS, LANES), f32),
-            pltpu.VMEM((arel, LANES), f32),
-            pltpu.VMEM(dst_slab.shape, bf16),
+            table, table, table, table, rel, rel,
+            pltpu.VMEM((2, 512, dst_slab.shape[1]), bf16),
             pltpu.VMEM((2, FLAT, LANES), f32),
             pltpu.VMEM((2, FLAT, LANES), f32),
             pltpu.VMEM((FLAT, LANES), f32),
@@ -338,123 +437,168 @@
             pltpu.VMEM((SPAN, LANES * GROUPS), bf16),
             pltpu.VMEM((SPAN, LANES * GROUPS), bf16),
             pltpu.VMEM((SPAN, SPAN), bf16),
-            pltpu.VMEM((2, packed, LANES), bf16),
-            pltpu.VMEM((2, LANES * 25 // 8, LANES), f32),
-            pltpu.SemaphoreType.DMA((4,)),
+            pltpu.VMEM((2, wire, LANES), bf16),
+            pltpu.SemaphoreType.DMA((2,)),
             pltpu.SemaphoreType.DMA((2, 2)),
+            pltpu.SemaphoreType.DMA((2,)),
             pltpu.SemaphoreType.DMA((2,)),
         ],
         compiler_params=pltpu.CompilerParams(vmem_limit_bytes=VMEM),
         name="edge_blocks",
-    )(count, src, rid, dst, neg, dst_slab, e_rows, r_rows)
-
-
-def unpack(x, n):
+    )(count, rid, dst, neg, dst_slab, e_rows, r_rows)
+
+
+def source_rows(count, src, values, rows):
+    packed = rows // PIECES * 25 // 8
+    table = pltpu.VMEM((rows * GROUPS, LANES), f32)
+    return pl.pallas_call(
+        source_kernel,
+        out_shape=jax.ShapeDtypeStruct((PIECES, packed, LANES), bf16),
+        in_specs=[smem()] * 2 + [hbm()],
+        out_specs=hbm(),
+        scratch_shapes=[
+            table, table, table, table,
+            pltpu.VMEM((2, FLAT, LANES), f32),
+            pltpu.VMEM((2, packed, LANES), bf16),
+            pltpu.SemaphoreType.DMA((2,)),
+            pltpu.SemaphoreType.DMA((2,)),
+        ],
+        compiler_params=pltpu.CompilerParams(vmem_limit_bytes=VMEM),
+        cost_estimate=pl.CostEstimate(flops=0, bytes_accessed=60_000_000, transcendentals=0),
+        name="source_rows",
+    )(count, src, values)
+
+
+def sum_kernel(x_ref, rows_ref, rel_ref):
+    n = rows_ref.shape[0]
+    m = x_ref.shape[1] - n
+    total = jnp.sum(x_ref[...].astype(f32), axis=0)
+    rows_ref[...] = total[:n].astype(bf16)
+    rel_ref[:m, :] = total[n:]
+    if rel_ref.shape[0] > m:
+        rel_ref[m:, :] = jnp.zeros((rel_ref.shape[0] - m, LANES), f32)
+
+
+def sum_pieces(x, packed, relrows):
+    return pl.pallas_call(
+        sum_kernel,
+        out_shape=(
+            jax.ShapeDtypeStruct((packed, LANES), bf16),
+            jax.ShapeDtypeStruct((relrows, LANES), f32),
+        ),
+        compiler_params=pltpu.CompilerParams(vmem_limit_bytes=VMEM),
+        name="sum_pieces",
+    )(x)
+
+
+def across(x, n):
     part = n // 8
-    rest = x[3 * n :]
-    cols = jnp.concatenate(
-        [rest if k == 0 else pltpu.roll(rest, LANES - k * REST, 1) for k in range(8)], axis=0
-    )
-    return jnp.concatenate([x[:n], x[n : 2 * n], x[2 * n : 3 * n], cols[:, :REST]], axis=1)
+    rest = x[3 * n : 3 * n + part].T
+    rest = jnp.concatenate([rest[k * REST : (k + 1) * REST] for k in range(8)], axis=1)
+    return jnp.concatenate([x[:n].T, x[n : 2 * n].T, x[2 * n : 3 * n].T, rest], axis=0)
 
 
 def update_kernel(a_ref, b_ref, emb_ref, out_ref):
-    n = emb_ref.shape[0]
-    part = n // 8
-    g = jnp.sum(a_ref[...].astype(f32), axis=0) + jnp.sum(b_ref[...].astype(f32), axis=0)
-    e = emb_ref[...].astype(f32)
-    for c in range(GROUPS - 1):
-        out_ref[c * n : (c + 1) * n, :] = (
-            e[:, c * LANES : (c + 1) * LANES] - 0.5 * g[c * n : (c + 1) * n]
-        ).astype(bf16)
-    rest = -0.5 * g[3 * n :]
-    last = jnp.concatenate([e[:, 3 * LANES :], jnp.zeros((n, LANES - REST), f32)], axis=1)
-    for k in range(8):
-        x = last[k * part : (k + 1) * part]
-        rest = rest + (x if k == 0 else pltpu.roll(x, k * REST, 1))
-    out_ref[3 * n :, :] = rest.astype(bf16)
+    width, n = emb_ref.shape
+    g = jnp.sum(a_ref[...].astype(f32), axis=0) + b_ref[...].astype(f32)
+    new = (emb_ref[...].astype(f32) - 0.5 * across(g, n)).astype(bf16)
+    for i in range(n // LANES):
+        out_ref[i * width : (i + 1) * width, :] = new[:, i * LANES : (i + 1) * LANES]
 
 
 def update(a, b, emb):
-    n = emb.shape[0]
+    width, n = emb.shape
     return pl.pallas_call(
         update_kernel,
-        out_shape=jax.ShapeDtypeStruct((n * 25 // 8, LANES), bf16),
+        out_shape=jax.ShapeDtypeStruct((width * n // LANES, LANES), bf16),
         compiler_params=pltpu.CompilerParams(vmem_limit_bytes=VMEM),
         name="update",
     )(a, b, emb)
 
 
 def finish_kernel(x_ref, dirty_ref, up_ref, check_ref):
-    n = up_ref.shape[0]
-    rows = unpack(x_ref[0].astype(f32), n)
-    up_ref[...] = rows.astype(bf16)
-    check_ref[...] = jnp.where(dirty_ref[...] == 1, rows, 0.0).astype(bf16)
-
-
-def finish(x, dirty, width):
-    pieces, packed, _ = x.shape
-    n = packed * 8 // 25
-    out = jax.ShapeDtypeStruct((pieces * n, width), bf16)
+    width, n = up_ref.shape
+    for i in range(n // LANES):
+        at = slice(i * LANES, (i + 1) * LANES)
+        x = x_ref[0, i * width : (i + 1) * width, :]
+        up_ref[:, at] = x
+        check_ref[:, at] = jnp.where(dirty_ref[:, at] == 1, x.astype(f32), 0.0).astype(bf16)
+
+
+def finish(x, dirty, width, rows):
+    pieces, wire, _ = x.shape
+    n = rows // pieces
+    out = jax.ShapeDtypeStruct((width, rows), bf16)
     return pl.pallas_call(
         finish_kernel,
         grid=(pieces,),
         in_specs=[
-            pl.BlockSpec((1, packed, LANES), lambda i: (i, 0, 0)),
-            pl.BlockSpec((n, 1), lambda i: (i, 0)),
+            pl.BlockSpec((1, wire, LANES), lambda i: (i, 0, 0)),
+            pl.BlockSpec((1, n), lambda i: (0, i)),
         ],
-        out_specs=[pl.BlockSpec((n, width), lambda i: (i, 0))] * 2,
+        out_specs=[pl.BlockSpec((width, n), lambda i: (0, i))] * 2,
         out_shape=(out, out),
         compiler_params=pltpu.CompilerParams(vmem_limit_bytes=VMEM),
         name="finish",
     )(x, dirty)
 
 
-def relation_kernel(x_ref, out_ref):
-    for i in range(x_ref.shape[0]):
-        rows = unpack(x_ref[i], LANES)
-        n = min(LANES, out_ref.shape[0] - i * LANES)
-        out_ref[i * LANES : i * LANES + n, :] = rows[:n]
-
-
-def relation_out(x, shape):
+def relation_kernel(m, x_ref, out_ref):
+    cols = jnp.concatenate(
+        [across(x_ref[i].astype(f32), m) for i in range(x_ref.shape[0])], axis=1
+    )
+    out_ref[...] = cols[:, : out_ref.shape[1]]
+
+
+def relation_out(x, m, shape):
     return pl.pallas_call(
-        relation_kernel,
+        functools.partial(relation_kernel, m),
         out_shape=jax.ShapeDtypeStruct(shape, f32),
         compiler_params=pltpu.CompilerParams(vmem_limit_bytes=VMEM),
         name="relation_out",
     )(x)
 
 
+def to_all(x, axes, count):
+    return lax.all_to_all(jnp.broadcast_to(x, (count,) + x.shape), axes, 0, 0, tiled=True)
+
+
 def local(
     embeddings, relation, source_ids, relation_ids, target_ids, negative_ids, edge_counts, dirty
 ):
     rows, width = embeddings.shape
+    nrel = relation.shape[0]
+    group = ("side", "rep")
+    doms = lax.axis_size("dom")
     count = edge_counts.reshape(1)
     nneg = negative_ids.shape[-1]
     src = source_ids.reshape(-1) * GROUPS
     rid = relation_ids.reshape(-1) * GROUPS
     dst = target_ids.reshape(-1) * GROUPS
     neg = (jnp.pad(negative_ids[0, 0, 0], ((0, 0), (0, SPAN - nneg))) * GROUPS).reshape(-1)
+    me = lax.axis_index("side") * lax.axis_size("rep") + lax.axis_index("rep")
+    piece = rows // PIECES
+    own = lax.dynamic_slice_in_dim(embeddings.T, me * piece, piece, 1)
 
     dst_slab = shifted(embeddings, "dom", -1)
     e_rows, r_rows = edge_rows(count, src, rid, embeddings, relation)
-    gdst, gsrc, grel = edge_blocks(
-        nneg, count, src, rid, dst, neg, dst_slab, e_rows, r_rows, relation.shape[0]
-    )
-
+    sent, values = edge_blocks(nneg, count, rid, dst, neg, dst_slab, e_rows, r_rows, nrel)
+    got = lax.all_to_all(sent, group, 0, 0, tiled=True)
+    gsrc = source_rows(count, src, values, rows)
+
+    packed = gsrc.shape[1]
+    relrows = -(-(sent.shape[1] - packed) // (8 * doms)) * 8 * doms
+    gdst, rel = sum_pieces(got, packed, relrows)
     returned = shifted(gdst, "dom", 1)
-    a = lax.all_to_all(gsrc, ("side", "rep"), 0, 0, tiled=True)
-    b = lax.all_to_all(returned, ("side", "rep"), 0, 0, tiled=True)
-    me = lax.axis_index("side") * lax.axis_size("rep") + lax.axis_index("rep")
-    piece = rows // PIECES
-    own = lax.dynamic_slice_in_dim(embeddings, me * piece, piece, 0)
-    mine = update(a, b, own)
-    both = lax.all_gather(mine, "rep")
-    gathered = lax.all_gather(both, "side").reshape(PIECES, -1, LANES)
-    updated, checkpoint = finish(gathered, dirty[:, None], width)
-    relation_grad = relation_out(lax.psum(grel, ("dom", "side", "rep")), relation.shape)
-    return (updated, relation_grad, checkpoint)
+    rel = lax.all_to_all(rel.reshape(doms, -1, LANES), "dom", 0, 0, tiled=True)
+    rel = to_all(jnp.sum(rel, axis=0).astype(bf16), "dom", doms).reshape(-1, LANES)
+    a = lax.all_to_all(gsrc, group, 0, 0, tiled=True)
+    mine = update(a, returned, own)
+    every = to_all(jnp.concatenate([mine, rel], axis=0), group, PIECES)
+    updated, checkpoint = finish(every[:, : mine.shape[0]], dirty[None, :], width, rows)
+    relm = -(-nrel // (PIECES * 64)) * 64
+    relation_grad = relation_out(every[:, mine.shape[0] :], relm, (width, nrel))
+    return (updated.T, relation_grad.T, checkpoint.T)
 
 
 def solution(mesh):

time: 503 us -> 393 us (0.78)
  waiting for transfers between devices: 221 us -> 53.3 us
  Pallas kernels: 75.6 us -> 130 us
  blocking collectives: 114 us -> 152 us
  between operations: 16.2 us -> 1.4 us
  starting transfers between devices: 35.2 us -> 21.6 us
  local copies, waits for them, and re-layouts: 34 us -> 25.9 us
    psum x1 -> x0, waiting for transfers between devices: 182 us -> none  [local(): lax.psum(grel, ('dom', 'side', 'rep'))]
    all_to_all x1 -> x2, blocking collectives: 102 us -> 152 us  [the longest x1 92 us: local(): got = lax.all_to_all(sent, group, 0, 0, tiled=True)]
    pallas_call x3 -> x5, Pallas kernels: 56.7 us -> 104 us  [the longest x1 75.6 us: edge_blocks(): pl.pallas_call(functools.partial(block_kernel, nneg), out_shape=(jax.Shap...]
    ppermute x2, starting transfers between devices: 30.7 us -> 0.85 us  [shifted(): return lax.ppermute(x, axis, [(i, (i + by) % count) for i in range(count)])]
    all_to_all x1 -> x3, waiting for transfers between devices: 23.8 us -> 47.7 us  [the longest x1 47.7 us: local(): a = lax.all_to_all(gsrc, group, 0, 0, tiled=True)]
    all_to_all x1 -> x3, starting transfers between devices: 4.47 us -> 20.7 us  [the longest x1 8.83 us: local(): rel = lax.all_to_all(rel.reshape(doms, -1, LANES), 'dom', 0, 0, tiled=True)]
    unnamed x18 -> x19, local copies, waits for them, and re-layouts: 24.2 us -> 11.8 us
    all_gather x1 -> x0, blocking collectives: 12.1 us -> none  [local(): both = lax.all_gather(mine, 'rep')]
  transfers between devices with their start and end apart: 5 -> 5, of which waited for: 3 -> 2; matrix products, arithmetic and copies ran while one was open for 4% -> 3% of each run, Pallas kernels for 4% -> 10%
where the time goes in v2:
time: 393 us; the launch traced here: 388 us
  blocking collectives  152 us (39%)
  Pallas kernels  130 us (33%)
  waiting for transfers between devices  53.3 us (14%)
  local copies, waits for them, and re-layouts  25.9 us (7%)
  starting transfers between devices  21.6 us (5%)
    all_to_all x1, blocking collectives, local(): got = lax.all_to_all(sent, group, 0, 0, tiled=True)  92 us
    pallas_call x1, Pallas kernels, edge_blocks(): pl.pallas_call(functools.partial(block_kernel, nneg), out_shape=(jax.Shap...  75.6 us
    all_to_all x1, blocking collectives, to_all(): lax.all_to_all(jnp.broadcast_to(x, (count,) + x.shape), axes, 0, 0, tiled...  60.5 us
    all_to_all x1, waiting for transfers between devices, local(): a = lax.all_to_all(gsrc, group, 0, 0, tiled=True)  47.7 us
    pallas_call x1, Pallas kernels, edge_rows(): pl.pallas_call(edge_rows_kernel, out_shape=(shape, shape), in_specs=[smem...  19.3 us
    pallas_call x1, Pallas kernels, source_rows(): pl.pallas_call(source_kernel, out_shape=jax.ShapeDtypeStruct((PIECES, pac...  17.5 us
    unnamed x19, local copies, waits for them, and re-layouts  11.8 us
    all_to_all x1, starting transfers between devices, local(): rel = lax.all_to_all(rel.reshape(doms, -1, LANES), 'dom', 0, 0, tiled=True)  8.83 us
  transfers between devices with their start and end apart: 5, of which 2 were waited for; matrix products, arithmetic and copies ran while one was open for 3% of the time, Pallas kernels for 10%

profile of v2, /device:TPU:96, one launch (start us, length us, event | category | flops | bytes accessed | tf_op | source)
XLA Modules:
  0.0 387.6 jit_solution(7627390645796565218)
XLA Ops:
  0.6 0.0 copy-start.3
  0.6 0.0 copy-start.1
  0.7 0.1 collective-permute-start
  0.7 6.1 %copy.14.emb_hbm = bf16[4096,400]{1,0:T(8,128)(2,1)} copy(bf16[4096,400]{0,1:T(8,128)(2,1)} %param.8) | data formatting | bytes 6553600 | tf_op args[0]
  6.9 0.0 copy-start.4
  6.9 0.0 copy-start.5
  7.5 0.0 copy-done.3
  7.5 0.6 broadcast_multiply_fusion.2
  8.2 0.0 copy-done.1
  8.2 2.2 copy.15.rel_ref
  10.3 0.0 copy-done.4
  10.4 0.6 copy.19
  11.0 0.0 copy-done.5
  11.0 0.6 broadcast_multiply_fusion.1
  11.6 0.0 copy-start.6
  11.6 19.3 %edge_rows.1 = (f32[8,4096,128]{2,1,0:T(8,128)}, f32[8,4096,128]{2,1,0:T(8,128)}) custom-call(s32[1]{0:T(128)} %bitcast.18.count, s32[8192]{0:T(1024)} %bitcast.24, s32[8192]{0:T(1024)} %bitcast.26, bf16[4096,400]{1,0:T(8,128)(2,1)} %copy.14.emb_hbm, f32[1345,400]{1,0:T(8,128)} %copy.15.rel_ref), custom_call_target="tpu_custom_call" | custom-call | bytes 60000000 | tf_op jit(solution)/shard_map/edge_rows/pallas_call | solution.py:395
  31.0 0.0 copy-done.6
  31.0 0.6 broadcast_multiply_fusion
  31.6 5.6 %collective-permute-done = bf16[4096,400]{0,1:T(8,128)(2,1)} collective-permute-done((bf16[4096,400]{0,1:T(8,128)(2,1)}, bf16[4096,400]{0,1:T(8,128)(2,1)}, u32[]{:S(2)}, u32[]{:S(2)}) %collective-permute-start) | collective-permute-done | bytes 3276832 | tf_op jit(solution)/shard_map/ppermute | solution.py:25
  37.2 6.1 %copy.16.dst_hbm = bf16[4096,400]{1,0:T(8,128)(2,1)} copy(bf16[4096,400]{0,1:T(8,128)(2,1)} %collective-permute-done) | data formatting | bytes 6553600 | tf_op jit(solution)/shard_map/ppermute | solution.py:25
  43.3 75.6 %edge_blocks.1 = (bf16[8,2208,128]{2,1,0:T(8,128)(2,1)}, f32[8,4096,128]{2,1,0:T(8,128)}) custom-call(s32[1]{0:T(128)} %bitcast.19.count, s32[8192]{0:T(1024)} %bitcast.27, s32[8192]{0:T(1024)} %bitcast.29, s32[8192]{0:T(1024)} %bitcast.28, bf16[4096,400]{1,0:T(8,128)(2,1)} %copy.16.dst_hbm, f32[8,4096,128]{2,1,0:T(8,128)} %get-tuple-element.11.e_hbm, ...), custom_call_target="tpu_custom_call" | custom-call | tf_op jit(solution)/shard_map/edge_blocks/pallas_call | solution.py:422
  118.9 92.0 %all_to_all.25.x_ref = bf16[8,2208,128]{2,1,0:T(8,128)(2,1)} all-to-all(bf16[8,2208,128]{2,1,0:T(8,128)(2,1)} %get-tuple-element.14), channel_id=1, replica_groups=mesh['dom'=16,'side'=4,'rep'=2] {'side','rep'}, dimensions={0} | all-to-all | bytes 9043968 | tf_op jit(solution)/shard_map/all_to_all | solution.py:586
  210.9 3.6 sum_pieces.1
  214.4 8.8 %all-to-all-start.2 = ((f32[16,40,128]{2,1,0:T(8,128)}), f32[16,40,128]{2,1,0:T(8,128)S(1)}, u32[]{:S(2)}, u32[]{:S(2)}) async-start(f32[16,40,128]{2,1,0:T(8,128)} %bitcast.23), calls=%async_computation.2 | async-start | bytes 655360 | tf_op jit(solution)/shard_map/all_to_all | solution.py:593
  223.3 17.5 %source_rows.1 = bf16[8,1600,128]{2,1,0:T(8,128)(2,1)} custom-call(s32[1]{0:T(128)} %bitcast.20.count, s32[8192]{0:T(1024)} %bitcast.25, f32[8,4096,128]{2,1,0:T(8,128)} %get-tuple-element.13.v_hbm), custom_call_target="tpu_custom_call" | custom-call | bytes 60000000 | tf_op jit(solution)/shard_map/source_rows/pallas_call | solution.py:454
  240.8 0.0 copy-start.7
  240.8 0.0 all-to-all-done.2
  240.8 7.3 %all-to-all-start = ((bf16[8,1600,128]{2,1,0:T(8,128)(2,1)}), bf16[8,1600,128]{2,1,0:T(8,128)(2,1)}, u32[]{:S(2)}, u32[]{:S(2)}) async-start(bf16[8,1600,128]{2,1,0:T(8,128)(2,1)} %source_rows.1), calls=%async_computation | async-start | bytes 6553600 | tf_op jit(solution)/shard_map/all_to_all | solution.py:595
  248.1 0.0 copy-done.7
  248.1 0.8 collective-permute-start.1
  248.9 47.7 %all-to-all-done.a_ref = bf16[8,1600,128]{2,1,0:T(8,128)(2,1)} async-done(((bf16[8,1600,128]{2,1,0:T(8,128)(2,1)}), bf16[8,1600,128]{2,1,0:T(8,128)(2,1)}, u32[]{:S(2)}, u32[]{:S(2)}) %all-to-all-start) | async-done | bytes 3276832 | tf_op jit(solution)/shard_map/all_to_all | solution.py:595
  296.6 0.7 broadcast_in_dim.9
  297.3 4.6 %all-to-all-start.3 = ((bf16[16,40,128]{2,1,0:T(8,128)(2,1)}), bf16[16,40,128]{2,1,0:T(8,128)(2,1)S(1)}, u32[]{:S(2)}, u32[]{:S(2)}) async-start(bf16[16,40,128]{2,1,0:T(8,128)(2,1)} %broadcast_in_dim.9), calls=%async_computation.3 | async-start | bytes 327680 | tf_op jit(solution)/shard_map/all_to_all | solution.py:563
  301.9 1.8 dynamic-slice_bitcast_fusion.emb_ref
  303.7 0.0 collective-permute-done.1.b_ref
  303.7 0.0 copy-start.2
  303.7 0.8 copy-done.2
  304.4 3.4 update.1
  307.9 0.0 all-to-all-done.3
  307.9 1.0 pad_maximum_fusion
  308.9 0.6 broadcast_in_dim.10
  309.5 60.5 %all_to_all.26 = bf16[8,2240,128]{2,1,0:T(8,128)(2,1)S(1)} all-to-all(bf16[8,2240,128]{2,1,0:T(8,128)(2,1)S(1)} %broadcast_in_dim.10), channel_id=1, replica_groups=mesh['dom'=16,'side'=4,'rep'=2] {'side','rep'}, dimensions={0} | all-to-all | bytes 9175040 | tf_op jit(solution)/shard_map/all_to_all | solution.py:563
  370.0 0.0 copy-start
  370.0 2.1 copy-done
  372.1 1.1 slice.9.x_ref
  373.3 3.5 relation_out.1
  376.8 3.8 slice.8.x_ref
  380.6 7.0 %finish.1 = (bf16[400,4096]{1,0:T(8,128)(2,1)}, bf16[400,4096]{1,0:T(8,128)(2,1)}) custom-call(bf16[8,1600,128]{2,1,0:T(8,128)(2,1)} %slice.8.x_ref, s32[1,4096]{1,0:T(1,128)} %bitcast.31), custom_call_target="tpu_custom_call" | custom-call | tf_op jit(solution)/shard_map/finish/pallas_call | solution.py:532
  (2 shorter events, 0.0 us)
Async XLA Ops:
  0.6 6.9 %copy-start.3 = (s32[1,1,1,8192]{3,2,1,0:T(1,128)S(1)}, s32[1,1,1,8192]{3,2,1,0:T(1,128)}, u32[]{:S(2)}) copy-start(s32[1,1,1,8192]{3,2,1,0:T(1,128)} %param.10) | copy-start | bytes 98308
  0.6 7.5 %copy-start.1 = (f32[1345,400]{0,1:T(8,128)S(1)}, f32[1345,400]{0,1:T(8,128)}, u32[]{:S(2)}) copy-start(f32[1345,400]{0,1:T(8,128)} %param.9) | copy-start | bytes 6456004
  0.7 36.6 %collective-permute-start = (bf16[4096,400]{0,1:T(8,128)(2,1)}, bf16[4096,400]{0,1:T(8,128)(2,1)}, u32[]{:S(2)}, u32[]{:S(2)}) collective-permute-start(bf16[4096,400]{0,1:T(8,128)(2,1)} %param.8), channel_id=1, source_target_pairs={{0,120},{8,0},{16,8},{24,16},{32,24},{40,32},{48,40},{56,48},{64,5... | collective-permute-start | bytes 9830408 | tf_op jit(solution)/shard_map/ppermute | solution.py:25
  6.9 3.5 copy-start.4
  6.9 4.1 %copy-start.5 = (s32[1,1,1,8192]{3,2,1,0:T(1,128)S(1)}, s32[1,1,1,8192]{3,2,1,0:T(1,128)}, u32[]{:S(2)}) copy-start(s32[1,1,1,8192]{3,2,1,0:T(1,128)} %param.11) | copy-start | bytes 98308
  11.6 19.3 %copy-start.6 = (s32[1,1,1,8192]{3,2,1,0:T(1,128)S(1)}, s32[1,1,1,8192]{3,2,1,0:T(1,128)}, u32[]{:S(2)}) copy-start(s32[1,1,1,8192]{3,2,1,0:T(1,128)} %param.12) | copy-start | bytes 98308
  214.4 26.4 %all-to-all-start.2 = ((f32[16,40,128]{2,1,0:T(8,128)}), f32[16,40,128]{2,1,0:T(8,128)S(1)}, u32[]{:S(2)}, u32[]{:S(2)}) async-start(f32[16,40,128]{2,1,0:T(8,128)} %bitcast.23), calls=%async_computation.2 | async-start | bytes 655360 | tf_op jit(solution)/shard_map/all_to_all | solution.py:593
  240.8 7.3 %copy-start.7 = (bf16[1600,128]{1,0:T(8,128)(2,1)S(1)}, bf16[1600,128]{1,0:T(8,128)(2,1)}, u32[]{:S(2)}) copy-start(bf16[1600,128]{1,0:T(8,128)(2,1)} %get-tuple-element.15) | copy-start | bytes 1228804
  240.8 55.8 %all-to-all-start = ((bf16[8,1600,128]{2,1,0:T(8,128)(2,1)}), bf16[8,1600,128]{2,1,0:T(8,128)(2,1)}, u32[]{:S(2)}, u32[]{:S(2)}) async-start(bf16[8,1600,128]{2,1,0:T(8,128)(2,1)} %source_rows.1), calls=%async_computation | async-start | bytes 6553600 | tf_op jit(solution)/shard_map/all_to_all | solution.py:595
  248.1 55.6 %collective-permute-start.1 = (bf16[1600,128]{1,0:T(8,128)(2,1)S(1)}, bf16[1600,128]{1,0:T(8,128)(2,1)S(1)}, u32[]{:S(2)}, u32[]{:S(2)}) collective-permute-start(bf16[1600,128]{1,0:T(8,128)(2,1)S(1)} %copy-done.7), channel_id=1, source_target_pairs={{0,8},{8,16},{16,24},{24,32},{32,40},{40,48},{48,56},{56,64},{64,7... | collective-permute-start | bytes 1228808 | tf_op jit(solution)/shard_map/ppermute | solution.py:25
  297.3 10.6 %all-to-all-start.3 = ((bf16[16,40,128]{2,1,0:T(8,128)(2,1)}), bf16[16,40,128]{2,1,0:T(8,128)(2,1)S(1)}, u32[]{:S(2)}, u32[]{:S(2)}) async-start(bf16[16,40,128]{2,1,0:T(8,128)(2,1)} %broadcast_in_dim.9), calls=%async_computation.3 | async-start | bytes 327680 | tf_op jit(solution)/shard_map/all_to_all | solution.py:563
  303.7 0.8 copy-start.2
  370.0 2.1 copy-start

commit v3 on v2

--- a/solution.py
+++ b/solution.py
@@ -179,8 +179,8 @@
 
 def block_kernel(
     nneg, count, rid_i, dst_i, neg_i, dst_hbm, e_hbm, r_hbm,
-    grad_out, v_out,
-    td, a0, a1, a2, r0_acc, r1_acc, raw, eb, rb, db, nb, lb, nbb, dn, stage, lsem, sems, vsem, osem,
+    lo_out, hi_out, rel_out, v_out,
+    td, a0, a1, a2, r0_acc, r1_acc, raw, eb, rb, db, nb, lb, nbb, dn, stage, rstage, lsem, sems, vsem, osem,
 ):
     total = count[0]
     nblocks = (total + SPAN - 1) // SPAN
@@ -304,20 +304,17 @@
     last = nblocks - 1
     put(last, lax.rem(last, 2)).wait()
 
-    n = td.shape[0] // GROUPS // PIECES
     m = r0_acc.shape[0] // GROUPS // PIECES
-    packed = n * 25 // 8
-    relp = m * 25 // 8
-    pad = grad_out.shape[1] - packed - relp
+    packed = m * 25 // 8
     grad, rel = plane((a0, a1, a2)), plane((r0_acc, r1_acc))
 
-    def fill(j, st):
-        write_piece(j * n, n, grad, st)
-        write_piece(j * m, m, rel, st.at[pl.ds(packed, relp)])
-        if pad:
-            st[packed + relp :, :] = jnp.zeros((pad, LANES), st.dtype)
-
-    emit(fill, grad_out, stage, osem)
+    def fill_rel(j, st):
+        write_piece(j * m, m, rel, st)
+        if st.shape[0] > packed:
+            st[packed:, :] = jnp.zeros((st.shape[0] - packed, LANES), st.dtype)
+
+    emit_halves(grad, td.shape[0] // GROUPS, lo_out, hi_out, stage, osem)
+    emit(fill_rel, rel_out, rstage, osem)
 
 
 def emit(fill, out, stage, sem):
@@ -339,7 +336,15 @@
         copy(j, j % 2).wait()
 
 
-def source_kernel(count, src_i, v_hbm, grad_out, a0, a1, a2, a3, vb, stage, sems, osem):
+def emit_halves(load, rows, lo_out, hi_out, stage, sem):
+    half = rows // PIECES // 2
+    for h, out in enumerate((lo_out, hi_out)):
+        emit(
+            lambda j, st, h=h: write_piece((2 * j + h) * half, half, load, st), out, stage, sem
+        )
+
+
+def source_kernel(count, src_i, v_hbm, lo_out, hi_out, a0, a1, a2, a3, vb, stage, sems, osem):
     nblocks = (count[0] + SPAN - 1) // SPAN
     accs = (a0, a1, a2, a3)
 
@@ -374,9 +379,7 @@
         return 0
 
     lax.fori_loop(0, nblocks, step, 0)
-    n = a0.shape[0] // GROUPS // PIECES
-    load = plane(accs)
-    emit(lambda j, st: write_piece(j * n, n, load, st), grad_out, stage, osem)
+    emit_halves(plane(accs), a0.shape[0] // GROUPS, lo_out, hi_out, stage, osem)
 
 
 def smem():
@@ -414,19 +417,22 @@
 
 def edge_blocks(nneg, count, rid, dst, neg, dst_slab, e_rows, r_rows, nrel):
     rows = dst_slab.shape[0]
-    packed = rows // PIECES * 25 // 8
+    packed = rows // PIECES // 2 * 25 // 8
+    half = jax.ShapeDtypeStruct((PIECES, packed, LANES), bf16)
     relm = -(-nrel // (PIECES * 64)) * 64
-    wire = -(-(packed + relm * 25 // 8) // 16) * 16
+    relrows = -(-(relm * 25 // 8) // 128) * 128
     table = pltpu.VMEM((rows * GROUPS, LANES), f32)
     rel = pltpu.VMEM((relm * PIECES * GROUPS, LANES), f32)
     return pl.pallas_call(
         functools.partial(block_kernel, nneg),
         out_shape=(
-            jax.ShapeDtypeStruct((PIECES, wire, LANES), bf16),
+            half,
+            half,
+            jax.ShapeDtypeStruct((PIECES, relrows, LANES), bf16),
             jax.ShapeDtypeStruct(r_rows.shape, f32),
         ),
         in_specs=[smem()] * 4 + [hbm()] * 3,
-        out_specs=(hbm(), hbm()),
+        out_specs=(hbm(), hbm(), hbm(), hbm()),
         scratch_shapes=[
             table, table, table, table, rel, rel,
             pltpu.VMEM((2, 512, dst_slab.shape[1]), bf16),
@@ -437,7 +443,8 @@
             pltpu.VMEM((SPAN, LANES * GROUPS), bf16),
             pltpu.VMEM((SPAN, LANES * GROUPS), bf16),
             pltpu.VMEM((SPAN, SPAN), bf16),
-            pltpu.VMEM((2, wire, LANES), bf16),
+            pltpu.VMEM((2, packed, LANES), bf16),
+            pltpu.VMEM((2, relrows, LANES), bf16),
             pltpu.SemaphoreType.DMA((2,)),
             pltpu.SemaphoreType.DMA((2, 2)),
             pltpu.SemaphoreType.DMA((2,)),
@@ -449,13 +456,14 @@
 
 
 def source_rows(count, src, values, rows):
-    packed = rows // PIECES * 25 // 8
+    packed = rows // PIECES // 2 * 25 // 8
+    half = jax.ShapeDtypeStruct((PIECES, packed, LANES), bf16)
     table = pltpu.VMEM((rows * GROUPS, LANES), f32)
     return pl.pallas_call(
         source_kernel,
-        out_shape=jax.ShapeDtypeStruct((PIECES, packed, LANES), bf16),
+        out_shape=(half, half),
         in_specs=[smem()] * 2 + [hbm()],
-        out_specs=hbm(),
+        out_specs=(hbm(), hbm()),
         scratch_shapes=[
             table, table, table, table,
             pltpu.VMEM((2, FLAT, LANES), f32),
@@ -469,26 +477,18 @@
     )(count, src, values)
 
 
-def sum_kernel(x_ref, rows_ref, rel_ref):
-    n = rows_ref.shape[0]
-    m = x_ref.shape[1] - n
-    total = jnp.sum(x_ref[...].astype(f32), axis=0)
-    rows_ref[...] = total[:n].astype(bf16)
-    rel_ref[:m, :] = total[n:]
-    if rel_ref.shape[0] > m:
-        rel_ref[m:, :] = jnp.zeros((rel_ref.shape[0] - m, LANES), f32)
-
-
-def sum_pieces(x, packed, relrows):
+def sum_kernel(x_ref, after_ref, out_ref):
+    out_ref[...] = jnp.sum(x_ref[...].astype(f32), axis=0)
+
+
+def sum_pieces(x, after):
     return pl.pallas_call(
         sum_kernel,
-        out_shape=(
-            jax.ShapeDtypeStruct((packed, LANES), bf16),
-            jax.ShapeDtypeStruct((relrows, LANES), f32),
-        ),
+        out_shape=jax.ShapeDtypeStruct(x.shape[1:], f32),
+        in_specs=[pl.BlockSpec(memory_space=pltpu.VMEM), hbm()],
         compiler_params=pltpu.CompilerParams(vmem_limit_bytes=VMEM),
         name="sum_pieces",
-    )(x)
+    )(x, after)
 
 
 def across(x, n):
@@ -498,69 +498,78 @@
     return jnp.concatenate([x[:n].T, x[n : 2 * n].T, x[2 * n : 3 * n].T, rest], axis=0)
 
 
-def update_kernel(a_ref, b_ref, emb_ref, out_ref):
+def update_kernel(a_ref, emb_ref, out_ref):
     width, n = emb_ref.shape
-    g = jnp.sum(a_ref[...].astype(f32), axis=0) + b_ref[...].astype(f32)
+    g = jnp.sum(a_ref[...].astype(f32), axis=0)
     new = (emb_ref[...].astype(f32) - 0.5 * across(g, n)).astype(bf16)
     for i in range(n // LANES):
         out_ref[i * width : (i + 1) * width, :] = new[:, i * LANES : (i + 1) * LANES]
 
 
-def update(a, b, emb):
+def update(a, emb):
     width, n = emb.shape
     return pl.pallas_call(
         update_kernel,
         out_shape=jax.ShapeDtypeStruct((width * n // LANES, LANES), bf16),
         compiler_params=pltpu.CompilerParams(vmem_limit_bytes=VMEM),
         name="update",
-    )(a, b, emb)
-
-
-def finish_kernel(x_ref, dirty_ref, up_ref, check_ref):
-    width, n = up_ref.shape
-    for i in range(n // LANES):
-        at = slice(i * LANES, (i + 1) * LANES)
-        x = x_ref[0, i * width : (i + 1) * width, :]
-        up_ref[:, at] = x
-        check_ref[:, at] = jnp.where(dirty_ref[:, at] == 1, x.astype(f32), 0.0).astype(bf16)
-
-
-def finish(x, dirty, width, rows):
-    pieces, wire, _ = x.shape
-    n = rows // pieces
-    out = jax.ShapeDtypeStruct((width, rows), bf16)
+    )(a, emb)
+
+
+def finish_kernel(place, a_ref, ar_ref, b0_ref, b1_ref, b2_ref, b3_ref, dirty_ref, up_ref, check_ref):
+    width = up_ref.shape[0]
+    half = dirty_ref.shape[1] // PIECES // 2
+    blocks = [(a_ref, k, k, 0) for k in range(4)] + [(ar_ref, k, 4 + k, 0) for k in range(4)]
+    for k, ref in enumerate((b0_ref, b1_ref, b2_ref, b3_ref)):
+        blocks += [(ref, 0, k, half), (ref, 1, 4 + k, half)]
+    for ref, i, at_place, off in blocks:
+        start = pl.multiple_of(place[at_place] * 2 * half + off, half)
+        for k in range(half // LANES):
+            at = pl.ds(pl.multiple_of(start + k * LANES, LANES), LANES)
+            x = ref[i, k * width : (k + 1) * width, :]
+            up_ref[:, at] = x
+            check_ref[:, at] = jnp.where(dirty_ref[:, at] == 1, x.astype(f32), 0.0).astype(bf16)
+
+
+def finish(place, parts, dirty, width):
+    out = jax.ShapeDtypeStruct((width, dirty.shape[1]), bf16)
     return pl.pallas_call(
         finish_kernel,
-        grid=(pieces,),
-        in_specs=[
-            pl.BlockSpec((1, wire, LANES), lambda i: (i, 0, 0)),
-            pl.BlockSpec((1, n), lambda i: (0, i)),
-        ],
-        out_specs=[pl.BlockSpec((width, n), lambda i: (0, i))] * 2,
+        in_specs=[smem()] + [pl.BlockSpec(memory_space=pltpu.VMEM)] * 7,
         out_shape=(out, out),
         compiler_params=pltpu.CompilerParams(vmem_limit_bytes=VMEM),
         name="finish",
-    )(x, dirty)
-
-
-def relation_kernel(m, x_ref, out_ref):
+    )(place, *parts, dirty)
+
+
+def relation_kernel(m, order, x_ref, out_ref):
     cols = jnp.concatenate(
-        [across(x_ref[i].astype(f32), m) for i in range(x_ref.shape[0])], axis=1
+        [across(x_ref[order[i]].astype(f32), m) for i in range(PIECES)], axis=1
     )
     out_ref[...] = cols[:, : out_ref.shape[1]]
 
 
-def relation_out(x, m, shape):
+def relation_out(order, x, m, shape):
     return pl.pallas_call(
         functools.partial(relation_kernel, m),
         out_shape=jax.ShapeDtypeStruct(shape, f32),
+        in_specs=[smem(), pl.BlockSpec(memory_space=pltpu.VMEM)],
         compiler_params=pltpu.CompilerParams(vmem_limit_bytes=VMEM),
         name="relation_out",
-    )(x)
-
-
-def to_all(x, axes, count):
-    return lax.all_to_all(jnp.broadcast_to(x, (count,) + x.shape), axes, 0, 0, tiled=True)
+    )(order, x)
+
+
+def around(x):
+    return [x] + [shifted(x, "side", by) for by in (1, -1, 2)]
+
+
+def both_reps(x):
+    return [x, shifted(x, "rep", 1)]
+
+
+def swapped(x, axis, bit):
+    count = lax.axis_size(axis)
+    return lax.ppermute(x, axis, [(i, i ^ bit) for i in range(count)])
 
 
 def local(
@@ -578,26 +587,36 @@
     neg = (jnp.pad(negative_ids[0, 0, 0], ((0, 0), (0, SPAN - nneg))) * GROUPS).reshape(-1)
     me = lax.axis_index("side") * lax.axis_size("rep") + lax.axis_index("rep")
     piece = rows // PIECES
-    own = lax.dynamic_slice_in_dim(embeddings.T, me * piece, piece, 1)
+    half = piece // 2
+    own = [lax.dynamic_slice_in_dim(embeddings.T, me * piece + h * half, half, 1) for h in (0, 1)]
+    side, rep = lax.axis_index("side"), lax.axis_index("rep")
+    sides = jnp.stack([side, (side + 3) % 4, (side + 1) % 4, (side + 2) % 4])
+    place = jnp.concatenate([sides * 2 + rep, sides * 2 + 1 - rep]).astype(jnp.int32)
+    order = jnp.argsort(place).astype(jnp.int32)
 
     dst_slab = shifted(embeddings, "dom", -1)
     e_rows, r_rows = edge_rows(count, src, rid, embeddings, relation)
-    sent, values = edge_blocks(nneg, count, rid, dst, neg, dst_slab, e_rows, r_rows, nrel)
-    got = lax.all_to_all(sent, group, 0, 0, tiled=True)
+    *gdst, grel, values = edge_blocks(nneg, count, rid, dst, neg, dst_slab, e_rows, r_rows, nrel)
+    returned = [shifted(g, "dom", 1) for g in gdst]
+    rel = lax.all_to_all(grel, group, 0, 0, tiled=True)
     gsrc = source_rows(count, src, values, rows)
-
-    packed = gsrc.shape[1]
-    relrows = -(-(sent.shape[1] - packed) // (8 * doms)) * 8 * doms
-    gdst, rel = sum_pieces(got, packed, relrows)
-    returned = shifted(gdst, "dom", 1)
-    rel = lax.all_to_all(rel.reshape(doms, -1, LANES), "dom", 0, 0, tiled=True)
-    rel = to_all(jnp.sum(rel, axis=0).astype(bf16), "dom", doms).reshape(-1, LANES)
-    a = lax.all_to_all(gsrc, group, 0, 0, tiled=True)
-    mine = update(a, returned, own)
-    every = to_all(jnp.concatenate([mine, rel], axis=0), group, PIECES)
-    updated, checkpoint = finish(every[:, : mine.shape[0]], dirty[None, :], width, rows)
+    rel = sum_pieces(rel, gsrc[0])
+    bit = 1
+    while bit < doms:
+        rel = rel + swapped(rel, "dom", bit)
+        bit *= 2
+    rel = jnp.concatenate(around(jnp.stack(both_reps(rel.astype(bf16)))))
     relm = -(-nrel // (PIECES * 64)) * 64
-    relation_grad = relation_out(every[:, mine.shape[0] :], relm, (width, nrel))
+    rel_order = (order % 4) * 2 + order // 4
+    relation_grad = relation_out(rel_order, rel, relm, (width, nrel))
+
+    mine = [
+        update(lax.all_to_all(gsrc[h] + returned[h], group, 0, 0, tiled=True), own[h])
+        for h in (0, 1)
+    ]
+    a4 = jnp.stack(around(mine[0]))
+    parts = both_reps(a4) + around(jnp.stack(both_reps(mine[1])))
+    updated, checkpoint = finish(place, parts, dirty[None, :], width)
     return (updated.T, relation_grad.T, checkpoint.T)
 
 

time: 393 us -> 325 us (0.83)
  blocking collectives: 152 us -> 0 us
  Pallas kernels: 130 us -> 182 us
  starting transfers between devices: 21.6 us -> 44.9 us
  other arithmetic: 2.99 us -> 15.1 us
    all_to_all x2 -> x0, blocking collectives: 152 us -> none  [the longest x1 92 us: local(): got = lax.all_to_all(sent, group, 0, 0, tiled=True)]
    pallas_call x4, Pallas kernels: 104 us -> 148 us  [the longest x1 115 us: edge_blocks(): pl.pallas_call(functools.partial(block_kernel, nneg), out_shape=(half, ha...]
    all_to_all x3, waiting for transfers between devices: 47.7 us -> 16.1 us  [the longest x2 16.1 us: local(): lax.all_to_all(gsrc[h] + returned[h], group, 0, 0, tiled=True)]
    ppermute x0 -> x4, waiting for transfers between devices: none -> 25.3 us  [swapped(): return lax.ppermute(x, axis, [(i, i ^ bit) for i in range(count)])]
    ppermute x2 -> x15, starting transfers between devices: 0.85 us -> 22.8 us  [shifted(): return lax.ppermute(x, axis, [(i, (i + by) % count) for i in range(count)])]
    add x0 -> x7, other arithmetic: none -> 8.24 us  [the longest x2 6.53 us: local(): gsrc[h] + returned[h]]
    ppermute x2 -> x15, waiting for transfers between devices: 5.62 us -> 13.6 us  [shifted(): return lax.ppermute(x, axis, [(i, (i + by) % count) for i in range(count)])]
    pallas_call x1, Pallas kernels: 19.3 us -> 25.4 us  [edge_rows(): pl.pallas_call(edge_rows_kernel, out_shape=(shape, shape), in_specs=[smem...]
  transfers between devices with their start and end apart: 5 -> 22, of which waited for: 2 -> 7; matrix products, arithmetic and copies ran while one was open for 3% -> 9% of each run, Pallas kernels for 10% -> 19%
where the time goes in v3:
time: 325 us; the launch traced here: 323 us
  Pallas kernels  182 us (56%)
  waiting for transfers between devices  55 us (17%)
  starting transfers between devices  44.9 us (14%)
  local copies, waits for them, and re-layouts  24.3 us (7%)
  other arithmetic  15.1 us (5%)
    pallas_call x1, Pallas kernels, edge_blocks(): pl.pallas_call(functools.partial(block_kernel, nneg), out_shape=(half, ha...  115 us
    pallas_call x1, Pallas kernels, edge_rows(): pl.pallas_call(edge_rows_kernel, out_shape=(shape, shape), in_specs=[smem...  25.4 us
    ppermute x4, waiting for transfers between devices, swapped(): return lax.ppermute(x, axis, [(i, i ^ bit) for i in range(count)])  25.3 us
    pallas_call x1, Pallas kernels, source_rows(): pl.pallas_call(source_kernel, out_shape=(half, half), in_specs=[smem()] *...  24.1 us
    ppermute x15, starting transfers between devices, shifted(): return lax.ppermute(x, axis, [(i, (i + by) % count) for i in range(count)])  22.8 us
    unnamed x34, local copies, waits for them, and re-layouts  16.4 us
    all_to_all x2, waiting for transfers between devices, local(): lax.all_to_all(gsrc[h] + returned[h], group, 0, 0, tiled=True)  16.1 us
    ppermute x15, waiting for transfers between devices, shifted(): return lax.ppermute(x, axis, [(i, (i + by) % count) for i in range(count)])  13.6 us
  transfers between devices with their start and end apart: 22, of which 7 were waited for; matrix products, arithmetic and copies ran while one was open for 9% of the time, Pallas kernels for 19%

profile of v3, /device:TPU:96, one launch (start us, length us, event | category | flops | bytes accessed | tf_op | source)
XLA Modules:
  0.0 322.6 jit_solution(13887979369261738446)
XLA Ops:
  0.7 0.1 collective-permute-start
  0.7 6.2 %copy.14.emb_hbm = bf16[4096,400]{1,0:T(8,128)(2,1)} copy(bf16[4096,400]{0,1:T(8,128)(2,1)} %param.8) | data formatting | bytes 6553600 | tf_op args[0]
  7.6 0.6 broadcast_multiply_fusion.2
  8.2 2.2 copy.15.rel_ref
  10.4 0.6 copy.19
  11.0 0.6 broadcast_multiply_fusion.1
  11.7 25.4 %edge_rows.1 = (f32[8,4096,128]{2,1,0:T(8,128)}, f32[8,4096,128]{2,1,0:T(8,128)}) custom-call(s32[1]{0:T(128)} %bitcast.32.count, s32[8192]{0:T(1024)} %bitcast.38, s32[8192]{0:T(1024)} %bitcast.40, bf16[4096,400]{1,0:T(8,128)(2,1)} %copy.14.emb_hbm, f32[1345,400]{1,0:T(8,128)} %copy.15.rel_ref), custom_call_target="tpu_custom_call" | custom-call | bytes 60000000 | tf_op jit(solution)/shard_map/edge_rows/pallas_call | solution.py:398
  37.1 0.6 broadcast_multiply_fusion
  37.7 0.0 collective-permute-done
  37.8 6.0 %copy.16.dst_hbm = bf16[4096,400]{1,0:T(8,128)(2,1)} copy(bf16[4096,400]{0,1:T(8,128)(2,1)} %collective-permute-done) | data formatting | bytes 6553600 | tf_op jit(solution)/shard_map/ppermute | solution.py:25
  43.8 115.5 %edge_blocks.1 = (bf16[8,800,128]{2,1,0:T(8,128)(2,1)}, bf16[8,800,128]{2,1,0:T(8,128)(2,1)}, bf16[8,640,128]{2,1,0:T(8,128)(2,1)}, f32[8,4096,128]{2,1,0:T(8,128)}) custom-call(s32[1]{0:T(128)} %bitcast.33.count, s32[8192]{0:T(1024)} %bitcast.41, s32[8192]{0:T(1024)} %bitcast.44, s32[8192]{0:T(1024)} %bitcast.43, bf16[4096,400]{1,0:T(8,128)(2,1)} %copy.16.dst_hbm, ...), custom_call_target="tpu_custom_call" | custom-call | tf_op jit(solution)/shard_map/edge_blocks/pallas_call | solution.py:426
  159.3 0.1 collective-permute-start.1
  159.4 10.0 %all-to-all-start.2 = ((bf16[8,640,128]{2,1,0:T(8,128)(2,1)}), bf16[8,640,128]{2,1,0:T(8,128)(2,1)S(1)}, u32[]{:S(2)}, u32[]{:S(2)}) async-start(bf16[8,640,128]{2,1,0:T(8,128)(2,1)} %get-tuple-element.23), calls=%async_computation.2 | async-start | bytes 2621440 | tf_op jit(solution)/shard_map/all_to_all | solution.py:601
  169.3 24.1 %source_rows.1 = (bf16[8,800,128]{2,1,0:T(8,128)(2,1)}, bf16[8,800,128]{2,1,0:T(8,128)(2,1)}) custom-call(s32[1]{0:T(128)} %bitcast.34.count, s32[8192]{0:T(1024)} %bitcast.39, f32[8,4096,128]{2,1,0:T(8,128)} %get-tuple-element.16.v_hbm), custom_call_target="tpu_custom_call" | custom-call | bytes 60000000 | tf_op jit(solution)/shard_map/source_rows/pallas_call | solution.py:462
  193.4 3.0 add.81
  196.4 0.0 all-to-all-done.2.x_ref
  196.4 1.1 copy-done.2
  197.5 5.6 %all-to-all-start = ((bf16[8,800,128]{2,1,0:T(8,128)(2,1)}), bf16[8,800,128]{2,1,0:T(8,128)(2,1)S(1)}, u32[]{:S(2)}, u32[]{:S(2)}) async-start(bf16[8,800,128]{2,1,0:T(8,128)(2,1)} %add.81), calls=%async_computation | async-start | bytes 3276800 | tf_op jit(solution)/shard_map/all_to_all | solution.py:614
  203.2 2.2 sum_pieces.1
  205.4 0.6 collective-permute-start.11
  206.0 1.5 collective-permute-done.11
  207.5 1.0 add.89
  208.5 1.4 collective-permute-start.12
  209.9 3.5 %add.84 = bf16[8,800,128]{2,1,0:T(8,128)(2,1)} add(bf16[8,800,128]{2,1,0:T(8,128)(2,1)} %get-tuple-element.19, bf16[8,800,128]{2,1,0:T(8,128)(2,1)} %collective-permute-done.6) | non-fusion elementwise | flops 819200 | bytes 4915200 | tf_op jit(solution)/shard_map/add | solution.py:614
  213.4 16.1 %all-to-all-done.a_ref = bf16[8,800,128]{2,1,0:T(8,128)(2,1)S(1)} async-done(((bf16[8,800,128]{2,1,0:T(8,128)(2,1)}), bf16[8,800,128]{2,1,0:T(8,128)(2,1)S(1)}, u32[]{:S(2)}, u32[]{:S(2)}) %all-to-all-start) | async-done | bytes 1638432 | tf_op jit(solution)/shard_map/all_to_all | solution.py:614
  229.5 1.2 copy-done.1
  230.7 4.4 %all-to-all-start.1 = ((bf16[8,800,128]{2,1,0:T(8,128)(2,1)}), bf16[8,800,128]{2,1,0:T(8,128)(2,1)S(1)}, u32[]{:S(2)}, u32[]{:S(2)}) async-start(bf16[8,800,128]{2,1,0:T(8,128)(2,1)} %add.84), calls=%async_computation.1 | async-start | bytes 3276800 | tf_op jit(solution)/shard_map/all_to_all | solution.py:614
  235.1 0.0 collective-permute-done.12
  235.1 0.1 collective-permute-start.13
  235.2 8.9 %collective-permute-done.13 = f32[640,128]{1,0:T(8,128)S(1)} collective-permute-done((f32[640,128]{1,0:T(8,128)S(1)}, f32[640,128]{1,0:T(8,128)S(1)}, u32[]{:S(2)}, u32[]{:S(2)}) %collective-permute-start.13) | collective-permute-done | bytes 327712 | tf_op jit(solution)/shard_map/ppermute | solution.py:572
  244.2 0.1 collective-permute-start.14
  244.3 0.1 broadcast_add_fusion
  244.4 14.9 %collective-permute-done.14 = f32[640,128]{1,0:T(8,128)S(1)} collective-permute-done((f32[640,128]{1,0:T(8,128)S(1)}, f32[640,128]{1,0:T(8,128)S(1)}, u32[]{:S(2)}, u32[]{:S(2)}) %collective-permute-start.14) | collective-permute-done | bytes 327712 | tf_op jit(solution)/shard_map/ppermute | solution.py:572
  259.3 0.7 constant_dynamic-update-slice_fusion.4
  260.0 4.8 %collective-permute-start.15 = (bf16[640,128]{1,0:T(8,128)(2,1)}, bf16[640,128]{1,0:T(8,128)(2,1)}, u32[]{:S(2)}, u32[]{:S(2)}) collective-permute-start(bf16[640,128]{1,0:T(8,128)(2,1)} %get-tuple-element.26), channel_id=1, source_target_pairs={{0,1},{1,0},{2,3},{3,2},{4,5},{5,4},{6,7},{7,6},{8,9},{9,8},{10,11... | collective-permute-start | bytes 491528 | tf_op jit(solution)/shard_map/ppermute | solution.py:25
  264.8 1.8 dynamic-slice_bitcast_fusion
  266.6 2.4 update.2
  269.0 0.6 collective-permute-start.2
  269.6 2.7 collective-permute-start.3
  272.3 1.2 collective-permute-start.4
  273.5 0.1 pad_add_fusion.place
  273.5 1.0 sort.17
  274.5 1.8 pad_maximum_fusion.2
  276.2 0.4 collective-permute-start.16
  276.7 2.8 collective-permute-start.17
  279.5 1.2 copy-done
  280.7 2.4 update.3
  283.1 1.4 collective-permute-start.7
  284.4 1.3 pad_maximum_fusion.a_ref
  285.8 2.2 collective-permute-start.5
  288.0 0.5 fusion.1.order
  288.6 1.1 collective-permute-start.18
  289.7 3.1 collective-permute-done.7
  292.9 1.2 collective-permute-start.10
  294.1 8.7 %collective-permute-done.17 = bf16[2,640,128]{2,1,0:T(8,128)(2,1)} collective-permute-done((bf16[2,640,128]{2,1,0:T(8,128)(2,1)}, bf16[2,640,128]{2,1,0:T(8,128)(2,1)}, u32[]{:S(2)}, u32[]{:S(2)}) %collective-permute-start.17) | collective-permute-done | bytes 327712 | tf_op jit(solution)/shard_map/ppermute | solution.py:25
  302.7 4.2 %collective-permute-start.9 = (bf16[2,800,128]{2,1,0:T(8,128)(2,1)S(1)}, bf16[2,800,128]{2,1,0:T(8,128)(2,1)}, u32[]{:S(2)}, u32[]{:S(2)}) collective-permute-start(bf16[2,800,128]{2,1,0:T(8,128)(2,1)S(1)} %pad_maximum_fusion.1.b0_ref), channel_id=1, source_target_pairs={{0,6},{2,0},{4,2},{6,4},{1,7},{3,1},{5,3},{7,5},{8,14},{10,8},{12,... | collective-permute-start | bytes 1228808 | tf_op jit(solution)/shard_map/ppermute | solution.py:25
  306.9 0.9 constant_dynamic-update-slice_fusion.3
  307.8 1.0 constant_dynamic-update-slice_fusion.2
  308.9 1.0 constant_dynamic-update-slice_fusion.1
  309.9 0.0 copy-start.5
  310.0 1.0 copy-done.5
  311.0 3.5 %relation_out.1 = f32[400,1345]{1,0:T(8,128)} custom-call(s32[8]{0:T(128)} %fusion.1.order, bf16[8,640,128]{2,1,0:T(8,128)(2,1)} %copy-done.5), custom_call_target="tpu_custom_call" | custom-call | tf_op jit(solution)/shard_map/relation_out/pallas_call | solution.py:553
  314.6 1.8 collective-permute-done.8.b1_ref
  316.4 6.2 %finish.1 = (bf16[400,4096]{1,0:T(8,128)(2,1)}, bf16[400,4096]{1,0:T(8,128)(2,1)}) custom-call(s32[8]{0:T(128)} %copy-done.13, bf16[4,800,128]{2,1,0:T(8,128)(2,1)} %copy-done.3, bf16[4,800,128]{2,1,0:T(8,128)(2,1)} %collective-permute-done.5.ar_ref, bf16[2,800,128]{2,1,0:T(8,128)(2,1)} %copy-done.6, bf16[2,800,128]{2,1,0:T(8,128)(2,1)} %collective-permute-done.8.b1_ref, ...), custom_call_target="tpu_custom_call" | custom-call | tf_op jit(solution)/shard_map/finish/pallas_call | solution.py:536
  (44 shorter events, 0.3 us)
Async XLA Ops:
  0.6 6.9 %copy-start.9 = (s32[1,1,1,8192]{3,2,1,0:T(1,128)S(1)}, s32[1,1,1,8192]{3,2,1,0:T(1,128)}, u32[]{:S(2)}) copy-start(s32[1,1,1,8192]{3,2,1,0:T(1,128)} %param.10) | copy-start | bytes 98308
  0.6 7.6 %copy-start.4 = (f32[1345,400]{0,1:T(8,128)S(1)}, f32[1345,400]{0,1:T(8,128)}, u32[]{:S(2)}) copy-start(f32[1345,400]{0,1:T(8,128)} %param.9) | copy-start | bytes 6456004
  0.7 37.1 %collective-permute-start = (bf16[4096,400]{0,1:T(8,128)(2,1)}, bf16[4096,400]{0,1:T(8,128)(2,1)}, u32[]{:S(2)}, u32[]{:S(2)}) collective-permute-start(bf16[4096,400]{0,1:T(8,128)(2,1)} %param.8), channel_id=1, source_target_pairs={{0,120},{8,0},{16,8},{24,16},{32,24},{40,32},{48,40},{56,48},{64,5... | collective-permute-start | bytes 9830408 | tf_op jit(solution)/shard_map/ppermute | solution.py:25
  8.2 2.2 copy-start.10
  8.2 2.8 copy-start.11
  11.7 25.4 %copy-start.12 = (s32[1,1,1,8192]{3,2,1,0:T(1,128)S(1)}, s32[1,1,1,8192]{3,2,1,0:T(1,128)}, u32[]{:S(2)}) copy-start(s32[1,1,1,8192]{3,2,1,0:T(1,128)} %param.12) | copy-start | bytes 98308
  159.3 34.1 %collective-permute-start.1 = (bf16[8,800,128]{2,1,0:T(8,128)(2,1)}, bf16[8,800,128]{2,1,0:T(8,128)(2,1)S(1)}, u32[]{:S(2)}, u32[]{:S(2)}) collective-permute-start(bf16[8,800,128]{2,1,0:T(8,128)(2,1)} %get-tuple-element.18), channel_id=1, source_target_pairs={{0,8},{8,16},{16,24},{24,32},{32,40},{40,48},{48,56},{56,64},{64,7... | collective-permute-start | bytes 4915208 | tf_op jit(solution)/shard_map/ppermute | solution.py:25
  159.4 37.1 %all-to-all-start.2 = ((bf16[8,640,128]{2,1,0:T(8,128)(2,1)}), bf16[8,640,128]{2,1,0:T(8,128)(2,1)S(1)}, u32[]{:S(2)}, u32[]{:S(2)}) async-start(bf16[8,640,128]{2,1,0:T(8,128)(2,1)} %get-tuple-element.23), calls=%async_computation.2 | async-start | bytes 2621440 | tf_op jit(solution)/shard_map/all_to_all | solution.py:601
  169.3 40.6 %collective-permute-start.6 = (bf16[8,800,128]{2,1,0:T(8,128)(2,1)}, bf16[8,800,128]{2,1,0:T(8,128)(2,1)}, u32[]{:S(2)}, u32[]{:S(2)}) collective-permute-start(bf16[8,800,128]{2,1,0:T(8,128)(2,1)} %get-tuple-element.20), channel_id=1, source_target_pairs={{0,8},{8,16},{16,24},{24,32},{32,40},{40,48},{48,56},{56,64},{64,7... | collective-permute-start | bytes 4915208 | tf_op jit(solution)/shard_map/ppermute | solution.py:25
  196.4 1.1 copy-start.2
  197.5 32.0 %all-to-all-start = ((bf16[8,800,128]{2,1,0:T(8,128)(2,1)}), bf16[8,800,128]{2,1,0:T(8,128)(2,1)S(1)}, u32[]{:S(2)}, u32[]{:S(2)}) async-start(bf16[8,800,128]{2,1,0:T(8,128)(2,1)} %add.81), calls=%async_computation | async-start | bytes 3276800 | tf_op jit(solution)/shard_map/all_to_all | solution.py:614
  205.4 2.1 collective-permute-start.11
  208.5 26.5 %collective-permute-start.12 = (f32[640,128]{1,0:T(8,128)S(1)}, f32[640,128]{1,0:T(8,128)S(1)}, u32[]{:S(2)}, u32[]{:S(2)}) collective-permute-start(f32[640,128]{1,0:T(8,128)S(1)} %add.89), channel_id=1, source_target_pairs={{0,16},{8,24},{16,0},{24,8},{32,48},{40,56},{48,32},{56,40},{64,80... | collective-permute-start | bytes 983048 | tf_op jit(solution)/shard_map/ppermute | solution.py:572
  229.5 1.2 copy-start.1
  230.7 48.8 %all-to-all-start.1 = ((bf16[8,800,128]{2,1,0:T(8,128)(2,1)}), bf16[8,800,128]{2,1,0:T(8,128)(2,1)S(1)}, u32[]{:S(2)}, u32[]{:S(2)}) async-start(bf16[8,800,128]{2,1,0:T(8,128)(2,1)} %add.84), calls=%async_computation.1 | async-start | bytes 3276800 | tf_op jit(solution)/shard_map/all_to_all | solution.py:614
  235.1 9.1 %collective-permute-start.13 = (f32[640,128]{1,0:T(8,128)S(1)}, f32[640,128]{1,0:T(8,128)S(1)}, u32[]{:S(2)}, u32[]{:S(2)}) collective-permute-start(f32[640,128]{1,0:T(8,128)S(1)} %add.90), channel_id=1, source_target_pairs={{0,32},{8,40},{16,48},{24,56},{32,0},{40,8},{48,16},{56,24},{64,96... | collective-permute-start | bytes 983048 | tf_op jit(solution)/shard_map/ppermute | solution.py:572
  244.2 15.1 %collective-permute-start.14 = (f32[640,128]{1,0:T(8,128)S(1)}, f32[640,128]{1,0:T(8,128)S(1)}, u32[]{:S(2)}, u32[]{:S(2)}) collective-permute-start(f32[640,128]{1,0:T(8,128)S(1)} %add.91), channel_id=1, source_target_pairs={{0,64},{8,72},{16,80},{24,88},{32,96},{40,104},{48,112},{56,120},{... | collective-permute-start | bytes 983048 | tf_op jit(solution)/shard_map/ppermute | solution.py:572
  260.0 14.5 %collective-permute-start.15 = (bf16[640,128]{1,0:T(8,128)(2,1)}, bf16[640,128]{1,0:T(8,128)(2,1)}, u32[]{:S(2)}, u32[]{:S(2)}) collective-permute-start(bf16[640,128]{1,0:T(8,128)(2,1)} %get-tuple-element.26), channel_id=1, source_target_pairs={{0,1},{1,0},{2,3},{3,2},{4,5},{5,4},{6,7},{7,6},{8,9},{9,8},{10,11... | collective-permute-start | bytes 491528 | tf_op jit(solution)/shard_map/ppermute | solution.py:25
  269.0 14.0 %collective-permute-start.2 = (bf16[800,128]{1,0:T(8,128)(2,1)}, bf16[800,128]{1,0:T(8,128)(2,1)}, u32[]{:S(2)}, u32[]{:S(2)}) collective-permute-start(bf16[800,128]{1,0:T(8,128)(2,1)} %update.2), channel_id=1, source_target_pairs={{0,2},{2,4},{4,6},{6,0},{1,3},{3,5},{5,7},{7,1},{8,10},{10,12},{12... | collective-permute-start | bytes 614408 | tf_op jit(solution)/shard_map/ppermute | solution.py:25
  269.6 14.8 %collective-permute-start.3 = (bf16[800,128]{1,0:T(8,128)(2,1)}, bf16[800,128]{1,0:T(8,128)(2,1)}, u32[]{:S(2)}, u32[]{:S(2)}) collective-permute-start(bf16[800,128]{1,0:T(8,128)(2,1)} %update.2), channel_id=1, source_target_pairs={{0,6},{2,0},{4,2},{6,4},{1,7},{3,1},{5,3},{7,5},{8,14},{10,8},{12,... | collective-permute-start | bytes 614408 | tf_op jit(solution)/shard_map/ppermute | solution.py:25
  272.3 12.2 %collective-permute-start.4 = (bf16[800,128]{1,0:T(8,128)(2,1)}, bf16[800,128]{1,0:T(8,128)(2,1)}, u32[]{:S(2)}, u32[]{:S(2)}) collective-permute-start(bf16[800,128]{1,0:T(8,128)(2,1)} %update.2), channel_id=1, source_target_pairs={{0,4},{2,6},{4,0},{6,2},{1,5},{3,7},{5,1},{7,3},{8,12},{10,14},{12... | collective-permute-start | bytes 614408 | tf_op jit(solution)/shard_map/ppermute | solution.py:25
  273.5 12.3 %copy-start.13 = (s32[8]{0:T(128)}, s32[8]{0:T(128)S(1)}, u32[]{:S(2)}) copy-start(s32[8]{0:T(128)S(1)} %pad_add_fusion.place) | copy-start | bytes 100
  276.2 17.8 %collective-permute-start.16 = (bf16[2,640,128]{2,1,0:T(8,128)(2,1)}, bf16[2,640,128]{2,1,0:T(8,128)(2,1)}, u32[]{:S(2)}, u32[]{:S(2)}) collective-permute-start(bf16[2,640,128]{2,1,0:T(8,128)(2,1)} %pad_maximum_fusion.2), channel_id=1, source_target_pairs={{0,2},{2,4},{4,6},{6,0},{1,3},{3,5},{5,7},{7,1},{8,10},{10,12},{12... | collective-permute-start | bytes 983048 | tf_op jit(solution)/shard_map/ppermute | solution.py:25
  276.7 26.1 %collective-permute-start.17 = (bf16[2,640,128]{2,1,0:T(8,128)(2,1)}, bf16[2,640,128]{2,1,0:T(8,128)(2,1)}, u32[]{:S(2)}, u32[]{:S(2)}) collective-permute-start(bf16[2,640,128]{2,1,0:T(8,128)(2,1)} %pad_maximum_fusion.2), channel_id=1, source_target_pairs={{0,6},{2,0},{4,2},{6,4},{1,7},{3,1},{5,3},{7,5},{8,14},{10,8},{12,... | collective-permute-start | bytes 983048 | tf_op jit(solution)/shard_map/ppermute | solution.py:25
  279.5 1.2 copy-start
  283.1 9.7 %copy-start.7 = (bf16[800,128]{1,0:T(8,128)(2,1)S(1)}, bf16[800,128]{1,0:T(8,128)(2,1)}, u32[]{:S(2)}) copy-start(bf16[800,128]{1,0:T(8,128)(2,1)} %update.3) | copy-start | bytes 614404
  283.1 9.7 %collective-permute-start.7 = (bf16[800,128]{1,0:T(8,128)(2,1)}, bf16[800,128]{1,0:T(8,128)(2,1)S(1)}, u32[]{:S(2)}, u32[]{:S(2)}) collective-permute-start(bf16[800,128]{1,0:T(8,128)(2,1)} %update.3), channel_id=1, source_target_pairs={{0,1},{1,0},{2,3},{3,2},{4,5},{5,4},{6,7},{7,6},{8,9},{9,8},{10,11... | collective-permute-start | bytes 614408 | tf_op jit(solution)/shard_map/ppermute | solution.py:25
  285.8 28.7 %copy-start.3 = (bf16[4,800,128]{2,1,0:T(8,128)(2,1)}, bf16[4,800,128]{2,1,0:T(8,128)(2,1)S(1)}, u32[]{:S(2)}) copy-start(bf16[4,800,128]{2,1,0:T(8,128)(2,1)S(1)} %pad_maximum_fusion.a_ref) | copy-start | bytes 2457604
  285.8 30.6 %collective-permute-start.5 = (bf16[4,800,128]{2,1,0:T(8,128)(2,1)S(1)}, bf16[4,800,128]{2,1,0:T(8,128)(2,1)}, u32[]{:S(2)}, u32[]{:S(2)}) collective-permute-start(bf16[4,800,128]{2,1,0:T(8,128)(2,1)S(1)} %pad_maximum_fusion.a_ref), channel_id=1, source_target_pairs={{0,1},{1,0},{2,3},{3,2},{4,5},{5,4},{6,7},{7,6},{8,9},{9,8},{10,11... | collective-permute-start | bytes 2457608 | tf_op jit(solution)/shard_map/ppermute | solution.py:25
  288.6 21.3 %collective-permute-start.18 = (bf16[2,640,128]{2,1,0:T(8,128)(2,1)}, bf16[2,640,128]{2,1,0:T(8,128)(2,1)S(1)}, u32[]{:S(2)}, u32[]{:S(2)}) collective-permute-start(bf16[2,640,128]{2,1,0:T(8,128)(2,1)} %pad_maximum_fusion.2), channel_id=1, source_target_pairs={{0,4},{2,6},{4,0},{6,2},{1,5},{3,7},{5,1},{7,3},{8,12},{10,14},{12... | collective-permute-start | bytes 983048 | tf_op jit(solution)/shard_map/ppermute | solution.py:25
  292.8 21.7 %copy-start.6 = (bf16[2,800,128]{2,1,0:T(8,128)(2,1)}, bf16[2,800,128]{2,1,0:T(8,128)(2,1)S(1)}, u32[]{:S(2)}) copy-start(bf16[2,800,128]{2,1,0:T(8,128)(2,1)S(1)} %pad_maximum_fusion.1.b0_ref) | copy-start | bytes 1228804
  292.9 21.7 %collective-permute-start.10 = (bf16[2,800,128]{2,1,0:T(8,128)(2,1)S(1)}, bf16[2,800,128]{2,1,0:T(8,128)(2,1)S(1)}, u32[]{:S(2)}, u32[]{:S(2)}) collective-permute-start(bf16[2,800,128]{2,1,0:T(8,128)(2,1)S(1)} %pad_maximum_fusion.1.b0_ref), channel_id=1, source_target_pairs={{0,4},{2,6},{4,0},{6,2},{1,5},{3,7},{5,1},{7,3},{8,12},{10,14},{12... | collective-permute-start | bytes 1228808 | tf_op jit(solution)/shard_map/ppermute | solution.py:25
  294.1 22.3 %collective-permute-start.8 = (bf16[2,800,128]{2,1,0:T(8,128)(2,1)S(1)}, bf16[2,800,128]{2,1,0:T(8,128)(2,1)}, u32[]{:S(2)}, u32[]{:S(2)}) collective-permute-start(bf16[2,800,128]{2,1,0:T(8,128)(2,1)S(1)} %pad_maximum_fusion.1.b0_ref), channel_id=1, source_target_pairs={{0,2},{2,4},{4,6},{6,0},{1,3},{3,5},{5,7},{7,1},{8,10},{10,12},{12... | collective-permute-start | bytes 1228808 | tf_op jit(solution)/shard_map/ppermute | solution.py:25
  302.7 13.6 %collective-permute-start.9 = (bf16[2,800,128]{2,1,0:T(8,128)(2,1)S(1)}, bf16[2,800,128]{2,1,0:T(8,128)(2,1)}, u32[]{:S(2)}, u32[]{:S(2)}) collective-permute-start(bf16[2,800,128]{2,1,0:T(8,128)(2,1)S(1)} %pad_maximum_fusion.1.b0_ref), channel_id=1, source_target_pairs={{0,6},{2,0},{4,2},{6,4},{1,7},{3,1},{5,3},{7,5},{8,14},{10,8},{12,... | collective-permute-start | bytes 1228808 | tf_op jit(solution)/shard_map/ppermute | solution.py:25
  309.9 1.1 copy-start.5
  314.5 1.8 copy-start.8

commit v4 on v3

--- a/solution.py
+++ b/solution.py
@@ -12,8 +12,10 @@
 GROUPS = 4
 REST = 16
 FLAT = SPAN * GROUPS
-CHUNK = 256
+CHUNK = SPAN // 2
+HALF = FLAT // 2
 PIECES = 8
+SLOTS = 4
 VMEM = 61 * 2**20
 
 f32 = jnp.float32
@@ -43,6 +45,15 @@
     n = cols[0].shape[0]
     x = jnp.concatenate([c.reshape(n // 8, 1, 8, LANES) for c in cols], axis=1)
     return x.reshape(n * GROUPS, LANES)
+
+
+def gather_rows(ops, base, n):
+    for k0 in range(0, n, 8):
+        ks = range(k0, k0 + 8)
+        held = [[table[row_of(ids[j + k]), :] for table, ids, j, _ in ops] for k in ks]
+        for k, rows in zip(ks, held):
+            for (_, _, _, out), x in zip(ops, rows):
+                out[slot_of(base, k), :] = x
 
 
 def fill_rows(x, table, first, n):
@@ -83,7 +94,9 @@
             copy(i + 2, slot).start()
 
 
-def edge_rows_kernel(count, src_i, rid_i, emb_hbm, rel_ref, e_out, r_out, ts, tr, raw, eb, rb, lsem, sems):
+def edge_rows_kernel(
+    count, src_i, rid_i, emb_hbm, rel_ref, e_out, r_out, ts, tr, raw, eb0, eb1, rb0, rb1, lsem, sems
+):
     load_table(emb_hbm, raw, lsem, ts)
     nrel = rel_ref.shape[0]
     whole = nrel // 64
@@ -97,12 +110,15 @@
         fill_rows(rel_ref[i : i + 1, :], tr, i, 1)
 
     nblocks = (count[0] + SPAN - 1) // SPAN
+    outs = ((eb0, e_out, 0), (eb1, e_out, 1), (rb0, r_out, 0), (rb1, r_out, 1))
 
     def copies(blk, slot):
-        return (
-            pltpu.make_async_copy(eb.at[slot], e_out.at[blk], sems.at[slot, 0]),
-            pltpu.make_async_copy(rb.at[slot], r_out.at[blk], sems.at[slot, 1]),
-        )
+        return [
+            pltpu.make_async_copy(
+                buf.at[slot], out.at[blk, pl.ds(h * HALF, HALF)], sems.at[slot, i]
+            )
+            for i, (buf, out, h) in enumerate(outs)
+        ]
 
     def step(blk, _):
         slot = lax.rem(blk, 2)
@@ -112,15 +128,22 @@
             for c in copies(blk - 2, slot):
                 c.wait()
 
-        es, rs = eb.at[slot], rb.at[slot]
-
-        @pl.loop(0, SPAN // 16)
+        e0, e1, r0, r1 = (x.at[slot] for x in (eb0, eb1, rb0, rb1))
+
+        @pl.loop(0, SPAN // 32)
         def _(q):
             base = pl.multiple_of(q * 16 * GROUPS, 64)
-            for k in range(16):
-                j = blk * SPAN + q * 16 + k
-                es[slot_of(base, k), :] = ts[row_of(src_i[j]), :]
-                rs[slot_of(base, k), :] = tr[row_of(rid_i[j]), :]
+            j = blk * SPAN + q * 16
+            gather_rows(
+                [
+                    (ts, src_i, j, e0),
+                    (ts, src_i, j + SPAN // 2, e1),
+                    (tr, rid_i, j, r0),
+                    (tr, rid_i, j + SPAN // 2, r1),
+                ],
+                base,
+                16,
+            )
 
         for c in copies(blk, slot):
             c.start()
@@ -180,7 +203,7 @@
 def block_kernel(
     nneg, count, rid_i, dst_i, neg_i, dst_hbm, e_hbm, r_hbm,
     lo_out, hi_out, rel_out, v_out,
-    td, a0, a1, a2, r0_acc, r1_acc, raw, eb, rb, db, nb, lb, nbb, dn, stage, rstage, lsem, sems, vsem, osem,
+    td, a0, a1, a2, r0_acc, r1_acc, raw, eb, rb, db0, db1, nb0, nb1, lb, nbb, dn, stage, rstage, lsem, sems, vsem, osem,
 ):
     total = count[0]
     nblocks = (total + SPAN - 1) // SPAN
@@ -215,29 +238,35 @@
         first = blk * SPAN
         es, rs = eb.at[slot], rb.at[slot]
 
-        @pl.loop(0, SPAN // 16)
+        @pl.loop(0, SPAN // 32)
         def _(q):
             base = pl.multiple_of(q * 16 * GROUPS, 64)
-            for k in range(16):
-                j = first + q * 16 + k
-                db[slot_of(base, k), :] = td[row_of(dst_i[j]), :]
-                nb[slot_of(base, k), :] = td[row_of(neg_i[j]), :]
-
-        for ch in range(SPAN // CHUNK):
-            cols = tiles(nb[ch * CHUNK * GROUPS : (ch + 1) * CHUNK * GROUPS, :])
+            j = first + q * 16
+            gather_rows(
+                [
+                    (td, dst_i, j, db0),
+                    (td, dst_i, j + CHUNK, db1),
+                    (td, neg_i, j, nb0),
+                    (td, neg_i, j + CHUNK, nb1),
+                ],
+                base,
+                16,
+            )
+
+        for ch, nb in enumerate((nb0, nb1)):
+            cols = tiles(nb[...])
             for c in range(GROUPS):
                 nbb[ch * CHUNK : (ch + 1) * CHUNK, c * LANES : (c + 1) * LANES] = cols[c].astype(bf16)
 
         for c in fetches(blk, slot):
             c.wait()
 
-        @pl.loop(0, SPAN // CHUNK)
-        def _(ch):
-            r0 = pl.multiple_of(ch * CHUNK, CHUNK)
-            flat = pl.ds(pl.multiple_of(ch * CHUNK * GROUPS, CHUNK * GROUPS), CHUNK * GROUPS)
+        for ch, db in enumerate((db0, db1)):
+            r0 = ch * CHUNK
+            flat = pl.ds(ch * HALF, HALF)
             e = tiles(es[flat, :])
             r = tiles(rs[flat, :])
-            d = tiles(db[flat, :])
+            d = tiles(db[...])
             left = [(e[c] * r[c]).astype(bf16) for c in range(GROUPS)]
             leftf = [x.astype(f32) for x in left]
             prod = leftf[0] * d[0]
@@ -249,8 +278,11 @@
             negative = lax.dot_general(
                 lc, nbb[...], (((1,), (1,)), ((), ())), preferred_element_type=f32
             )
-            lane = lax.broadcasted_iota(jnp.int32, negative.shape, 1)
-            negative = jnp.where(lane < nneg, negative, -jnp.inf)
+            edge = nneg // LANES * LANES
+            lane = lax.broadcasted_iota(jnp.int32, (CHUNK, SPAN - edge), 1)
+            negative = jnp.concatenate(
+                [negative[:, :edge], jnp.where(lane < nneg - edge, negative[:, edge:], -jnp.inf)], axis=1
+            )
             top = jnp.maximum(positive, jnp.max(negative, axis=1, keepdims=True))
             e_pos = jnp.exp(positive - top)
             e_neg = jnp.exp(negative - top)
@@ -263,22 +295,24 @@
             dn[pl.ds(r0, CHUNK), :] = d_neg
             dl = jnp.dot(d_neg, nbb[...], preferred_element_type=f32)
             x = [d_pos * d[c] + dl[:, c * LANES : (c + 1) * LANES] for c in range(GROUPS)]
-            db[flat, :] = untiles([d_pos * leftf[c] for c in range(GROUPS)])
+            db[...] = untiles([d_pos * leftf[c] for c in range(GROUPS)])
             es[flat, :] = untiles([x[c] * e[c] for c in range(GROUPS)])
             rs[flat, :] = untiles([x[c] * r[c] for c in range(GROUPS)])
 
         put(blk, slot).start()
 
-        for ch in range(SPAN // CHUNK):
+        for ch, nb in enumerate((nb0, nb1)):
             part = lax.dot_general(
                 dn[:, ch * CHUNK : (ch + 1) * CHUNK], lb[...], (((0,), (0,)), ((), ())),
                 preferred_element_type=f32,
             )
-            nb[ch * CHUNK * GROUPS : (ch + 1) * CHUNK * GROUPS, :] = untiles(
+            nb[...] = untiles(
                 [part[:, c * LANES : (c + 1) * LANES] for c in range(GROUPS)]
             )
 
-        def scatter(j0, base, n):
+        def scatter(h, start, base, n):
+            db, nb, ev = ((db0, nb0), (db1, nb1))[h] + (es.at[pl.ds(h * HALF, HALF)],)
+            j0 = first + h * CHUNK + start
             for t in range(0, n, 3):
                 ks = list(range(t, min(t + 3, n)))
                 at = [slot_of(base, k) for k in ks]
@@ -286,18 +320,20 @@
                 dst = [(copies[i], row_of(dst_i[j0 + k]), db, at[i]) for i, k in enumerate(ks)]
                 neg = [(copies[i], row_of(neg_i[j0 + k]), nb, at[i]) for i, k in enumerate(ks)]
                 rel = [
-                    ((r0_acc, r1_acc)[i % 2], row_of(rid_i[j0 + k]), es, at[i])
+                    ((r0_acc, r1_acc)[i % 2], row_of(rid_i[j0 + k]), ev, at[i])
                     for i, k in enumerate(ks)
                 ]
                 add_rows(dst + rel[:2])
                 add_rows(neg + rel[2:])
 
-        @pl.loop(0, SPAN // 24)
-        def _(q):
-            scatter(first + q * 24, pl.multiple_of(q * 24 * GROUPS, 32), 24)
-
-        done = SPAN // 24 * 24
-        scatter(first + done, done * GROUPS, SPAN - done)
+        for h in (0, 1):
+
+            @pl.loop(0, CHUNK // 24)
+            def _(q):
+                scatter(h, q * 24, pl.multiple_of(q * 24 * GROUPS, 32), 24)
+
+            done = CHUNK // 24 * 24
+            scatter(h, done, done * GROUPS, CHUNK - done)
         return 0
 
     lax.fori_loop(0, nblocks, step, 0)
@@ -323,17 +359,17 @@
 
     @pl.loop(0, PIECES)
     def _(j):
-        slot = lax.rem(j, 2)
-
-        @pl.when(j >= 2)
+        slot = lax.rem(j, SLOTS)
+
+        @pl.when(j >= SLOTS)
         def _():
-            copy(j - 2, slot).wait()
+            copy(j - SLOTS, slot).wait()
 
         fill(j, stage.at[slot])
         copy(j, slot).start()
 
-    for j in (PIECES - 2, PIECES - 1):
-        copy(j, j % 2).wait()
+    for j in range(PIECES - SLOTS, PIECES):
+        copy(j, j % SLOTS).wait()
 
 
 def emit_halves(load, rows, lo_out, hi_out, stage, sem):
@@ -404,10 +440,12 @@
             pltpu.VMEM((rows * GROUPS, LANES), f32),
             pltpu.VMEM((-(-nrel // 8) * 8 * GROUPS, LANES), f32),
             pltpu.VMEM((2, 512, emb.shape[1]), bf16),
-            pltpu.VMEM((2, FLAT, LANES), f32),
-            pltpu.VMEM((2, FLAT, LANES), f32),
+            pltpu.VMEM((2, HALF, LANES), f32),
+            pltpu.VMEM((2, HALF, LANES), f32),
+            pltpu.VMEM((2, HALF, LANES), f32),
+            pltpu.VMEM((2, HALF, LANES), f32),
             pltpu.SemaphoreType.DMA((2,)),
-            pltpu.SemaphoreType.DMA((2, 2)),
+            pltpu.SemaphoreType.DMA((2, 4)),
         ],
         compiler_params=pltpu.CompilerParams(vmem_limit_bytes=VMEM),
         cost_estimate=pl.CostEstimate(flops=0, bytes_accessed=60_000_000, transcendentals=0),
@@ -438,17 +476,19 @@
             pltpu.VMEM((2, 512, dst_slab.shape[1]), bf16),
             pltpu.VMEM((2, FLAT, LANES), f32),
             pltpu.VMEM((2, FLAT, LANES), f32),
-            pltpu.VMEM((FLAT, LANES), f32),
-            pltpu.VMEM((FLAT, LANES), f32),
+            pltpu.VMEM((HALF, LANES), f32),
+            pltpu.VMEM((HALF, LANES), f32),
+            pltpu.VMEM((HALF, LANES), f32),
+            pltpu.VMEM((HALF, LANES), f32),
             pltpu.VMEM((SPAN, LANES * GROUPS), bf16),
             pltpu.VMEM((SPAN, LANES * GROUPS), bf16),
             pltpu.VMEM((SPAN, SPAN), bf16),
-            pltpu.VMEM((2, packed, LANES), bf16),
-            pltpu.VMEM((2, relrows, LANES), bf16),
+            pltpu.VMEM((SLOTS, packed, LANES), bf16),
+            pltpu.VMEM((SLOTS, relrows, LANES), bf16),
             pltpu.SemaphoreType.DMA((2,)),
             pltpu.SemaphoreType.DMA((2, 2)),
             pltpu.SemaphoreType.DMA((2,)),
-            pltpu.SemaphoreType.DMA((2,)),
+            pltpu.SemaphoreType.DMA((SLOTS,)),
         ],
         compiler_params=pltpu.CompilerParams(vmem_limit_bytes=VMEM),
         name="edge_blocks",
@@ -467,9 +507,9 @@
         scratch_shapes=[
             table, table, table, table,
             pltpu.VMEM((2, FLAT, LANES), f32),
-            pltpu.VMEM((2, packed, LANES), bf16),
+            pltpu.VMEM((SLOTS, packed, LANES), bf16),
             pltpu.SemaphoreType.DMA((2,)),
-            pltpu.SemaphoreType.DMA((2,)),
+            pltpu.SemaphoreType.DMA((SLOTS,)),
         ],
         compiler_params=pltpu.CompilerParams(vmem_limit_bytes=VMEM),
         cost_estimate=pl.CostEstimate(flops=0, bytes_accessed=60_000_000, transcendentals=0),
@@ -477,18 +517,32 @@
     )(count, src, values)
 
 
-def sum_kernel(x_ref, after_ref, out_ref):
-    out_ref[...] = jnp.sum(x_ref[...].astype(f32), axis=0)
-
-
-def sum_pieces(x, after):
+def sum_kernel(rep, x_ref, after_ref, keep_ref, send_ref):
+    n = keep_ref.shape[0]
+
+    def total(r):
+        at = pl.ds(pl.multiple_of(r * n, n), n)
+        out = x_ref[0, at, :].astype(f32)
+        for i in range(1, x_ref.shape[0]):
+            out = out + x_ref[i, at, :].astype(f32)
+        return out
+
+    keep_ref[...] = total(rep[0])
+    send_ref[...] = total(1 - rep[0]).astype(bf16)
+
+
+def sum_sides(rep, x, after):
+    n = x.shape[1] // 2
     return pl.pallas_call(
         sum_kernel,
-        out_shape=jax.ShapeDtypeStruct(x.shape[1:], f32),
-        in_specs=[pl.BlockSpec(memory_space=pltpu.VMEM), hbm()],
+        out_shape=(
+            jax.ShapeDtypeStruct((n, LANES), f32),
+            jax.ShapeDtypeStruct((n, LANES), bf16),
+        ),
+        in_specs=[smem(), pl.BlockSpec(memory_space=pltpu.VMEM), hbm()],
         compiler_params=pltpu.CompilerParams(vmem_limit_bytes=VMEM),
-        name="sum_pieces",
-    )(x, after)
+        name="sum_sides",
+    )(rep, x, after)
 
 
 def across(x, n):
@@ -498,22 +552,22 @@
     return jnp.concatenate([x[:n].T, x[n : 2 * n].T, x[2 * n : 3 * n].T, rest], axis=0)
 
 
-def update_kernel(a_ref, emb_ref, out_ref):
+def update_kernel(a_ref, b_ref, emb_ref, out_ref):
     width, n = emb_ref.shape
-    g = jnp.sum(a_ref[...].astype(f32), axis=0)
+    g = a_ref[...] + b_ref[...].astype(f32)
     new = (emb_ref[...].astype(f32) - 0.5 * across(g, n)).astype(bf16)
     for i in range(n // LANES):
         out_ref[i * width : (i + 1) * width, :] = new[:, i * LANES : (i + 1) * LANES]
 
 
-def update(a, emb):
+def update(a, b, emb):
     width, n = emb.shape
     return pl.pallas_call(
         update_kernel,
         out_shape=jax.ShapeDtypeStruct((width * n // LANES, LANES), bf16),
         compiler_params=pltpu.CompilerParams(vmem_limit_bytes=VMEM),
         name="update",
-    )(a, emb)
+    )(a, b, emb)
 
 
 def finish_kernel(place, a_ref, ar_ref, b0_ref, b1_ref, b2_ref, b3_ref, dirty_ref, up_ref, check_ref):
@@ -559,6 +613,11 @@
     )(order, x)
 
 
+def by_side(x):
+    sides = lax.axis_size("side")
+    return lax.all_to_all(x.reshape(sides, -1, LANES), "side", 0, 0, tiled=True)
+
+
 def around(x):
     return [x] + [shifted(x, "side", by) for by in (1, -1, 2)]
 
@@ -577,7 +636,6 @@
 ):
     rows, width = embeddings.shape
     nrel = relation.shape[0]
-    group = ("side", "rep")
     doms = lax.axis_size("dom")
     count = edge_counts.reshape(1)
     nneg = negative_ids.shape[-1]
@@ -598,9 +656,11 @@
     e_rows, r_rows = edge_rows(count, src, rid, embeddings, relation)
     *gdst, grel, values = edge_blocks(nneg, count, rid, dst, neg, dst_slab, e_rows, r_rows, nrel)
     returned = [shifted(g, "dom", 1) for g in gdst]
-    rel = lax.all_to_all(grel, group, 0, 0, tiled=True)
+    which = rep.reshape(1).astype(jnp.int32)
+    rel = by_side(grel)
     gsrc = source_rows(count, src, values, rows)
-    rel = sum_pieces(rel, gsrc[0])
+    rel, sent = sum_sides(which, rel, gsrc[0])
+    rel = rel + shifted(sent, "rep", 1).astype(f32)
     bit = 1
     while bit < doms:
         rel = rel + swapped(rel, "dom", bit)
@@ -610,10 +670,10 @@
     rel_order = (order % 4) * 2 + order // 4
     relation_grad = relation_out(rel_order, rel, relm, (width, nrel))
 
-    mine = [
-        update(lax.all_to_all(gsrc[h] + returned[h], group, 0, 0, tiled=True), own[h])
-        for h in (0, 1)
-    ]
+    mine = []
+    for h in (0, 1):
+        keep, sent = sum_sides(which, by_side(gsrc[h] + returned[h]), own[h])
+        mine.append(update(keep, shifted(sent, "rep", 1), own[h]))
     a4 = jnp.stack(around(mine[0]))
     parts = both_reps(a4) + around(jnp.stack(both_reps(mine[1])))
     updated, checkpoint = finish(place, parts, dirty[None, :], width)

time: 325 us -> 298 us (0.917)
  Pallas kernels: 182 us -> 140 us
  starting transfers between devices: 44.9 us -> 76.4 us
  waiting for transfers between devices: 55 us -> 41.5 us
    pallas_call x1, Pallas kernels: 115 us -> 80.1 us  [edge_blocks(): pl.pallas_call(functools.partial(block_kernel, nneg), out_shape=(half, ha...]
    all_to_all x3, starting transfers between devices: 20 us -> 35.5 us  [by_side(): return lax.all_to_all(x.reshape(sides, -1, LANES), 'side', 0, 0, tiled=True)]
    all_to_all x3, waiting for transfers between devices: 16.1 us -> 0.89 us  [by_side(): return lax.all_to_all(x.reshape(sides, -1, LANES), 'side', 0, 0, tiled=True)]
    ppermute x15 -> x18, waiting for transfers between devices: 13.6 us -> 26.6 us  [shifted(): return lax.ppermute(x, axis, [(i, (i + by) % count) for i in range(count)])]
    ppermute x4, waiting for transfers between devices: 25.3 us -> 14 us  [swapped(): return lax.ppermute(x, axis, [(i, i ^ bit) for i in range(count)])]
    ppermute x4, starting transfers between devices: 2.18 us -> 10.7 us  [swapped(): return lax.ppermute(x, axis, [(i, i ^ bit) for i in range(count)])]
    ppermute x15 -> x18, starting transfers between devices: 22.8 us -> 30.3 us  [shifted(): return lax.ppermute(x, axis, [(i, (i + by) % count) for i in range(count)])]
    pallas_call x1, Pallas kernels: 24.1 us -> 18.4 us  [source_rows(): pl.pallas_call(source_kernel, out_shape=(half, half), in_specs=[smem()] *...]
  transfers between devices with their start and end apart: 22 -> 25, of which waited for: 7 -> 13; matrix products, arithmetic and copies ran while one was open for 9% -> 8% of each run, Pallas kernels for 19% -> 18%
where the time goes in v4:
time: 298 us; the launch traced here: 295 us
  Pallas kernels  140 us (47%)
  starting transfers between devices  76.4 us (26%)
  waiting for transfers between devices  41.5 us (14%)
  local copies, waits for them, and re-layouts  23.6 us (8%)
  other arithmetic  12.1 us (4%)
    pallas_call x1, Pallas kernels, edge_blocks(): pl.pallas_call(functools.partial(block_kernel, nneg), out_shape=(half, ha...  80.1 us
    all_to_all x3, starting transfers between devices, by_side(): return lax.all_to_all(x.reshape(sides, -1, LANES), 'side', 0, 0, tiled=True)  35.5 us
    ppermute x18, starting transfers between devices, shifted(): return lax.ppermute(x, axis, [(i, (i + by) % count) for i in range(count)])  30.3 us
    ppermute x18, waiting for transfers between devices, shifted(): return lax.ppermute(x, axis, [(i, (i + by) % count) for i in range(count)])  26.6 us
    pallas_call x1, Pallas kernels, edge_rows(): pl.pallas_call(edge_rows_kernel, out_shape=(shape, shape), in_specs=[smem...  20.8 us
    pallas_call x1, Pallas kernels, source_rows(): pl.pallas_call(source_kernel, out_shape=(half, half), in_specs=[smem()] *...  18.4 us
    unnamed x44, local copies, waits for them, and re-layouts  15.7 us
    ppermute x4, waiting for transfers between devices, swapped(): return lax.ppermute(x, axis, [(i, i ^ bit) for i in range(count)])  14 us
  transfers between devices with their start and end apart: 25, of which 13 were waited for; matrix products, arithmetic and copies ran while one was open for 8% of the time, Pallas kernels for 18%

profile of v4, /device:TPU:96, one launch (start us, length us, event | category | flops | bytes accessed | tf_op | source)
XLA Modules:
  0.0 295.1 jit_solution(11159446999272794479)
XLA Ops:
  0.7 6.1 %copy.14.emb_hbm = bf16[4096,400]{1,0:T(8,128)(2,1)} copy(bf16[4096,400]{0,1:T(8,128)(2,1)} %param.8) | data formatting | bytes 6553600 | tf_op args[0]
  7.5 0.6 broadcast_multiply_fusion.2
  8.2 2.2 copy.15.rel_ref
  10.4 0.6 copy.19
  11.0 0.6 broadcast_multiply_fusion.1
  11.6 20.8 %edge_rows.1 = (f32[8,4096,128]{2,1,0:T(8,128)}, f32[8,4096,128]{2,1,0:T(8,128)}) custom-call(s32[1]{0:T(128)} %bitcast.36.count, s32[8192]{0:T(1024)} %bitcast.47, s32[8192]{0:T(1024)} %bitcast.49, bf16[4096,400]{1,0:T(8,128)(2,1)} %copy.14.emb_hbm, f32[1345,400]{1,0:T(8,128)} %copy.15.rel_ref), custom_call_target="tpu_custom_call" | custom-call | bytes 60000000 | tf_op jit(solution)/shard_map/edge_rows/pallas_call | solution.py:434
  32.4 0.6 broadcast_multiply_fusion
  33.1 4.2 %collective-permute-done = bf16[4096,400]{0,1:T(8,128)(2,1)} collective-permute-done((bf16[4096,400]{0,1:T(8,128)(2,1)}, bf16[4096,400]{0,1:T(8,128)(2,1)}, u32[]{:S(2)}, u32[]{:S(2)}) %collective-permute-start) | collective-permute-done | bytes 3276832 | tf_op jit(solution)/shard_map/ppermute | solution.py:27
  37.2 6.0 %copy.16.dst_hbm = bf16[4096,400]{1,0:T(8,128)(2,1)} copy(bf16[4096,400]{0,1:T(8,128)(2,1)} %collective-permute-done) | data formatting | bytes 6553600 | tf_op jit(solution)/shard_map/ppermute | solution.py:27
  43.2 80.1 %edge_blocks.1 = (bf16[8,800,128]{2,1,0:T(8,128)(2,1)}, bf16[8,800,128]{2,1,0:T(8,128)(2,1)}, bf16[8,640,128]{2,1,0:T(8,128)(2,1)}, f32[8,4096,128]{2,1,0:T(8,128)}) custom-call(s32[1]{0:T(128)} %bitcast.37.count, s32[8192]{0:T(1024)} %bitcast.50, s32[8192]{0:T(1024)} %bitcast.56, s32[8192]{0:T(1024)} %bitcast.55, bf16[4096,400]{1,0:T(8,128)(2,1)} %copy.16.dst_hbm, ...), custom_call_target="tpu_custom_call" | custom-call | tf_op jit(solution)/shard_map/edge_blocks/pallas_call | solution.py:464
  123.4 27.5 %all-to-all-start.2 = ((bf16[4,1280,128]{2,1,0:T(8,128)(2,1)}), bf16[4,1280,128]{2,1,0:T(8,128)(2,1)S(1)}, u32[]{:S(2)}, u32[]{:S(2)}) async-start(bf16[4,1280,128]{2,1,0:T(8,128)(2,1)} %bitcast.42), calls=%async_computation.2 | async-start | bytes 2621440 | tf_op jit(solution)/shard_map/all_to_all | solution.py:618
  150.9 18.4 %source_rows.1 = (bf16[8,800,128]{2,1,0:T(8,128)(2,1)}, bf16[8,800,128]{2,1,0:T(8,128)(2,1)}) custom-call(s32[1]{0:T(128)} %bitcast.38.count, s32[8192]{0:T(1024)} %bitcast.48, f32[8,4096,128]{2,1,0:T(8,128)} %get-tuple-element.22.v_hbm), custom_call_target="tpu_custom_call" | custom-call | bytes 60000000 | tf_op jit(solution)/shard_map/source_rows/pallas_call | solution.py:502
  169.3 3.0 %add.84 = bf16[8,800,128]{2,1,0:T(8,128)(2,1)} add(bf16[8,800,128]{2,1,0:T(8,128)(2,1)} %get-tuple-element.23.after_ref, bf16[8,800,128]{2,1,0:T(8,128)(2,1)S(1)} %collective-permute-done.1) | non-fusion elementwise | flops 819200 | bytes 4915200 | tf_op jit(solution)/shard_map/add | solution.py:675
  172.3 1.1 copy-done.1
  173.4 3.6 %all-to-all-start = ((bf16[4,1600,128]{2,1,0:T(8,128)(2,1)}), bf16[4,1600,128]{2,1,0:T(8,128)(2,1)S(1)}, u32[]{:S(2)}, u32[]{:S(2)}) async-start(bf16[4,1600,128]{2,1,0:T(8,128)(2,1)} %bitcast.40), calls=%async_computation | async-start | bytes 3276800 | tf_op jit(solution)/shard_map/all_to_all | solution.py:618
  177.0 2.2 sum_sides.5
  179.2 6.2 %collective-permute-start.13 = (bf16[640,128]{1,0:T(8,128)(2,1)}, bf16[640,128]{1,0:T(8,128)(2,1)S(1)}, u32[]{:S(2)}, u32[]{:S(2)}) collective-permute-start(bf16[640,128]{1,0:T(8,128)(2,1)} %get-tuple-element.35), channel_id=1, source_target_pairs={{0,1},{1,0},{2,3},{3,2},{4,5},{5,4},{6,7},{7,6},{8,9},{9,8},{10,11... | collective-permute-start | bytes 491528 | tf_op jit(solution)/shard_map/ppermute | solution.py:27
  185.4 4.0 %collective-permute-done.13 = bf16[640,128]{1,0:T(8,128)(2,1)S(1)} collective-permute-done((bf16[640,128]{1,0:T(8,128)(2,1)}, bf16[640,128]{1,0:T(8,128)(2,1)S(1)}, u32[]{:S(2)}, u32[]{:S(2)}) %collective-permute-start.13) | collective-permute-done | bytes 163872 | tf_op jit(solution)/shard_map/ppermute | solution.py:27
  189.4 1.0 convert_add_fusion
  190.4 1.5 collective-permute-start.14
  191.9 1.3 collective-permute-done.14
  193.2 0.8 collective-permute-start.15
  194.0 3.0 %add.87 = bf16[8,800,128]{2,1,0:T(8,128)(2,1)} add(bf16[8,800,128]{2,1,0:T(8,128)(2,1)S(1)} %copy-done.5, bf16[8,800,128]{2,1,0:T(8,128)(2,1)} %collective-permute-done.7) | non-fusion elementwise | flops 819200 | bytes 4915200 | tf_op jit(solution)/shard_map/add | solution.py:675
  197.0 0.9 all-to-all-done.x_ref
  197.9 1.2 copy-done
  199.1 4.3 %all-to-all-start.1 = ((bf16[4,1600,128]{2,1,0:T(8,128)(2,1)}), bf16[4,1600,128]{2,1,0:T(8,128)(2,1)}, u32[]{:S(2)}, u32[]{:S(2)}) async-start(bf16[4,1600,128]{2,1,0:T(8,128)(2,1)} %bitcast.39), calls=%async_computation.1 | async-start | bytes 3276800 | tf_op jit(solution)/shard_map/all_to_all | solution.py:618
  203.5 3.9 %collective-permute-start.16 = (f32[640,128]{1,0:T(8,128)S(1)}, f32[640,128]{1,0:T(8,128)S(1)}, u32[]{:S(2)}, u32[]{:S(2)}) collective-permute-start(f32[640,128]{1,0:T(8,128)S(1)} %add.94), channel_id=1, source_target_pairs={{0,32},{8,40},{16,48},{24,56},{32,0},{40,8},{48,16},{56,24},{64,96... | collective-permute-start | bytes 983048 | tf_op jit(solution)/shard_map/ppermute | solution.py:631
  207.4 8.1 %collective-permute-done.16 = f32[640,128]{1,0:T(8,128)S(1)} collective-permute-done((f32[640,128]{1,0:T(8,128)S(1)}, f32[640,128]{1,0:T(8,128)S(1)}, u32[]{:S(2)}, u32[]{:S(2)}) %collective-permute-start.16) | collective-permute-done | bytes 327712 | tf_op jit(solution)/shard_map/ppermute | solution.py:631
  215.5 4.5 %collective-permute-start.17 = (f32[640,128]{1,0:T(8,128)S(1)}, f32[640,128]{1,0:T(8,128)S(1)}, u32[]{:S(2)}, u32[]{:S(2)}) collective-permute-start(f32[640,128]{1,0:T(8,128)S(1)} %add.95), channel_id=1, source_target_pairs={{0,64},{8,72},{16,80},{24,88},{32,96},{40,104},{48,112},{56,120},{... | collective-permute-start | bytes 983048 | tf_op jit(solution)/shard_map/ppermute | solution.py:631
  220.0 0.1 broadcast_add_fusion
  220.1 1.8 dynamic-slice_bitcast_fusion
  221.9 4.6 %collective-permute-done.17 = f32[640,128]{1,0:T(8,128)S(1)} collective-permute-done((f32[640,128]{1,0:T(8,128)S(1)}, f32[640,128]{1,0:T(8,128)S(1)}, u32[]{:S(2)}, u32[]{:S(2)}) %collective-permute-start.17) | collective-permute-done | bytes 327712 | tf_op jit(solution)/shard_map/ppermute | solution.py:631
  226.6 6.1 %collective-permute-start.18 = (bf16[640,128]{1,0:T(8,128)(2,1)S(1)}, bf16[640,128]{1,0:T(8,128)(2,1)S(1)}, u32[]{:S(2)}, u32[]{:S(2)}) collective-permute-start(bf16[640,128]{1,0:T(8,128)(2,1)S(1)} %get-tuple-element.38), channel_id=1, source_target_pairs={{0,1},{1,0},{2,3},{3,2},{4,5},{5,4},{6,7},{7,6},{8,9},{9,8},{10,11... | collective-permute-start | bytes 491528 | tf_op jit(solution)/shard_map/ppermute | solution.py:27
  232.7 2.4 sum_sides.3
  235.1 2.4 sum_sides.4
  237.5 3.5 %collective-permute-start.8 = (bf16[800,128]{1,0:T(8,128)(2,1)}, bf16[800,128]{1,0:T(8,128)(2,1)S(1)}, u32[]{:S(2)}, u32[]{:S(2)}) collective-permute-start(bf16[800,128]{1,0:T(8,128)(2,1)} %get-tuple-element.30), channel_id=1, source_target_pairs={{0,1},{1,0},{2,3},{3,2},{4,5},{5,4},{6,7},{7,6},{8,9},{9,8},{10,11... | collective-permute-start | bytes 614408 | tf_op jit(solution)/shard_map/ppermute | solution.py:27
  241.0 3.7 %collective-permute-done.2.b_ref = bf16[800,128]{1,0:T(8,128)(2,1)S(1)} collective-permute-done((bf16[800,128]{1,0:T(8,128)(2,1)}, bf16[800,128]{1,0:T(8,128)(2,1)S(1)}, u32[]{:S(2)}, u32[]{:S(2)}) %collective-permute-start.2) | collective-permute-done | bytes 204832 | tf_op jit(solution)/shard_map/ppermute | solution.py:27
  244.7 0.7 copy-done.13
  245.4 2.1 update.2
  247.5 1.3 collective-permute-start.3
  248.8 1.9 collective-permute-start.4
  250.7 1.7 collective-permute-start.5
  252.5 1.0 sort.17
  253.5 0.5 collective-permute-start.19
  254.1 2.8 collective-permute-start.20
  256.8 2.1 update.3
  259.0 0.1 collective-permute-start.9
  259.1 1.7 collective-permute-done.5
  260.8 0.7 copy-done.11
  261.4 1.2 pad_maximum_fusion.a_ref
  262.7 2.0 collective-permute-start.6
  264.7 0.5 fusion.1.order
  265.2 0.6 collective-permute-start.21
  265.8 3.0 %collective-permute-done.9 = bf16[800,128]{1,0:T(8,128)(2,1)S(1)} collective-permute-done((bf16[800,128]{1,0:T(8,128)(2,1)}, bf16[800,128]{1,0:T(8,128)(2,1)S(1)}, u32[]{:S(2)}, u32[]{:S(2)}) %collective-permute-start.9) | collective-permute-done | bytes 204832 | tf_op jit(solution)/shard_map/ppermute | solution.py:27
  268.9 3.2 %collective-permute-start.11 = (bf16[2,800,128]{2,1,0:T(8,128)(2,1)S(1)}, bf16[2,800,128]{2,1,0:T(8,128)(2,1)}, u32[]{:S(2)}, u32[]{:S(2)}) collective-permute-start(bf16[2,800,128]{2,1,0:T(8,128)(2,1)S(1)} %pad_maximum_fusion.1.b0_ref), channel_id=1, source_target_pairs={{0,6},{2,0},{4,2},{6,4},{1,7},{3,1},{5,3},{7,5},{8,14},{10,8},{12,... | collective-permute-start | bytes 1228808 | tf_op jit(solution)/shard_map/ppermute | solution.py:27
  272.2 1.0 constant_dynamic-update-slice_fusion.2
  273.2 1.0 constant_dynamic-update-slice_fusion.1
  274.2 3.2 %collective-permute-done.21 = bf16[2,640,128]{2,1,0:T(8,128)(2,1)S(1)} collective-permute-done((bf16[2,640,128]{2,1,0:T(8,128)(2,1)S(1)}, bf16[2,640,128]{2,1,0:T(8,128)(2,1)S(1)}, u32[]{:S(2)}, u32[]{:S(2)}) %collective-permute-start.21) | collective-permute-done | bytes 327712 | tf_op jit(solution)/shard_map/ppermute | solution.py:27
  277.5 1.0 copy-done.4
  278.5 3.5 %relation_out.1 = f32[400,1345]{1,0:T(8,128)} custom-call(s32[8]{0:T(128)} %fusion.1.order, bf16[8,640,128]{2,1,0:T(8,128)(2,1)} %copy-done.4), custom_call_target="tpu_custom_call" | custom-call | tf_op jit(solution)/shard_map/relation_out/pallas_call | solution.py:607
  282.1 2.4 collective-permute-done.10.b1_ref
  284.5 2.8 collective-permute-done.11.b2_ref
  287.3 1.7 collective-permute-done.12.b3_ref
  289.0 6.2 %finish.1 = (bf16[400,4096]{1,0:T(8,128)(2,1)}, bf16[400,4096]{1,0:T(8,128)(2,1)}) custom-call(s32[8]{0:T(128)} %copy-done.18, bf16[4,800,128]{2,1,0:T(8,128)(2,1)} %copy-done.2, bf16[4,800,128]{2,1,0:T(8,128)(2,1)} %collective-permute-done.6.ar_ref, bf16[2,800,128]{2,1,0:T(8,128)(2,1)} %copy-done.6, bf16[2,800,128]{2,1,0:T(8,128)(2,1)} %collective-permute-done.10.b1_ref, ...), custom_call_target="tpu_custom_call" | custom-call | tf_op jit(solution)/shard_map/finish/pallas_call | solution.py:590
  (63 shorter events, 0.7 us)
Async XLA Ops:
  0.6 6.9 %copy-start.14 = (s32[1,1,1,8192]{3,2,1,0:T(1,128)S(1)}, s32[1,1,1,8192]{3,2,1,0:T(1,128)}, u32[]{:S(2)}) copy-start(s32[1,1,1,8192]{3,2,1,0:T(1,128)} %param.10) | copy-start | bytes 98308
  0.6 7.5 %copy-start.3 = (f32[1345,400]{0,1:T(8,128)S(1)}, f32[1345,400]{0,1:T(8,128)}, u32[]{:S(2)}) copy-start(f32[1345,400]{0,1:T(8,128)} %param.9) | copy-start | bytes 6456004
  0.7 36.6 %collective-permute-start = (bf16[4096,400]{0,1:T(8,128)(2,1)}, bf16[4096,400]{0,1:T(8,128)(2,1)}, u32[]{:S(2)}, u32[]{:S(2)}) collective-permute-start(bf16[4096,400]{0,1:T(8,128)(2,1)} %param.8), channel_id=1, source_target_pairs={{0,120},{8,0},{16,8},{24,16},{32,24},{40,32},{48,40},{56,48},{64,5... | collective-permute-start | bytes 9830408 | tf_op jit(solution)/shard_map/ppermute | solution.py:27
  8.2 2.2 copy-start.15
  8.2 2.8 copy-start.16
  11.6 20.8 %copy-start.17 = (s32[1,1,1,8192]{3,2,1,0:T(1,128)S(1)}, s32[1,1,1,8192]{3,2,1,0:T(1,128)}, u32[]{:S(2)}) copy-start(s32[1,1,1,8192]{3,2,1,0:T(1,128)} %param.12) | copy-start | bytes 98308
  123.3 46.0 %collective-permute-start.1 = (bf16[8,800,128]{2,1,0:T(8,128)(2,1)}, bf16[8,800,128]{2,1,0:T(8,128)(2,1)S(1)}, u32[]{:S(2)}, u32[]{:S(2)}) collective-permute-start(bf16[8,800,128]{2,1,0:T(8,128)(2,1)} %get-tuple-element.24), channel_id=1, source_target_pairs={{0,8},{8,16},{16,24},{24,32},{32,40},{40,48},{48,56},{56,64},{64,7... | collective-permute-start | bytes 4915208 | tf_op jit(solution)/shard_map/ppermute | solution.py:27
  123.4 48.9 %all-to-all-start.2 = ((bf16[4,1280,128]{2,1,0:T(8,128)(2,1)}), bf16[4,1280,128]{2,1,0:T(8,128)(2,1)S(1)}, u32[]{:S(2)}, u32[]{:S(2)}) async-start(bf16[4,1280,128]{2,1,0:T(8,128)(2,1)} %bitcast.42), calls=%async_computation.2 | async-start | bytes 2621440 | tf_op jit(solution)/shard_map/all_to_all | solution.py:618
  150.9 43.1 %collective-permute-start.7 = (bf16[8,800,128]{2,1,0:T(8,128)(2,1)}, bf16[8,800,128]{2,1,0:T(8,128)(2,1)}, u32[]{:S(2)}, u32[]{:S(2)}) collective-permute-start(bf16[8,800,128]{2,1,0:T(8,128)(2,1)} %get-tuple-element.28), channel_id=1, source_target_pairs={{0,8},{8,16},{16,24},{24,32},{32,40},{40,48},{48,56},{56,64},{64,7... | collective-permute-start | bytes 4915208 | tf_op jit(solution)/shard_map/ppermute | solution.py:27
  172.3 1.1 copy-start.1
  173.4 24.5 %all-to-all-start = ((bf16[4,1600,128]{2,1,0:T(8,128)(2,1)}), bf16[4,1600,128]{2,1,0:T(8,128)(2,1)S(1)}, u32[]{:S(2)}, u32[]{:S(2)}) async-start(bf16[4,1600,128]{2,1,0:T(8,128)(2,1)} %bitcast.40), calls=%async_computation | async-start | bytes 3276800 | tf_op jit(solution)/shard_map/all_to_all | solution.py:618
  179.2 14.8 %copy-start.5 = (bf16[8,800,128]{2,1,0:T(8,128)(2,1)S(1)}, bf16[8,800,128]{2,1,0:T(8,128)(2,1)}, u32[]{:S(2)}) copy-start(bf16[8,800,128]{2,1,0:T(8,128)(2,1)} %get-tuple-element.27) | copy-start | bytes 4915204
  179.2 10.2 %collective-permute-start.13 = (bf16[640,128]{1,0:T(8,128)(2,1)}, bf16[640,128]{1,0:T(8,128)(2,1)S(1)}, u32[]{:S(2)}, u32[]{:S(2)}) collective-permute-start(bf16[640,128]{1,0:T(8,128)(2,1)} %get-tuple-element.35), channel_id=1, source_target_pairs={{0,1},{1,0},{2,3},{3,2},{4,5},{5,4},{6,7},{7,6},{8,9},{9,8},{10,11... | collective-permute-start | bytes 491528 | tf_op jit(solution)/shard_map/ppermute | solution.py:27
  190.4 2.8 collective-permute-start.14
  193.2 10.2 %collective-permute-start.15 = (f32[640,128]{1,0:T(8,128)S(1)}, f32[640,128]{1,0:T(8,128)S(1)}, u32[]{:S(2)}, u32[]{:S(2)}) collective-permute-start(f32[640,128]{1,0:T(8,128)S(1)} %add.93), channel_id=1, source_target_pairs={{0,16},{8,24},{16,0},{24,8},{32,48},{40,56},{48,32},{56,40},{64,80... | collective-permute-start | bytes 983048 | tf_op jit(solution)/shard_map/ppermute | solution.py:631
  197.9 1.2 copy-start
  199.1 36.0 %all-to-all-start.1 = ((bf16[4,1600,128]{2,1,0:T(8,128)(2,1)}), bf16[4,1600,128]{2,1,0:T(8,128)(2,1)}, u32[]{:S(2)}, u32[]{:S(2)}) async-start(bf16[4,1600,128]{2,1,0:T(8,128)(2,1)} %bitcast.39), calls=%async_computation.1 | async-start | bytes 3276800 | tf_op jit(solution)/shard_map/all_to_all | solution.py:618
  203.5 12.0 %collective-permute-start.16 = (f32[640,128]{1,0:T(8,128)S(1)}, f32[640,128]{1,0:T(8,128)S(1)}, u32[]{:S(2)}, u32[]{:S(2)}) collective-permute-start(f32[640,128]{1,0:T(8,128)S(1)} %add.94), channel_id=1, source_target_pairs={{0,32},{8,40},{16,48},{24,56},{32,0},{40,8},{48,16},{56,24},{64,96... | collective-permute-start | bytes 983048 | tf_op jit(solution)/shard_map/ppermute | solution.py:631
  215.5 11.0 %collective-permute-start.17 = (f32[640,128]{1,0:T(8,128)S(1)}, f32[640,128]{1,0:T(8,128)S(1)}, u32[]{:S(2)}, u32[]{:S(2)}) collective-permute-start(f32[640,128]{1,0:T(8,128)S(1)} %add.95), channel_id=1, source_target_pairs={{0,64},{8,72},{16,80},{24,88},{32,96},{40,104},{48,112},{56,120},{... | collective-permute-start | bytes 983048 | tf_op jit(solution)/shard_map/ppermute | solution.py:631
  226.6 26.9 %collective-permute-start.18 = (bf16[640,128]{1,0:T(8,128)(2,1)S(1)}, bf16[640,128]{1,0:T(8,128)(2,1)S(1)}, u32[]{:S(2)}, u32[]{:S(2)}) collective-permute-start(bf16[640,128]{1,0:T(8,128)(2,1)S(1)} %get-tuple-element.38), channel_id=1, source_target_pairs={{0,1},{1,0},{2,3},{3,2},{4,5},{5,4},{6,7},{7,6},{8,9},{9,8},{10,11... | collective-permute-start | bytes 491528 | tf_op jit(solution)/shard_map/ppermute | solution.py:27
  235.0 9.6 %collective-permute-start.2 = (bf16[800,128]{1,0:T(8,128)(2,1)}, bf16[800,128]{1,0:T(8,128)(2,1)S(1)}, u32[]{:S(2)}, u32[]{:S(2)}) collective-permute-start(bf16[800,128]{1,0:T(8,128)(2,1)} %get-tuple-element.26), channel_id=1, source_target_pairs={{0,1},{1,0},{2,3},{3,2},{4,5},{5,4},{6,7},{7,6},{8,9},{9,8},{10,11... | collective-permute-start | bytes 614408 | tf_op jit(solution)/shard_map/ppermute | solution.py:27
  237.5 16.6 %collective-permute-start.8 = (bf16[800,128]{1,0:T(8,128)(2,1)}, bf16[800,128]{1,0:T(8,128)(2,1)S(1)}, u32[]{:S(2)}, u32[]{:S(2)}) collective-permute-start(bf16[800,128]{1,0:T(8,128)(2,1)} %get-tuple-element.30), channel_id=1, source_target_pairs={{0,1},{1,0},{2,3},{3,2},{4,5},{5,4},{6,7},{7,6},{8,9},{9,8},{10,11... | collective-permute-start | bytes 614408 | tf_op jit(solution)/shard_map/ppermute | solution.py:27
  244.7 0.7 copy-start.13
  247.5 13.9 %copy-start.7 = (bf16[800,128]{1,0:T(8,128)(2,1)S(1)}, bf16[800,128]{1,0:T(8,128)(2,1)}, u32[]{:S(2)}) copy-start(bf16[800,128]{1,0:T(8,128)(2,1)} %update.2) | copy-start | bytes 614404
  247.5 11.5 %collective-permute-start.3 = (bf16[800,128]{1,0:T(8,128)(2,1)}, bf16[800,128]{1,0:T(8,128)(2,1)S(1)}, u32[]{:S(2)}, u32[]{:S(2)}) collective-permute-start(bf16[800,128]{1,0:T(8,128)(2,1)} %update.2), channel_id=1, source_target_pairs={{0,2},{2,4},{4,6},{6,0},{1,3},{3,5},{5,7},{7,1},{8,10},{10,12},{12... | collective-permute-start | bytes 614408 | tf_op jit(solution)/shard_map/ppermute | solution.py:27
  248.8 10.3 %collective-permute-start.4 = (bf16[800,128]{1,0:T(8,128)(2,1)}, bf16[800,128]{1,0:T(8,128)(2,1)S(1)}, u32[]{:S(2)}, u32[]{:S(2)}) collective-permute-start(bf16[800,128]{1,0:T(8,128)(2,1)} %update.2), channel_id=1, source_target_pairs={{0,6},{2,0},{4,2},{6,4},{1,7},{3,1},{5,3},{7,5},{8,14},{10,8},{12,... | collective-permute-start | bytes 614408 | tf_op jit(solution)/shard_map/ppermute | solution.py:27
  250.7 10.0 %collective-permute-start.5 = (bf16[800,128]{1,0:T(8,128)(2,1)}, bf16[800,128]{1,0:T(8,128)(2,1)S(1)}, u32[]{:S(2)}, u32[]{:S(2)}) collective-permute-start(bf16[800,128]{1,0:T(8,128)(2,1)} %update.2), channel_id=1, source_target_pairs={{0,4},{2,6},{4,0},{6,2},{1,5},{3,7},{5,1},{7,3},{8,12},{10,14},{12... | collective-permute-start | bytes 614408 | tf_op jit(solution)/shard_map/ppermute | solution.py:27
  252.5 10.2 %copy-start.18 = (s32[8]{0:T(128)}, s32[8]{0:T(128)S(1)}, u32[]{:S(2)}) copy-start(s32[8]{0:T(128)S(1)} %pad_add_fusion.place) | copy-start | bytes 100
  253.5 15.4 %collective-permute-start.19 = (bf16[2,640,128]{2,1,0:T(8,128)(2,1)S(1)}, bf16[2,640,128]{2,1,0:T(8,128)(2,1)}, u32[]{:S(2)}, u32[]{:S(2)}) collective-permute-start(bf16[2,640,128]{2,1,0:T(8,128)(2,1)S(1)} %pad_maximum_fusion.2), channel_id=1, source_target_pairs={{0,2},{2,4},{4,6},{6,0},{1,3},{3,5},{5,7},{7,1},{8,10},{10,12},{12... | collective-permute-start | bytes 983048 | tf_op jit(solution)/shard_map/ppermute | solution.py:27
  254.1 2.8 copy-start.12
  254.1 18.1 %collective-permute-start.20 = (bf16[2,640,128]{2,1,0:T(8,128)(2,1)S(1)}, bf16[2,640,128]{2,1,0:T(8,128)(2,1)}, u32[]{:S(2)}, u32[]{:S(2)}) collective-permute-start(bf16[2,640,128]{2,1,0:T(8,128)(2,1)S(1)} %pad_maximum_fusion.2), channel_id=1, source_target_pairs={{0,6},{2,0},{4,2},{6,4},{1,7},{3,1},{5,3},{7,5},{8,14},{10,8},{12,... | collective-permute-start | bytes 983048 | tf_op jit(solution)/shard_map/ppermute | solution.py:27
  259.0 9.8 %copy-start.8 = (bf16[800,128]{1,0:T(8,128)(2,1)S(1)}, bf16[800,128]{1,0:T(8,128)(2,1)}, u32[]{:S(2)}) copy-start(bf16[800,128]{1,0:T(8,128)(2,1)} %update.3) | copy-start | bytes 614404
  259.0 1.8 copy-start.9
  259.0 9.8 %collective-permute-start.9 = (bf16[800,128]{1,0:T(8,128)(2,1)}, bf16[800,128]{1,0:T(8,128)(2,1)S(1)}, u32[]{:S(2)}, u32[]{:S(2)}) collective-permute-start(bf16[800,128]{1,0:T(8,128)(2,1)} %update.3), channel_id=1, source_target_pairs={{0,1},{1,0},{2,3},{3,2},{4,5},{5,4},{6,7},{7,6},{8,9},{9,8},{10,11... | collective-permute-start | bytes 614408 | tf_op jit(solution)/shard_map/ppermute | solution.py:27
  259.1 1.7 copy-start.10
  260.7 0.7 copy-start.11
  262.7 19.4 %copy-start.2 = (bf16[4,800,128]{2,1,0:T(8,128)(2,1)}, bf16[4,800,128]{2,1,0:T(8,128)(2,1)S(1)}, u32[]{:S(2)}) copy-start(bf16[4,800,128]{2,1,0:T(8,128)(2,1)S(1)} %pad_maximum_fusion.a_ref) | copy-start | bytes 2457604
  262.7 26.3 %collective-permute-start.6 = (bf16[4,800,128]{2,1,0:T(8,128)(2,1)S(1)}, bf16[4,800,128]{2,1,0:T(8,128)(2,1)}, u32[]{:S(2)}, u32[]{:S(2)}) collective-permute-start(bf16[4,800,128]{2,1,0:T(8,128)(2,1)S(1)} %pad_maximum_fusion.a_ref), channel_id=1, source_target_pairs={{0,1},{1,0},{2,3},{3,2},{4,5},{5,4},{6,7},{7,6},{8,9},{9,8},{10,11... | collective-permute-start | bytes 2457608 | tf_op jit(solution)/shard_map/ppermute | solution.py:27
  265.2 12.3 %collective-permute-start.21 = (bf16[2,640,128]{2,1,0:T(8,128)(2,1)S(1)}, bf16[2,640,128]{2,1,0:T(8,128)(2,1)S(1)}, u32[]{:S(2)}, u32[]{:S(2)}) collective-permute-start(bf16[2,640,128]{2,1,0:T(8,128)(2,1)S(1)} %pad_maximum_fusion.2), channel_id=1, source_target_pairs={{0,4},{2,6},{4,0},{6,2},{1,5},{3,7},{5,1},{7,3},{8,12},{10,14},{12... | collective-permute-start | bytes 983048 | tf_op jit(solution)/shard_map/ppermute | solution.py:27
  268.8 13.3 %copy-start.6 = (bf16[2,800,128]{2,1,0:T(8,128)(2,1)}, bf16[2,800,128]{2,1,0:T(8,128)(2,1)S(1)}, u32[]{:S(2)}) copy-start(bf16[2,800,128]{2,1,0:T(8,128)(2,1)S(1)} %pad_maximum_fusion.1.b0_ref) | copy-start | bytes 1228804
  268.8 15.7 %collective-permute-start.10 = (bf16[2,800,128]{2,1,0:T(8,128)(2,1)S(1)}, bf16[2,800,128]{2,1,0:T(8,128)(2,1)}, u32[]{:S(2)}, u32[]{:S(2)}) collective-permute-start(bf16[2,800,128]{2,1,0:T(8,128)(2,1)S(1)} %pad_maximum_fusion.1.b0_ref), channel_id=1, source_target_pairs={{0,2},{2,4},{4,6},{6,0},{1,3},{3,5},{5,7},{7,1},{8,10},{10,12},{12... | collective-permute-start | bytes 1228808 | tf_op jit(solution)/shard_map/ppermute | solution.py:27
  268.9 18.3 %collective-permute-start.11 = (bf16[2,800,128]{2,1,0:T(8,128)(2,1)S(1)}, bf16[2,800,128]{2,1,0:T(8,128)(2,1)}, u32[]{:S(2)}, u32[]{:S(2)}) collective-permute-start(bf16[2,800,128]{2,1,0:T(8,128)(2,1)S(1)} %pad_maximum_fusion.1.b0_ref), channel_id=1, source_target_pairs={{0,6},{2,0},{4,2},{6,4},{1,7},{3,1},{5,3},{7,5},{8,14},{10,8},{12,... | collective-permute-start | bytes 1228808 | tf_op jit(solution)/shard_map/ppermute | solution.py:27
  272.1 16.8 %collective-permute-start.12 = (bf16[2,800,128]{2,1,0:T(8,128)(2,1)S(1)}, bf16[2,800,128]{2,1,0:T(8,128)(2,1)}, u32[]{:S(2)}, u32[]{:S(2)}) collective-permute-start(bf16[2,800,128]{2,1,0:T(8,128)(2,1)S(1)} %pad_maximum_fusion.1.b0_ref), channel_id=1, source_target_pairs={{0,4},{2,6},{4,0},{6,2},{1,5},{3,7},{5,1},{7,3},{8,12},{10,14},{12... | collective-permute-start | bytes 1228808 | tf_op jit(solution)/shard_map/ppermute | solution.py:27
  277.5 1.1 copy-start.4

commit v5 on v4

--- a/solution.py
+++ b/solution.py
@@ -15,6 +15,9 @@
 CHUNK = SPAN // 2
 HALF = FLAT // 2
 PIECES = 8
+INE = 512
+INN = 256
+NCOPY = 3
 SLOTS = 4
 VMEM = 61 * 2**20
 
@@ -261,7 +264,7 @@
         for c in fetches(blk, slot):
             c.wait()
 
-        for ch, db in enumerate((db0, db1)):
+        def dense(ch, db):
             r0 = ch * CHUNK
             flat = pl.ds(ch * HALF, HALF)
             e = tiles(es[flat, :])
@@ -299,41 +302,55 @@
             es[flat, :] = untiles([x[c] * e[c] for c in range(GROUPS)])
             rs[flat, :] = untiles([x[c] * r[c] for c in range(GROUPS)])
 
-        put(blk, slot).start()
-
-        for ch, nb in enumerate((nb0, nb1)):
+
+        def negative_rows(ch, nb):
             part = lax.dot_general(
                 dn[:, ch * CHUNK : (ch + 1) * CHUNK], lb[...], (((0,), (0,)), ((), ())),
                 preferred_element_type=f32,
             )
-            nb[...] = untiles(
-                [part[:, c * LANES : (c + 1) * LANES] for c in range(GROUPS)]
-            )
-
-        def scatter(h, start, base, n):
-            db, nb, ev = ((db0, nb0), (db1, nb1))[h] + (es.at[pl.ds(h * HALF, HALF)],)
+            nb[...] = untiles([part[:, c * LANES : (c + 1) * LANES] for c in range(GROUPS)])
+
+        def add_edges(h, start, base, n):
+            db, ev = (db0, db1)[h], es.at[pl.ds(h * HALF, HALF)]
             j0 = first + h * CHUNK + start
-            for t in range(0, n, 3):
-                ks = list(range(t, min(t + 3, n)))
-                at = [slot_of(base, k) for k in ks]
-                copies = (a0, a1, a2)
-                dst = [(copies[i], row_of(dst_i[j0 + k]), db, at[i]) for i, k in enumerate(ks)]
-                neg = [(copies[i], row_of(neg_i[j0 + k]), nb, at[i]) for i, k in enumerate(ks)]
-                rel = [
-                    ((r0_acc, r1_acc)[i % 2], row_of(rid_i[j0 + k]), ev, at[i])
-                    for i, k in enumerate(ks)
-                ]
-                add_rows(dst + rel[:2])
-                add_rows(neg + rel[2:])
-
-        for h in (0, 1):
-
-            @pl.loop(0, CHUNK // 24)
+            for t in range(0, n, 2):
+                ops = []
+                for i in range(2):
+                    k, at = t + i, slot_of(base, t + i)
+                    ops.append(((a0, a1)[i], row_of(dst_i[j0 + k]), db, at))
+                    ops.append(((r0_acc, r1_acc)[i], row_of(rid_i[j0 + k]), ev, at))
+                add_rows(ops)
+
+        def add_negatives(h, start, base, n):
+            nb = (nb0, nb1)[h]
+            j0 = first + h * CHUNK + start
+            for t in range(0, n, NCOPY):
+                add_rows(
+                    [
+                        ((a0, a1, a2)[i], row_of(neg_i[j0 + t + i]), nb, slot_of(base, t + i))
+                        for i in range(min(NCOPY, n - t))
+                    ]
+                )
+
+        def looped(step, h, start, stop):
+            @pl.loop(0, (stop - start) // 16)
             def _(q):
-                scatter(h, q * 24, pl.multiple_of(q * 24 * GROUPS, 32), 24)
-
-            done = CHUNK // 24 * 24
-            scatter(h, done, done * GROUPS, CHUNK - done)
+                at = pl.multiple_of(start + q * 16, 16)
+                step(h, at, pl.multiple_of(at * GROUPS, 64), 16)
+
+        dense(0, db0)
+        add_edges(0, 0, 0, CHUNK)
+        dense(1, db1)
+        put(blk, slot).start()
+        add_edges(1, 0, 0, INE)
+        negative_rows(0, nb0)
+        add_negatives(0, 0, 0, INN)
+        negative_rows(1, nb1)
+        if INE < CHUNK:
+            looped(add_edges, 1, INE, CHUNK)
+        if INN < CHUNK:
+            looped(add_negatives, 0, INN, CHUNK)
+        looped(add_negatives, 1, 0, CHUNK)
         return 0
 
     lax.fori_loop(0, nblocks, step, 0)

time: 298 us -> 288 us (0.966)
  starting transfers between devices: 76.4 us -> 56.5 us
  Pallas kernels: 140 us -> 145 us
  waiting for transfers between devices: 41.5 us -> 45.1 us
    all_to_all x3, starting transfers between devices: 35.5 us -> 15.6 us  [by_side(): return lax.all_to_all(x.reshape(sides, -1, LANES), 'side', 0, 0, tiled=True)]
    ppermute x18, starting transfers between devices: 30.3 us -> 36.9 us  [shifted(): return lax.ppermute(x, axis, [(i, (i + by) % count) for i in range(count)])]
    ppermute x4, starting transfers between devices: 10.7 us -> 4.02 us  [swapped(): return lax.ppermute(x, axis, [(i, i ^ bit) for i in range(count)])]
    all_to_all x3, waiting for transfers between devices: 0.89 us -> 4.23 us  [by_side(): return lax.all_to_all(x.reshape(sides, -1, LANES), 'side', 0, 0, tiled=True)]
  transfers between devices with their start and end apart: 25 -> 25, of which waited for: 13 -> 12; matrix products, arithmetic and copies ran while one was open for 8% -> 9% of each run, Pallas kernels for 18% -> 20%
where the time goes in v5:
time: 288 us; the launch traced here: 284 us
  Pallas kernels  145 us (50%)
  starting transfers between devices  56.5 us (20%)
  waiting for transfers between devices  45.1 us (16%)
  local copies, waits for them, and re-layouts  23.6 us (8%)
  other arithmetic  12.1 us (4%)
    pallas_call x1, Pallas kernels, edge_blocks(): pl.pallas_call(functools.partial(block_kernel, nneg), out_shape=(half, ha...  81.7 us
    ppermute x18, starting transfers between devices, shifted(): return lax.ppermute(x, axis, [(i, (i + by) % count) for i in range(count)])  36.9 us
    ppermute x18, waiting for transfers between devices, shifted(): return lax.ppermute(x, axis, [(i, (i + by) % count) for i in range(count)])  26.3 us
    pallas_call x1, Pallas kernels, edge_rows(): pl.pallas_call(edge_rows_kernel, out_shape=(shape, shape), in_specs=[smem...  22.7 us
    pallas_call x1, Pallas kernels, source_rows(): pl.pallas_call(source_kernel, out_shape=(half, half), in_specs=[smem()] *...  19.9 us
    unnamed x44, local copies, waits for them, and re-layouts  15.7 us
    all_to_all x3, starting transfers between devices, by_side(): return lax.all_to_all(x.reshape(sides, -1, LANES), 'side', 0, 0, tiled=True)  15.6 us
    ppermute x4, waiting for transfers between devices, swapped(): return lax.ppermute(x, axis, [(i, i ^ bit) for i in range(count)])  14.6 us
  transfers between devices with their start and end apart: 25, of which 12 were waited for; matrix products, arithmetic and copies ran while one was open for 9% of the time, Pallas kernels for 20%

profile of v5, /device:TPU:96, one launch (start us, length us, event | category | flops | bytes accessed | tf_op | source)
XLA Modules:
  0.0 284.0 jit_solution(12042910112502276880)
XLA Ops:
  0.7 6.1 %copy.14.emb_hbm = bf16[4096,400]{1,0:T(8,128)(2,1)} copy(bf16[4096,400]{0,1:T(8,128)(2,1)} %param.8) | data formatting | bytes 6553600 | tf_op args[0]
  7.5 0.6 broadcast_multiply_fusion.2
  8.2 2.2 copy.15.rel_ref
  10.4 0.6 copy.19
  11.0 0.6 broadcast_multiply_fusion.1
  11.6 22.7 %edge_rows.1 = (f32[8,4096,128]{2,1,0:T(8,128)}, f32[8,4096,128]{2,1,0:T(8,128)}) custom-call(s32[1]{0:T(128)} %bitcast.36.count, s32[8192]{0:T(1024)} %bitcast.47, s32[8192]{0:T(1024)} %bitcast.49, bf16[4096,400]{1,0:T(8,128)(2,1)} %copy.14.emb_hbm, f32[1345,400]{1,0:T(8,128)} %copy.15.rel_ref), custom_call_target="tpu_custom_call" | custom-call | bytes 60000000 | tf_op jit(solution)/shard_map/edge_rows/pallas_call | solution.py:451
  34.3 0.6 broadcast_multiply_fusion
  34.9 2.3 collective-permute-done
  37.2 6.0 %copy.16.dst_hbm = bf16[4096,400]{1,0:T(8,128)(2,1)} copy(bf16[4096,400]{0,1:T(8,128)(2,1)} %collective-permute-done) | data formatting | bytes 6553600 | tf_op jit(solution)/shard_map/ppermute | solution.py:30
  43.2 81.7 %edge_blocks.1 = (bf16[8,800,128]{2,1,0:T(8,128)(2,1)}, bf16[8,800,128]{2,1,0:T(8,128)(2,1)}, bf16[8,640,128]{2,1,0:T(8,128)(2,1)}, f32[8,4096,128]{2,1,0:T(8,128)}) custom-call(s32[1]{0:T(128)} %bitcast.37.count, s32[8192]{0:T(1024)} %bitcast.50, s32[8192]{0:T(1024)} %bitcast.56, s32[8192]{0:T(1024)} %bitcast.55, bf16[4096,400]{1,0:T(8,128)(2,1)} %copy.16.dst_hbm, ...), custom_call_target="tpu_custom_call" | custom-call | tf_op jit(solution)/shard_map/edge_blocks/pallas_call | solution.py:481
  125.0 6.6 %all-to-all-start.2 = ((bf16[4,1280,128]{2,1,0:T(8,128)(2,1)}), bf16[4,1280,128]{2,1,0:T(8,128)(2,1)S(1)}, u32[]{:S(2)}, u32[]{:S(2)}) async-start(bf16[4,1280,128]{2,1,0:T(8,128)(2,1)} %bitcast.42), calls=%async_computation.2 | async-start | bytes 2621440 | tf_op jit(solution)/shard_map/all_to_all | solution.py:635
  131.6 10.3 %collective-permute-start.7 = (bf16[8,800,128]{2,1,0:T(8,128)(2,1)}, bf16[8,800,128]{2,1,0:T(8,128)(2,1)}, u32[]{:S(2)}, u32[]{:S(2)}) collective-permute-start(bf16[8,800,128]{2,1,0:T(8,128)(2,1)} %get-tuple-element.28), channel_id=1, source_target_pairs={{0,8},{8,16},{16,24},{24,32},{32,40},{40,48},{48,56},{56,64},{64,7... | collective-permute-start | bytes 4915208 | tf_op jit(solution)/shard_map/ppermute | solution.py:30
  141.9 19.9 %source_rows.1 = (bf16[8,800,128]{2,1,0:T(8,128)(2,1)}, bf16[8,800,128]{2,1,0:T(8,128)(2,1)}) custom-call(s32[1]{0:T(128)} %bitcast.38.count, s32[8192]{0:T(1024)} %bitcast.48, f32[8,4096,128]{2,1,0:T(8,128)} %get-tuple-element.22.v_hbm), custom_call_target="tpu_custom_call" | custom-call | bytes 60000000 | tf_op jit(solution)/shard_map/source_rows/pallas_call | solution.py:519
  161.8 3.0 %add.84 = bf16[8,800,128]{2,1,0:T(8,128)(2,1)} add(bf16[8,800,128]{2,1,0:T(8,128)(2,1)} %get-tuple-element.23.after_ref, bf16[8,800,128]{2,1,0:T(8,128)(2,1)S(1)} %collective-permute-done.1) | non-fusion elementwise | flops 819200 | bytes 4915200 | tf_op jit(solution)/shard_map/add | solution.py:692
  164.8 1.1 copy-done.1
  165.9 4.5 %all-to-all-start = ((bf16[4,1600,128]{2,1,0:T(8,128)(2,1)}), bf16[4,1600,128]{2,1,0:T(8,128)(2,1)S(1)}, u32[]{:S(2)}, u32[]{:S(2)}) async-start(bf16[4,1600,128]{2,1,0:T(8,128)(2,1)} %bitcast.40), calls=%async_computation | async-start | bytes 3276800 | tf_op jit(solution)/shard_map/all_to_all | solution.py:635
  170.5 2.2 sum_sides.5
  172.7 1.2 collective-permute-start.13
  173.9 7.1 %collective-permute-done.13 = bf16[640,128]{1,0:T(8,128)(2,1)S(1)} collective-permute-done((bf16[640,128]{1,0:T(8,128)(2,1)}, bf16[640,128]{1,0:T(8,128)(2,1)S(1)}, u32[]{:S(2)}, u32[]{:S(2)}) %collective-permute-start.13) | collective-permute-done | bytes 163872 | tf_op jit(solution)/shard_map/ppermute | solution.py:30
  181.0 1.0 convert_add_fusion
  182.0 0.3 collective-permute-start.14
  182.4 1.4 collective-permute-done.14
  183.9 3.0 %add.87 = bf16[8,800,128]{2,1,0:T(8,128)(2,1)} add(bf16[8,800,128]{2,1,0:T(8,128)(2,1)S(1)} %copy-done.5, bf16[8,800,128]{2,1,0:T(8,128)(2,1)} %collective-permute-done.7) | non-fusion elementwise | flops 819200 | bytes 4915200 | tf_op jit(solution)/shard_map/add | solution.py:692
  186.9 4.2 %all-to-all-done.x_ref = bf16[4,1600,128]{2,1,0:T(8,128)(2,1)S(1)} async-done(((bf16[4,1600,128]{2,1,0:T(8,128)(2,1)}), bf16[4,1600,128]{2,1,0:T(8,128)(2,1)S(1)}, u32[]{:S(2)}, u32[]{:S(2)}) %all-to-all-start) | async-done | bytes 1638432 | tf_op jit(solution)/shard_map/all_to_all | solution.py:635
  191.1 1.2 copy-done
  192.3 4.5 %all-to-all-start.1 = ((bf16[4,1600,128]{2,1,0:T(8,128)(2,1)}), bf16[4,1600,128]{2,1,0:T(8,128)(2,1)}, u32[]{:S(2)}, u32[]{:S(2)}) async-start(bf16[4,1600,128]{2,1,0:T(8,128)(2,1)} %bitcast.39), calls=%async_computation.1 | async-start | bytes 3276800 | tf_op jit(solution)/shard_map/all_to_all | solution.py:635
  197.0 9.0 %collective-permute-done.16 = f32[640,128]{1,0:T(8,128)S(1)} collective-permute-done((f32[640,128]{1,0:T(8,128)S(1)}, f32[640,128]{1,0:T(8,128)S(1)}, u32[]{:S(2)}, u32[]{:S(2)}) %collective-permute-start.16) | collective-permute-done | bytes 327712 | tf_op jit(solution)/shard_map/ppermute | solution.py:648
  206.0 3.5 %collective-permute-start.17 = (f32[640,128]{1,0:T(8,128)S(1)}, f32[640,128]{1,0:T(8,128)S(1)}, u32[]{:S(2)}, u32[]{:S(2)}) collective-permute-start(f32[640,128]{1,0:T(8,128)S(1)} %add.95), channel_id=1, source_target_pairs={{0,64},{8,72},{16,80},{24,88},{32,96},{40,104},{48,112},{56,120},{... | collective-permute-start | bytes 983048 | tf_op jit(solution)/shard_map/ppermute | solution.py:648
  209.6 1.8 dynamic-slice_bitcast_fusion
  211.4 4.2 %collective-permute-done.17 = f32[640,128]{1,0:T(8,128)S(1)} collective-permute-done((f32[640,128]{1,0:T(8,128)S(1)}, f32[640,128]{1,0:T(8,128)S(1)}, u32[]{:S(2)}, u32[]{:S(2)}) %collective-permute-start.17) | collective-permute-done | bytes 327712 | tf_op jit(solution)/shard_map/ppermute | solution.py:648
  215.7 3.0 %collective-permute-start.18 = (bf16[640,128]{1,0:T(8,128)(2,1)S(1)}, bf16[640,128]{1,0:T(8,128)(2,1)S(1)}, u32[]{:S(2)}, u32[]{:S(2)}) collective-permute-start(bf16[640,128]{1,0:T(8,128)(2,1)S(1)} %get-tuple-element.38), channel_id=1, source_target_pairs={{0,1},{1,0},{2,3},{3,2},{4,5},{5,4},{6,7},{7,6},{8,9},{9,8},{10,11... | collective-permute-start | bytes 491528 | tf_op jit(solution)/shard_map/ppermute | solution.py:30
  218.6 2.4 sum_sides.3
  221.0 0.7 collective-permute-start.2
  221.7 2.4 sum_sides.4
  224.1 2.9 %collective-permute-start.8 = (bf16[800,128]{1,0:T(8,128)(2,1)}, bf16[800,128]{1,0:T(8,128)(2,1)S(1)}, u32[]{:S(2)}, u32[]{:S(2)}) collective-permute-start(bf16[800,128]{1,0:T(8,128)(2,1)} %get-tuple-element.30), channel_id=1, source_target_pairs={{0,1},{1,0},{2,3},{3,2},{4,5},{5,4},{6,7},{7,6},{8,9},{9,8},{10,11... | collective-permute-start | bytes 614408 | tf_op jit(solution)/shard_map/ppermute | solution.py:30
  226.9 3.7 %collective-permute-done.2.b_ref = bf16[800,128]{1,0:T(8,128)(2,1)S(1)} collective-permute-done((bf16[800,128]{1,0:T(8,128)(2,1)}, bf16[800,128]{1,0:T(8,128)(2,1)S(1)}, u32[]{:S(2)}, u32[]{:S(2)}) %collective-permute-start.2) | collective-permute-done | bytes 204832 | tf_op jit(solution)/shard_map/ppermute | solution.py:30
  230.7 0.7 copy-done.13
  231.3 2.1 update.2
  233.4 2.6 collective-permute-start.3
  236.0 0.9 collective-permute-start.4
  236.9 2.7 collective-permute-start.5
  239.6 1.0 sort.17
  240.6 0.3 collective-permute-start.19
  240.9 3.0 %collective-permute-start.20 = (bf16[2,640,128]{2,1,0:T(8,128)(2,1)S(1)}, bf16[2,640,128]{2,1,0:T(8,128)(2,1)}, u32[]{:S(2)}, u32[]{:S(2)}) collective-permute-start(bf16[2,640,128]{2,1,0:T(8,128)(2,1)S(1)} %pad_maximum_fusion.2), channel_id=1, source_target_pairs={{0,6},{2,0},{4,2},{6,4},{1,7},{3,1},{5,3},{7,5},{8,14},{10,8},{12,... | collective-permute-start | bytes 983048 | tf_op jit(solution)/shard_map/ppermute | solution.py:30
  243.9 2.1 update.3
  246.1 0.1 collective-permute-start.9
  246.2 2.7 collective-permute-done.5
  248.9 0.7 copy-done.11
  249.6 1.2 pad_maximum_fusion.a_ref
  250.9 0.9 collective-permute-start.6
  251.8 0.5 fusion.1.order
  252.3 3.1 %collective-permute-start.21 = (bf16[2,640,128]{2,1,0:T(8,128)(2,1)S(1)}, bf16[2,640,128]{2,1,0:T(8,128)(2,1)S(1)}, u32[]{:S(2)}, u32[]{:S(2)}) collective-permute-start(bf16[2,640,128]{2,1,0:T(8,128)(2,1)S(1)} %pad_maximum_fusion.2), channel_id=1, source_target_pairs={{0,4},{2,6},{4,0},{6,2},{1,5},{3,7},{5,1},{7,3},{8,12},{10,14},{12... | collective-permute-start | bytes 983048 | tf_op jit(solution)/shard_map/ppermute | solution.py:30
  255.4 0.5 collective-permute-done.9
  255.9 0.3 collective-permute-start.10
  256.2 3.0 %collective-permute-start.11 = (bf16[2,800,128]{2,1,0:T(8,128)(2,1)S(1)}, bf16[2,800,128]{2,1,0:T(8,128)(2,1)}, u32[]{:S(2)}, u32[]{:S(2)}) collective-permute-start(bf16[2,800,128]{2,1,0:T(8,128)(2,1)S(1)} %pad_maximum_fusion.1.b0_ref), channel_id=1, source_target_pairs={{0,6},{2,0},{4,2},{6,4},{1,7},{3,1},{5,3},{7,5},{8,14},{10,8},{12,... | collective-permute-start | bytes 1228808 | tf_op jit(solution)/shard_map/ppermute | solution.py:30
  259.2 1.9 collective-permute-start.12
  261.2 1.0 constant_dynamic-update-slice_fusion.2
  262.2 1.0 constant_dynamic-update-slice_fusion.1
  263.2 1.2 collective-permute-done.21
  264.5 1.0 copy-done.4
  265.5 3.5 %relation_out.1 = f32[400,1345]{1,0:T(8,128)} custom-call(s32[8]{0:T(128)} %fusion.1.order, bf16[8,640,128]{2,1,0:T(8,128)(2,1)} %copy-done.4), custom_call_target="tpu_custom_call" | custom-call | tf_op jit(solution)/shard_map/relation_out/pallas_call | solution.py:624
  269.1 3.7 %collective-permute-done.10.b1_ref = bf16[2,800,128]{2,1,0:T(8,128)(2,1)} collective-permute-done((bf16[2,800,128]{2,1,0:T(8,128)(2,1)S(1)}, bf16[2,800,128]{2,1,0:T(8,128)(2,1)}, u32[]{:S(2)}, u32[]{:S(2)}) %collective-permute-start.10) | collective-permute-done | bytes 409632 | tf_op jit(solution)/shard_map/ppermute | solution.py:30
  272.8 5.0 %collective-permute-done.12.b3_ref = bf16[2,800,128]{2,1,0:T(8,128)(2,1)} collective-permute-done((bf16[2,800,128]{2,1,0:T(8,128)(2,1)S(1)}, bf16[2,800,128]{2,1,0:T(8,128)(2,1)}, u32[]{:S(2)}, u32[]{:S(2)}) %collective-permute-start.12) | collective-permute-done | bytes 409632 | tf_op jit(solution)/shard_map/ppermute | solution.py:30
  277.8 6.2 %finish.1 = (bf16[400,4096]{1,0:T(8,128)(2,1)}, bf16[400,4096]{1,0:T(8,128)(2,1)}) custom-call(s32[8]{0:T(128)} %copy-done.18, bf16[4,800,128]{2,1,0:T(8,128)(2,1)} %copy-done.2, bf16[4,800,128]{2,1,0:T(8,128)(2,1)} %collective-permute-done.6.ar_ref, bf16[2,800,128]{2,1,0:T(8,128)(2,1)} %copy-done.6, bf16[2,800,128]{2,1,0:T(8,128)(2,1)} %collective-permute-done.10.b1_ref, ...), custom_call_target="tpu_custom_call" | custom-call | tf_op jit(solution)/shard_map/finish/pallas_call | solution.py:607
  (63 shorter events, 0.9 us)
Async XLA Ops:
  0.6 6.9 %copy-start.14 = (s32[1,1,1,8192]{3,2,1,0:T(1,128)S(1)}, s32[1,1,1,8192]{3,2,1,0:T(1,128)}, u32[]{:S(2)}) copy-start(s32[1,1,1,8192]{3,2,1,0:T(1,128)} %param.10) | copy-start | bytes 98308
  0.6 7.5 %copy-start.3 = (f32[1345,400]{0,1:T(8,128)S(1)}, f32[1345,400]{0,1:T(8,128)}, u32[]{:S(2)}) copy-start(f32[1345,400]{0,1:T(8,128)} %param.9) | copy-start | bytes 6456004
  0.7 36.6 %collective-permute-start = (bf16[4096,400]{0,1:T(8,128)(2,1)}, bf16[4096,400]{0,1:T(8,128)(2,1)}, u32[]{:S(2)}, u32[]{:S(2)}) collective-permute-start(bf16[4096,400]{0,1:T(8,128)(2,1)} %param.8), channel_id=1, source_target_pairs={{0,120},{8,0},{16,8},{24,16},{32,24},{40,32},{48,40},{56,48},{64,5... | collective-permute-start | bytes 9830408 | tf_op jit(solution)/shard_map/ppermute | solution.py:30
  8.2 2.2 copy-start.15
  8.2 2.8 copy-start.16
  11.6 22.7 %copy-start.17 = (s32[1,1,1,8192]{3,2,1,0:T(1,128)S(1)}, s32[1,1,1,8192]{3,2,1,0:T(1,128)}, u32[]{:S(2)}) copy-start(s32[1,1,1,8192]{3,2,1,0:T(1,128)} %param.12) | copy-start | bytes 98308
  124.9 36.9 %collective-permute-start.1 = (bf16[8,800,128]{2,1,0:T(8,128)(2,1)}, bf16[8,800,128]{2,1,0:T(8,128)(2,1)S(1)}, u32[]{:S(2)}, u32[]{:S(2)}) collective-permute-start(bf16[8,800,128]{2,1,0:T(8,128)(2,1)} %get-tuple-element.24), channel_id=1, source_target_pairs={{0,8},{8,16},{16,24},{24,32},{32,40},{40,48},{48,56},{56,64},{64,7... | collective-permute-start | bytes 4915208 | tf_op jit(solution)/shard_map/ppermute | solution.py:30
  125.0 39.8 %all-to-all-start.2 = ((bf16[4,1280,128]{2,1,0:T(8,128)(2,1)}), bf16[4,1280,128]{2,1,0:T(8,128)(2,1)S(1)}, u32[]{:S(2)}, u32[]{:S(2)}) async-start(bf16[4,1280,128]{2,1,0:T(8,128)(2,1)} %bitcast.42), calls=%async_computation.2 | async-start | bytes 2621440 | tf_op jit(solution)/shard_map/all_to_all | solution.py:635
  131.6 52.3 %collective-permute-start.7 = (bf16[8,800,128]{2,1,0:T(8,128)(2,1)}, bf16[8,800,128]{2,1,0:T(8,128)(2,1)}, u32[]{:S(2)}, u32[]{:S(2)}) collective-permute-start(bf16[8,800,128]{2,1,0:T(8,128)(2,1)} %get-tuple-element.28), channel_id=1, source_target_pairs={{0,8},{8,16},{16,24},{24,32},{32,40},{40,48},{48,56},{56,64},{64,7... | collective-permute-start | bytes 4915208 | tf_op jit(solution)/shard_map/ppermute | solution.py:30
  164.8 1.1 copy-start.1
  165.9 25.2 %all-to-all-start = ((bf16[4,1600,128]{2,1,0:T(8,128)(2,1)}), bf16[4,1600,128]{2,1,0:T(8,128)(2,1)S(1)}, u32[]{:S(2)}, u32[]{:S(2)}) async-start(bf16[4,1600,128]{2,1,0:T(8,128)(2,1)} %bitcast.40), calls=%async_computation | async-start | bytes 3276800 | tf_op jit(solution)/shard_map/all_to_all | solution.py:635
  172.7 11.2 %copy-start.5 = (bf16[8,800,128]{2,1,0:T(8,128)(2,1)S(1)}, bf16[8,800,128]{2,1,0:T(8,128)(2,1)}, u32[]{:S(2)}) copy-start(bf16[8,800,128]{2,1,0:T(8,128)(2,1)} %get-tuple-element.27) | copy-start | bytes 4915204
  172.7 8.4 %collective-permute-start.13 = (bf16[640,128]{1,0:T(8,128)(2,1)}, bf16[640,128]{1,0:T(8,128)(2,1)S(1)}, u32[]{:S(2)}, u32[]{:S(2)}) collective-permute-start(bf16[640,128]{1,0:T(8,128)(2,1)} %get-tuple-element.35), channel_id=1, source_target_pairs={{0,1},{1,0},{2,3},{3,2},{4,5},{5,4},{6,7},{7,6},{8,9},{9,8},{10,11... | collective-permute-start | bytes 491528 | tf_op jit(solution)/shard_map/ppermute | solution.py:30
  182.0 1.7 collective-permute-start.14
  183.8 13.1 %collective-permute-start.15 = (f32[640,128]{1,0:T(8,128)S(1)}, f32[640,128]{1,0:T(8,128)S(1)}, u32[]{:S(2)}, u32[]{:S(2)}) collective-permute-start(f32[640,128]{1,0:T(8,128)S(1)} %add.93), channel_id=1, source_target_pairs={{0,16},{8,24},{16,0},{24,8},{32,48},{40,56},{48,32},{56,40},{64,80... | collective-permute-start | bytes 983048 | tf_op jit(solution)/shard_map/ppermute | solution.py:648
  191.1 1.2 copy-start
  192.3 29.4 %all-to-all-start.1 = ((bf16[4,1600,128]{2,1,0:T(8,128)(2,1)}), bf16[4,1600,128]{2,1,0:T(8,128)(2,1)}, u32[]{:S(2)}, u32[]{:S(2)}) async-start(bf16[4,1600,128]{2,1,0:T(8,128)(2,1)} %bitcast.39), calls=%async_computation.1 | async-start | bytes 3276800 | tf_op jit(solution)/shard_map/all_to_all | solution.py:635
  196.9 9.1 %collective-permute-start.16 = (f32[640,128]{1,0:T(8,128)S(1)}, f32[640,128]{1,0:T(8,128)S(1)}, u32[]{:S(2)}, u32[]{:S(2)}) collective-permute-start(f32[640,128]{1,0:T(8,128)S(1)} %add.94), channel_id=1, source_target_pairs={{0,32},{8,40},{16,48},{24,56},{32,0},{40,8},{48,16},{56,24},{64,96... | collective-permute-start | bytes 983048 | tf_op jit(solution)/shard_map/ppermute | solution.py:648
  206.0 9.6 %collective-permute-start.17 = (f32[640,128]{1,0:T(8,128)S(1)}, f32[640,128]{1,0:T(8,128)S(1)}, u32[]{:S(2)}, u32[]{:S(2)}) collective-permute-start(f32[640,128]{1,0:T(8,128)S(1)} %add.95), channel_id=1, source_target_pairs={{0,64},{8,72},{16,80},{24,88},{32,96},{40,104},{48,112},{56,120},{... | collective-permute-start | bytes 983048 | tf_op jit(solution)/shard_map/ppermute | solution.py:648
  215.7 24.9 %collective-permute-start.18 = (bf16[640,128]{1,0:T(8,128)(2,1)S(1)}, bf16[640,128]{1,0:T(8,128)(2,1)S(1)}, u32[]{:S(2)}, u32[]{:S(2)}) collective-permute-start(bf16[640,128]{1,0:T(8,128)(2,1)S(1)} %get-tuple-element.38), channel_id=1, source_target_pairs={{0,1},{1,0},{2,3},{3,2},{4,5},{5,4},{6,7},{7,6},{8,9},{9,8},{10,11... | collective-permute-start | bytes 491528 | tf_op jit(solution)/shard_map/ppermute | solution.py:30
  221.0 9.6 %collective-permute-start.2 = (bf16[800,128]{1,0:T(8,128)(2,1)}, bf16[800,128]{1,0:T(8,128)(2,1)S(1)}, u32[]{:S(2)}, u32[]{:S(2)}) collective-permute-start(bf16[800,128]{1,0:T(8,128)(2,1)} %get-tuple-element.26), channel_id=1, source_target_pairs={{0,1},{1,0},{2,3},{3,2},{4,5},{5,4},{6,7},{7,6},{8,9},{9,8},{10,11... | collective-permute-start | bytes 614408 | tf_op jit(solution)/shard_map/ppermute | solution.py:30
  224.1 16.8 %collective-permute-start.8 = (bf16[800,128]{1,0:T(8,128)(2,1)}, bf16[800,128]{1,0:T(8,128)(2,1)S(1)}, u32[]{:S(2)}, u32[]{:S(2)}) collective-permute-start(bf16[800,128]{1,0:T(8,128)(2,1)} %get-tuple-element.30), channel_id=1, source_target_pairs={{0,1},{1,0},{2,3},{3,2},{4,5},{5,4},{6,7},{7,6},{8,9},{9,8},{10,11... | collective-permute-start | bytes 614408 | tf_op jit(solution)/shard_map/ppermute | solution.py:30
  230.7 0.7 copy-start.13
  233.4 16.2 %copy-start.7 = (bf16[800,128]{1,0:T(8,128)(2,1)S(1)}, bf16[800,128]{1,0:T(8,128)(2,1)}, u32[]{:S(2)}) copy-start(bf16[800,128]{1,0:T(8,128)(2,1)} %update.2) | copy-start | bytes 614404
  233.4 12.6 %collective-permute-start.3 = (bf16[800,128]{1,0:T(8,128)(2,1)}, bf16[800,128]{1,0:T(8,128)(2,1)S(1)}, u32[]{:S(2)}, u32[]{:S(2)}) collective-permute-start(bf16[800,128]{1,0:T(8,128)(2,1)} %update.2), channel_id=1, source_target_pairs={{0,2},{2,4},{4,6},{6,0},{1,3},{3,5},{5,7},{7,1},{8,10},{10,12},{12... | collective-permute-start | bytes 614408 | tf_op jit(solution)/shard_map/ppermute | solution.py:30
  236.0 10.2 %collective-permute-start.4 = (bf16[800,128]{1,0:T(8,128)(2,1)}, bf16[800,128]{1,0:T(8,128)(2,1)S(1)}, u32[]{:S(2)}, u32[]{:S(2)}) collective-permute-start(bf16[800,128]{1,0:T(8,128)(2,1)} %update.2), channel_id=1, source_target_pairs={{0,6},{2,0},{4,2},{6,4},{1,7},{3,1},{5,3},{7,5},{8,14},{10,8},{12,... | collective-permute-start | bytes 614408 | tf_op jit(solution)/shard_map/ppermute | solution.py:30
  236.9 12.0 %collective-permute-start.5 = (bf16[800,128]{1,0:T(8,128)(2,1)}, bf16[800,128]{1,0:T(8,128)(2,1)S(1)}, u32[]{:S(2)}, u32[]{:S(2)}) collective-permute-start(bf16[800,128]{1,0:T(8,128)(2,1)} %update.2), channel_id=1, source_target_pairs={{0,4},{2,6},{4,0},{6,2},{1,5},{3,7},{5,1},{7,3},{8,12},{10,14},{12... | collective-permute-start | bytes 614408 | tf_op jit(solution)/shard_map/ppermute | solution.py:30
  239.6 11.2 %copy-start.18 = (s32[8]{0:T(128)}, s32[8]{0:T(128)S(1)}, u32[]{:S(2)}) copy-start(s32[8]{0:T(128)S(1)} %pad_add_fusion.place) | copy-start | bytes 100
  240.6 15.6 %collective-permute-start.19 = (bf16[2,640,128]{2,1,0:T(8,128)(2,1)S(1)}, bf16[2,640,128]{2,1,0:T(8,128)(2,1)}, u32[]{:S(2)}, u32[]{:S(2)}) collective-permute-start(bf16[2,640,128]{2,1,0:T(8,128)(2,1)S(1)} %pad_maximum_fusion.2), channel_id=1, source_target_pairs={{0,2},{2,4},{4,6},{6,0},{1,3},{3,5},{5,7},{7,1},{8,10},{10,12},{12... | collective-permute-start | bytes 983048 | tf_op jit(solution)/shard_map/ppermute | solution.py:30
  240.9 3.0 %copy-start.12 = (bf16[800,128]{1,0:T(8,128)(2,1)}, bf16[800,128]{1,0:T(8,128)(2,1)S(1)}, u32[]{:S(2)}) copy-start(bf16[800,128]{1,0:T(8,128)(2,1)S(1)} %collective-permute-done.8.b_ref) | copy-start | bytes 614404
  240.9 18.3 %collective-permute-start.20 = (bf16[2,640,128]{2,1,0:T(8,128)(2,1)S(1)}, bf16[2,640,128]{2,1,0:T(8,128)(2,1)}, u32[]{:S(2)}, u32[]{:S(2)}) collective-permute-start(bf16[2,640,128]{2,1,0:T(8,128)(2,1)S(1)} %pad_maximum_fusion.2), channel_id=1, source_target_pairs={{0,6},{2,0},{4,2},{6,4},{1,7},{3,1},{5,3},{7,5},{8,14},{10,8},{12,... | collective-permute-start | bytes 983048 | tf_op jit(solution)/shard_map/ppermute | solution.py:30
  246.1 9.8 %copy-start.8 = (bf16[800,128]{1,0:T(8,128)(2,1)S(1)}, bf16[800,128]{1,0:T(8,128)(2,1)}, u32[]{:S(2)}) copy-start(bf16[800,128]{1,0:T(8,128)(2,1)} %update.3) | copy-start | bytes 614404
  246.1 2.9 %copy-start.9 = (bf16[800,128]{1,0:T(8,128)(2,1)}, bf16[800,128]{1,0:T(8,128)(2,1)S(1)}, u32[]{:S(2)}) copy-start(bf16[800,128]{1,0:T(8,128)(2,1)S(1)} %collective-permute-done.3) | copy-start | bytes 614404
  246.1 9.8 %collective-permute-start.9 = (bf16[800,128]{1,0:T(8,128)(2,1)}, bf16[800,128]{1,0:T(8,128)(2,1)S(1)}, u32[]{:S(2)}, u32[]{:S(2)}) collective-permute-start(bf16[800,128]{1,0:T(8,128)(2,1)} %update.3), channel_id=1, source_target_pairs={{0,1},{1,0},{2,3},{3,2},{4,5},{5,4},{6,7},{7,6},{8,9},{9,8},{10,11... | collective-permute-start | bytes 614408 | tf_op jit(solution)/shard_map/ppermute | solution.py:30
  246.2 2.7 copy-start.10
  248.9 0.7 copy-start.11
  250.8 18.2 %copy-start.2 = (bf16[4,800,128]{2,1,0:T(8,128)(2,1)}, bf16[4,800,128]{2,1,0:T(8,128)(2,1)S(1)}, u32[]{:S(2)}) copy-start(bf16[4,800,128]{2,1,0:T(8,128)(2,1)S(1)} %pad_maximum_fusion.a_ref) | copy-start | bytes 2457604
  250.9 26.9 %collective-permute-start.6 = (bf16[4,800,128]{2,1,0:T(8,128)(2,1)S(1)}, bf16[4,800,128]{2,1,0:T(8,128)(2,1)}, u32[]{:S(2)}, u32[]{:S(2)}) collective-permute-start(bf16[4,800,128]{2,1,0:T(8,128)(2,1)S(1)} %pad_maximum_fusion.a_ref), channel_id=1, source_target_pairs={{0,1},{1,0},{2,3},{3,2},{4,5},{5,4},{6,7},{7,6},{8,9},{9,8},{10,11... | collective-permute-start | bytes 2457608 | tf_op jit(solution)/shard_map/ppermute | solution.py:30
  252.3 12.2 %collective-permute-start.21 = (bf16[2,640,128]{2,1,0:T(8,128)(2,1)S(1)}, bf16[2,640,128]{2,1,0:T(8,128)(2,1)S(1)}, u32[]{:S(2)}, u32[]{:S(2)}) collective-permute-start(bf16[2,640,128]{2,1,0:T(8,128)(2,1)S(1)} %pad_maximum_fusion.2), channel_id=1, source_target_pairs={{0,4},{2,6},{4,0},{6,2},{1,5},{3,7},{5,1},{7,3},{8,12},{10,14},{12... | collective-permute-start | bytes 983048 | tf_op jit(solution)/shard_map/ppermute | solution.py:30
  255.9 13.2 %copy-start.6 = (bf16[2,800,128]{2,1,0:T(8,128)(2,1)}, bf16[2,800,128]{2,1,0:T(8,128)(2,1)S(1)}, u32[]{:S(2)}) copy-start(bf16[2,800,128]{2,1,0:T(8,128)(2,1)S(1)} %pad_maximum_fusion.1.b0_ref) | copy-start | bytes 1228804
  255.9 16.9 %collective-permute-start.10 = (bf16[2,800,128]{2,1,0:T(8,128)(2,1)S(1)}, bf16[2,800,128]{2,1,0:T(8,128)(2,1)}, u32[]{:S(2)}, u32[]{:S(2)}) collective-permute-start(bf16[2,800,128]{2,1,0:T(8,128)(2,1)S(1)} %pad_maximum_fusion.1.b0_ref), channel_id=1, source_target_pairs={{0,2},{2,4},{4,6},{6,0},{1,3},{3,5},{5,7},{7,1},{8,10},{10,12},{12... | collective-permute-start | bytes 1228808 | tf_op jit(solution)/shard_map/ppermute | solution.py:30
  256.2 16.6 %collective-permute-start.11 = (bf16[2,800,128]{2,1,0:T(8,128)(2,1)S(1)}, bf16[2,800,128]{2,1,0:T(8,128)(2,1)}, u32[]{:S(2)}, u32[]{:S(2)}) collective-permute-start(bf16[2,800,128]{2,1,0:T(8,128)(2,1)S(1)} %pad_maximum_fusion.1.b0_ref), channel_id=1, source_target_pairs={{0,6},{2,0},{4,2},{6,4},{1,7},{3,1},{5,3},{7,5},{8,14},{10,8},{12,... | collective-permute-start | bytes 1228808 | tf_op jit(solution)/shard_map/ppermute | solution.py:30
  259.2 18.5 %collective-permute-start.12 = (bf16[2,800,128]{2,1,0:T(8,128)(2,1)S(1)}, bf16[2,800,128]{2,1,0:T(8,128)(2,1)}, u32[]{:S(2)}, u32[]{:S(2)}) collective-permute-start(bf16[2,800,128]{2,1,0:T(8,128)(2,1)S(1)} %pad_maximum_fusion.1.b0_ref), channel_id=1, source_target_pairs={{0,4},{2,6},{4,0},{6,2},{1,5},{3,7},{5,1},{7,3},{8,12},{10,14},{12... | collective-permute-start | bytes 1228808 | tf_op jit(solution)/shard_map/ppermute | solution.py:30
  264.5 1.1 copy-start.4

commit v6 on v5

--- a/solution.py
+++ b/solution.py
@@ -677,12 +677,12 @@
     rel = by_side(grel)
     gsrc = source_rows(count, src, values, rows)
     rel, sent = sum_sides(which, rel, gsrc[0])
-    rel = rel + shifted(sent, "rep", 1).astype(f32)
+    rel = (rel + shifted(sent, "rep", 1).astype(f32)).astype(bf16)
     bit = 1
     while bit < doms:
-        rel = rel + swapped(rel, "dom", bit)
+        rel = (rel.astype(f32) + swapped(rel, "dom", bit).astype(f32)).astype(bf16)
         bit *= 2
-    rel = jnp.concatenate(around(jnp.stack(both_reps(rel.astype(bf16)))))
+    rel = jnp.concatenate(around(jnp.stack(both_reps(rel))))
     relm = -(-nrel // (PIECES * 64)) * 64
     rel_order = (order % 4) * 2 + order // 4
     relation_grad = relation_out(rel_order, rel, relm, (width, nrel))

time: 288 us -> 279 us (0.969)
  Pallas kernels: 145 us -> 107 us
  starting transfers between devices: 56.5 us -> 93.6 us
  waiting for transfers between devices: 45.1 us -> 36.7 us
    pallas_call x1, Pallas kernels: 81.7 us -> 54 us  [edge_blocks(): pl.pallas_call(functools.partial(block_kernel, nneg), out_shape=(half, ha...]
    all_to_all x3, starting transfers between devices: 15.6 us -> 40.9 us  [by_side(): return lax.all_to_all(x.reshape(sides, -1, LANES), 'side', 0, 0, tiled=True)]
    ppermute x4, starting transfers between devices: 4.02 us -> 11.2 us  [swapped(): return lax.ppermute(x, axis, [(i, i ^ bit) for i in range(count)])]
    ppermute x4, waiting for transfers between devices: 14.6 us -> 8.4 us  [swapped(): return lax.ppermute(x, axis, [(i, i ^ bit) for i in range(count)])]
    pallas_call x1, Pallas kernels: 22.7 us -> 16.8 us  [edge_rows(): pl.pallas_call(edge_rows_kernel, out_shape=(shape, shape), in_specs=[smem...]
    pallas_call x1, Pallas kernels: 19.9 us -> 15.2 us  [source_rows(): pl.pallas_call(source_kernel, out_shape=(half, half), in_specs=[smem()] *...]
    ppermute x18, starting transfers between devices: 36.9 us -> 41.5 us  [shifted(): return lax.ppermute(x, axis, [(i, (i + by) % count) for i in range(count)])]
    unnamed x44 -> x40, local copies, waits for them, and re-layouts: 15.7 us -> 15.8 us
  transfers between devices with their start and end apart: 25 -> 25, of which waited for: 12 -> 11; matrix products, arithmetic and copies ran while one was open for 9% -> 9% of each run, Pallas kernels for 20% -> 17%
where the time goes in v6:
time: 279 us; the launch traced here: 275 us
  Pallas kernels  107 us (38%)
  starting transfers between devices  93.6 us (34%)
  waiting for transfers between devices  36.7 us (13%)
  local copies, waits for them, and re-layouts  23.6 us (8%)
  other arithmetic  12.5 us (4%)
    pallas_call x1, Pallas kernels, edge_blocks(): pl.pallas_call(functools.partial(block_kernel, nneg), out_shape=(half, ha...  54 us
    ppermute x18, starting transfers between devices, shifted(): return lax.ppermute(x, axis, [(i, (i + by) % count) for i in range(count)])  41.5 us
    all_to_all x3, starting transfers between devices, by_side(): return lax.all_to_all(x.reshape(sides, -1, LANES), 'side', 0, 0, tiled=True)  40.9 us
    ppermute x18, waiting for transfers between devices, shifted(): return lax.ppermute(x, axis, [(i, (i + by) % count) for i in range(count)])  25.8 us
    pallas_call x1, Pallas kernels, edge_rows(): pl.pallas_call(edge_rows_kernel, out_shape=(shape, shape), in_specs=[smem...  16.8 us
    unnamed x40, local copies, waits for them, and re-layouts  15.8 us
    pallas_call x1, Pallas kernels, source_rows(): pl.pallas_call(source_kernel, out_shape=(half, half), in_specs=[smem()] *...  15.2 us
    ppermute x4, starting transfers between devices, swapped(): return lax.ppermute(x, axis, [(i, i ^ bit) for i in range(count)])  11.2 us
  transfers between devices with their start and end apart: 25, of which 11 were waited for; matrix products, arithmetic and copies ran while one was open for 9% of the time, Pallas kernels for 17%

profile of v6, /device:TPU:96, one launch (start us, length us, event | category | flops | bytes accessed | tf_op | source)
XLA Modules:
  0.0 275.0 jit_solution(6699483188083561159)
XLA Ops:
  0.7 6.2 %copy.14.emb_hbm = bf16[4096,400]{1,0:T(8,128)(2,1)} copy(bf16[4096,400]{0,1:T(8,128)(2,1)} %param.8) | data formatting | bytes 6553600 | tf_op args[0]
  7.6 0.6 broadcast_multiply_fusion.2
  8.2 2.2 copy.15.rel_ref
  10.4 0.6 copy.19
  11.0 0.6 broadcast_multiply_fusion.1
  11.6 16.8 %edge_rows.1 = (f32[8,4096,128]{2,1,0:T(8,128)}, f32[8,4096,128]{2,1,0:T(8,128)}) custom-call(s32[1]{0:T(128)} %bitcast.36.count, s32[8192]{0:T(1024)} %bitcast.47, s32[8192]{0:T(1024)} %bitcast.49, bf16[4096,400]{1,0:T(8,128)(2,1)} %copy.14.emb_hbm, f32[1345,400]{1,0:T(8,128)} %copy.15.rel_ref), custom_call_target="tpu_custom_call" | custom-call | bytes 60000000 | tf_op jit(solution)/shard_map/edge_rows/pallas_call | solution.py:451
  28.5 0.6 broadcast_multiply_fusion
  29.1 8.1 %collective-permute-done = bf16[4096,400]{0,1:T(8,128)(2,1)} collective-permute-done((bf16[4096,400]{0,1:T(8,128)(2,1)}, bf16[4096,400]{0,1:T(8,128)(2,1)}, u32[]{:S(2)}, u32[]{:S(2)}) %collective-permute-start) | collective-permute-done | bytes 3276832 | tf_op jit(solution)/shard_map/ppermute | solution.py:30
  37.2 6.0 %copy.16.dst_hbm = bf16[4096,400]{1,0:T(8,128)(2,1)} copy(bf16[4096,400]{0,1:T(8,128)(2,1)} %collective-permute-done) | data formatting | bytes 6553600 | tf_op jit(solution)/shard_map/ppermute | solution.py:30
  43.2 54.0 %edge_blocks.1 = (bf16[8,800,128]{2,1,0:T(8,128)(2,1)}, bf16[8,800,128]{2,1,0:T(8,128)(2,1)}, bf16[8,640,128]{2,1,0:T(8,128)(2,1)}, f32[8,4096,128]{2,1,0:T(8,128)}) custom-call(s32[1]{0:T(128)} %bitcast.37.count, s32[8192]{0:T(1024)} %bitcast.50, s32[8192]{0:T(1024)} %bitcast.56, s32[8192]{0:T(1024)} %bitcast.55, bf16[4096,400]{1,0:T(8,128)(2,1)} %copy.16.dst_hbm, ...), custom_call_target="tpu_custom_call" | custom-call | tf_op jit(solution)/shard_map/edge_blocks/pallas_call | solution.py:481
  97.3 13.1 %collective-permute-start.1 = (bf16[8,800,128]{2,1,0:T(8,128)(2,1)}, bf16[8,800,128]{2,1,0:T(8,128)(2,1)S(1)}, u32[]{:S(2)}, u32[]{:S(2)}) collective-permute-start(bf16[8,800,128]{2,1,0:T(8,128)(2,1)} %get-tuple-element.24), channel_id=1, source_target_pairs={{0,8},{8,16},{16,24},{24,32},{32,40},{40,48},{48,56},{56,64},{64,7... | collective-permute-start | bytes 4915208 | tf_op jit(solution)/shard_map/ppermute | solution.py:30
  110.4 30.3 %all-to-all-start.2 = ((bf16[4,1280,128]{2,1,0:T(8,128)(2,1)}), bf16[4,1280,128]{2,1,0:T(8,128)(2,1)S(1)}, u32[]{:S(2)}, u32[]{:S(2)}) async-start(bf16[4,1280,128]{2,1,0:T(8,128)(2,1)} %bitcast.42), calls=%async_computation.2 | async-start | bytes 2621440 | tf_op jit(solution)/shard_map/all_to_all | solution.py:635
  140.7 15.2 %source_rows.1 = (bf16[8,800,128]{2,1,0:T(8,128)(2,1)}, bf16[8,800,128]{2,1,0:T(8,128)(2,1)}) custom-call(s32[1]{0:T(128)} %bitcast.38.count, s32[8192]{0:T(1024)} %bitcast.48, f32[8,4096,128]{2,1,0:T(8,128)} %get-tuple-element.22.v_hbm), custom_call_target="tpu_custom_call" | custom-call | bytes 60000000 | tf_op jit(solution)/shard_map/source_rows/pallas_call | solution.py:519
  156.0 3.0 %add.84 = bf16[8,800,128]{2,1,0:T(8,128)(2,1)} add(bf16[8,800,128]{2,1,0:T(8,128)(2,1)} %get-tuple-element.23.after_ref, bf16[8,800,128]{2,1,0:T(8,128)(2,1)S(1)} %collective-permute-done.1) | non-fusion elementwise | flops 819200 | bytes 4915200 | tf_op jit(solution)/shard_map/add | solution.py:692
  159.0 1.1 copy-done.1
  160.2 6.1 %all-to-all-start = ((bf16[4,1600,128]{2,1,0:T(8,128)(2,1)}), bf16[4,1600,128]{2,1,0:T(8,128)(2,1)S(1)}, u32[]{:S(2)}, u32[]{:S(2)}) async-start(bf16[4,1600,128]{2,1,0:T(8,128)(2,1)} %bitcast.40), calls=%async_computation | async-start | bytes 3276800 | tf_op jit(solution)/shard_map/all_to_all | solution.py:635
  166.2 2.2 sum_sides.5
  168.4 4.1 %collective-permute-start.13 = (bf16[640,128]{1,0:T(8,128)(2,1)}, bf16[640,128]{1,0:T(8,128)(2,1)S(1)}, u32[]{:S(2)}, u32[]{:S(2)}) collective-permute-start(bf16[640,128]{1,0:T(8,128)(2,1)} %get-tuple-element.35), channel_id=1, source_target_pairs={{0,1},{1,0},{2,3},{3,2},{4,5},{5,4},{6,7},{7,6},{8,9},{9,8},{10,11... | collective-permute-start | bytes 491528 | tf_op jit(solution)/shard_map/ppermute | solution.py:30
  172.5 3.6 %collective-permute-done.13 = bf16[640,128]{1,0:T(8,128)(2,1)S(1)} collective-permute-done((bf16[640,128]{1,0:T(8,128)(2,1)}, bf16[640,128]{1,0:T(8,128)(2,1)S(1)}, u32[]{:S(2)}, u32[]{:S(2)}) %collective-permute-start.13) | collective-permute-done | bytes 163872 | tf_op jit(solution)/shard_map/ppermute | solution.py:30
  176.2 1.0 add_convert_fusion.4
  177.2 2.0 collective-permute-start.14
  179.2 1.0 collective-permute-done.14
  180.3 0.1 collective-permute-start.15
  180.4 3.5 %add.87 = bf16[8,800,128]{2,1,0:T(8,128)(2,1)} add(bf16[8,800,128]{2,1,0:T(8,128)(2,1)} %get-tuple-element.27, bf16[8,800,128]{2,1,0:T(8,128)(2,1)} %collective-permute-done.7) | non-fusion elementwise | flops 819200 | bytes 4915200 | tf_op jit(solution)/shard_map/add | solution.py:692
  183.9 2.5 all-to-all-done.x_ref
  186.4 1.2 copy-done
  187.6 4.5 %all-to-all-start.1 = ((bf16[4,1600,128]{2,1,0:T(8,128)(2,1)}), bf16[4,1600,128]{2,1,0:T(8,128)(2,1)}, u32[]{:S(2)}, u32[]{:S(2)}) async-start(bf16[4,1600,128]{2,1,0:T(8,128)(2,1)} %bitcast.39), calls=%async_computation.1 | async-start | bytes 3276800 | tf_op jit(solution)/shard_map/all_to_all | solution.py:635
  192.2 1.4 collective-permute-start.16
  193.6 5.7 %collective-permute-done.16 = bf16[640,128]{1,0:T(8,128)(2,1)S(1)} collective-permute-done((bf16[640,128]{1,0:T(8,128)(2,1)S(1)}, bf16[640,128]{1,0:T(8,128)(2,1)S(1)}, u32[]{:S(2)}, u32[]{:S(2)}) %collective-permute-start.16) | collective-permute-done | bytes 163872 | tf_op jit(solution)/shard_map/ppermute | solution.py:648
  199.3 7.7 %collective-permute-start.17 = (bf16[640,128]{1,0:T(8,128)(2,1)S(1)}, bf16[640,128]{1,0:T(8,128)(2,1)S(1)}, u32[]{:S(2)}, u32[]{:S(2)}) collective-permute-start(bf16[640,128]{1,0:T(8,128)(2,1)S(1)} %add_convert_fusion.1), channel_id=1, source_target_pairs={{0,64},{8,72},{16,80},{24,88},{32,96},{40,104},{48,112},{56,120},{... | collective-permute-start | bytes 491528 | tf_op jit(solution)/shard_map/ppermute | solution.py:648
  207.1 1.8 dynamic-slice_bitcast_fusion
  208.9 1.7 collective-permute-done.17
  210.6 0.1 collective-permute-start.18
  210.7 2.4 sum_sides.3
  213.1 3.5 %collective-permute-start.2 = (bf16[800,128]{1,0:T(8,128)(2,1)}, bf16[800,128]{1,0:T(8,128)(2,1)S(1)}, u32[]{:S(2)}, u32[]{:S(2)}) collective-permute-start(bf16[800,128]{1,0:T(8,128)(2,1)} %get-tuple-element.26), channel_id=1, source_target_pairs={{0,1},{1,0},{2,3},{3,2},{4,5},{5,4},{6,7},{7,6},{8,9},{9,8},{10,11... | collective-permute-start | bytes 614408 | tf_op jit(solution)/shard_map/ppermute | solution.py:30
  216.6 2.4 sum_sides.4
  219.0 3.3 %collective-permute-done.2.b_ref = bf16[800,128]{1,0:T(8,128)(2,1)S(1)} collective-permute-done((bf16[800,128]{1,0:T(8,128)(2,1)}, bf16[800,128]{1,0:T(8,128)(2,1)S(1)}, u32[]{:S(2)}, u32[]{:S(2)}) %collective-permute-start.2) | collective-permute-done | bytes 204832 | tf_op jit(solution)/shard_map/ppermute | solution.py:30
  222.3 0.7 copy-done.11
  223.0 2.1 update.2
  225.1 1.8 collective-permute-start.3
  226.8 1.5 collective-permute-start.4
  228.3 2.1 collective-permute-start.5
  230.5 1.0 sort.17
  231.5 0.6 collective-permute-start.19
  232.1 2.7 collective-permute-start.20
  234.8 2.1 update.3
  236.9 3.5 %collective-permute-start.9 = (bf16[800,128]{1,0:T(8,128)(2,1)}, bf16[800,128]{1,0:T(8,128)(2,1)S(1)}, u32[]{:S(2)}, u32[]{:S(2)}) collective-permute-start(bf16[800,128]{1,0:T(8,128)(2,1)} %update.3), channel_id=1, source_target_pairs={{0,1},{1,0},{2,3},{3,2},{4,5},{5,4},{6,7},{7,6},{8,9},{9,8},{10,11... | collective-permute-start | bytes 614408 | tf_op jit(solution)/shard_map/ppermute | solution.py:30
  240.4 0.7 copy-done.8
  241.1 1.1 pad_maximum_fusion.a_ref
  242.3 0.9 collective-permute-start.6
  243.2 0.6 fusion.1.order
  243.8 2.3 collective-permute-start.21
  246.1 0.5 collective-permute-done.9
  246.7 0.6 collective-permute-start.10
  247.3 2.7 collective-permute-start.11
  250.0 1.9 collective-permute-start.12
  251.9 1.0 constant_dynamic-update-slice_fusion.2
  252.9 1.0 constant_dynamic-update-slice_fusion.1
  254.0 2.1 collective-permute-done.21
  256.1 1.0 copy-done.4
  257.1 3.5 %relation_out.1 = f32[400,1345]{1,0:T(8,128)} custom-call(s32[8]{0:T(128)} %fusion.1.order, bf16[8,640,128]{2,1,0:T(8,128)(2,1)} %copy-done.4), custom_call_target="tpu_custom_call" | custom-call | tf_op jit(solution)/shard_map/relation_out/pallas_call | solution.py:624
  260.7 3.2 %collective-permute-done.10.b1_ref = bf16[2,800,128]{2,1,0:T(8,128)(2,1)} collective-permute-done((bf16[2,800,128]{2,1,0:T(8,128)(2,1)S(1)}, bf16[2,800,128]{2,1,0:T(8,128)(2,1)}, u32[]{:S(2)}, u32[]{:S(2)}) %collective-permute-start.10) | collective-permute-done | bytes 409632 | tf_op jit(solution)/shard_map/ppermute | solution.py:30
  263.9 4.9 %collective-permute-done.12.b3_ref = bf16[2,800,128]{2,1,0:T(8,128)(2,1)} collective-permute-done((bf16[2,800,128]{2,1,0:T(8,128)(2,1)S(1)}, bf16[2,800,128]{2,1,0:T(8,128)(2,1)}, u32[]{:S(2)}, u32[]{:S(2)}) %collective-permute-start.12) | collective-permute-done | bytes 409632 | tf_op jit(solution)/shard_map/ppermute | solution.py:30
  268.8 6.2 %finish.1 = (bf16[400,4096]{1,0:T(8,128)(2,1)}, bf16[400,4096]{1,0:T(8,128)(2,1)}) custom-call(s32[8]{0:T(128)} %copy-done.16, bf16[4,800,128]{2,1,0:T(8,128)(2,1)} %copy-done.2, bf16[4,800,128]{2,1,0:T(8,128)(2,1)} %collective-permute-done.6.ar_ref, bf16[2,800,128]{2,1,0:T(8,128)(2,1)} %copy-done.5, bf16[2,800,128]{2,1,0:T(8,128)(2,1)} %collective-permute-done.10.b1_ref, ...), custom_call_target="tpu_custom_call" | custom-call | tf_op jit(solution)/shard_map/finish/pallas_call | solution.py:607
  (59 shorter events, 0.7 us)
Async XLA Ops:
  0.6 6.9 %copy-start.12 = (s32[1,1,1,8192]{3,2,1,0:T(1,128)S(1)}, s32[1,1,1,8192]{3,2,1,0:T(1,128)}, u32[]{:S(2)}) copy-start(s32[1,1,1,8192]{3,2,1,0:T(1,128)} %param.10) | copy-start | bytes 98308
  0.6 7.5 %copy-start.3 = (f32[1345,400]{0,1:T(8,128)S(1)}, f32[1345,400]{0,1:T(8,128)}, u32[]{:S(2)}) copy-start(f32[1345,400]{0,1:T(8,128)} %param.9) | copy-start | bytes 6456004
  0.7 36.6 %collective-permute-start = (bf16[4096,400]{0,1:T(8,128)(2,1)}, bf16[4096,400]{0,1:T(8,128)(2,1)}, u32[]{:S(2)}, u32[]{:S(2)}) collective-permute-start(bf16[4096,400]{0,1:T(8,128)(2,1)} %param.8), channel_id=1, source_target_pairs={{0,120},{8,0},{16,8},{24,16},{32,24},{40,32},{48,40},{56,48},{64,5... | collective-permute-start | bytes 9830408 | tf_op jit(solution)/shard_map/ppermute | solution.py:30
  8.2 2.2 copy-start.13
  8.2 2.8 %copy-start.14 = (s32[1,1,1,8192]{3,2,1,0:T(1,128)S(1)}, s32[1,1,1,8192]{3,2,1,0:T(1,128)}, u32[]{:S(2)}) copy-start(s32[1,1,1,8192]{3,2,1,0:T(1,128)} %param.11) | copy-start | bytes 98308
  11.6 16.8 %copy-start.15 = (s32[1,1,1,8192]{3,2,1,0:T(1,128)S(1)}, s32[1,1,1,8192]{3,2,1,0:T(1,128)}, u32[]{:S(2)}) copy-start(s32[1,1,1,8192]{3,2,1,0:T(1,128)} %param.12) | copy-start | bytes 98308
  97.3 58.7 %collective-permute-start.1 = (bf16[8,800,128]{2,1,0:T(8,128)(2,1)}, bf16[8,800,128]{2,1,0:T(8,128)(2,1)S(1)}, u32[]{:S(2)}, u32[]{:S(2)}) collective-permute-start(bf16[8,800,128]{2,1,0:T(8,128)(2,1)} %get-tuple-element.24), channel_id=1, source_target_pairs={{0,8},{8,16},{16,24},{24,32},{32,40},{40,48},{48,56},{56,64},{64,7... | collective-permute-start | bytes 4915208 | tf_op jit(solution)/shard_map/ppermute | solution.py:30
  110.4 48.6 %all-to-all-start.2 = ((bf16[4,1280,128]{2,1,0:T(8,128)(2,1)}), bf16[4,1280,128]{2,1,0:T(8,128)(2,1)S(1)}, u32[]{:S(2)}, u32[]{:S(2)}) async-start(bf16[4,1280,128]{2,1,0:T(8,128)(2,1)} %bitcast.42), calls=%async_computation.2 | async-start | bytes 2621440 | tf_op jit(solution)/shard_map/all_to_all | solution.py:635
  140.7 39.6 %collective-permute-start.7 = (bf16[8,800,128]{2,1,0:T(8,128)(2,1)}, bf16[8,800,128]{2,1,0:T(8,128)(2,1)}, u32[]{:S(2)}, u32[]{:S(2)}) collective-permute-start(bf16[8,800,128]{2,1,0:T(8,128)(2,1)} %get-tuple-element.28), channel_id=1, source_target_pairs={{0,8},{8,16},{16,24},{24,32},{32,40},{40,48},{48,56},{56,64},{64,7... | collective-permute-start | bytes 4915208 | tf_op jit(solution)/shard_map/ppermute | solution.py:30
  159.0 1.1 copy-start.1
  160.2 26.2 %all-to-all-start = ((bf16[4,1600,128]{2,1,0:T(8,128)(2,1)}), bf16[4,1600,128]{2,1,0:T(8,128)(2,1)S(1)}, u32[]{:S(2)}, u32[]{:S(2)}) async-start(bf16[4,1600,128]{2,1,0:T(8,128)(2,1)} %bitcast.40), calls=%async_computation | async-start | bytes 3276800 | tf_op jit(solution)/shard_map/all_to_all | solution.py:635
  168.4 7.8 %collective-permute-start.13 = (bf16[640,128]{1,0:T(8,128)(2,1)}, bf16[640,128]{1,0:T(8,128)(2,1)S(1)}, u32[]{:S(2)}, u32[]{:S(2)}) collective-permute-start(bf16[640,128]{1,0:T(8,128)(2,1)} %get-tuple-element.35), channel_id=1, source_target_pairs={{0,1},{1,0},{2,3},{3,2},{4,5},{5,4},{6,7},{7,6},{8,9},{9,8},{10,11... | collective-permute-start | bytes 491528 | tf_op jit(solution)/shard_map/ppermute | solution.py:30
  177.2 3.1 %collective-permute-start.14 = (bf16[640,128]{1,0:T(8,128)(2,1)S(1)}, bf16[640,128]{1,0:T(8,128)(2,1)S(1)}, u32[]{:S(2)}, u32[]{:S(2)}) collective-permute-start(bf16[640,128]{1,0:T(8,128)(2,1)S(1)} %add_convert_fusion.4), channel_id=1, source_target_pairs={{0,8},{8,0},{16,24},{24,16},{32,40},{40,32},{48,56},{56,48},{64,72... | collective-permute-start | bytes 491528 | tf_op jit(solution)/shard_map/ppermute | solution.py:648
  180.3 11.8 %collective-permute-start.15 = (bf16[640,128]{1,0:T(8,128)(2,1)S(1)}, bf16[640,128]{1,0:T(8,128)(2,1)S(1)}, u32[]{:S(2)}, u32[]{:S(2)}) collective-permute-start(bf16[640,128]{1,0:T(8,128)(2,1)S(1)} %add_convert_fusion.3), channel_id=1, source_target_pairs={{0,16},{8,24},{16,0},{24,8},{32,48},{40,56},{48,32},{56,40},{64,80... | collective-permute-start | bytes 491528 | tf_op jit(solution)/shard_map/ppermute | solution.py:648
  186.4 1.2 copy-start
  187.6 29.0 %all-to-all-start.1 = ((bf16[4,1600,128]{2,1,0:T(8,128)(2,1)}), bf16[4,1600,128]{2,1,0:T(8,128)(2,1)}, u32[]{:S(2)}, u32[]{:S(2)}) async-start(bf16[4,1600,128]{2,1,0:T(8,128)(2,1)} %bitcast.39), calls=%async_computation.1 | async-start | bytes 3276800 | tf_op jit(solution)/shard_map/all_to_all | solution.py:635
  192.2 7.1 %collective-permute-start.16 = (bf16[640,128]{1,0:T(8,128)(2,1)S(1)}, bf16[640,128]{1,0:T(8,128)(2,1)S(1)}, u32[]{:S(2)}, u32[]{:S(2)}) collective-permute-start(bf16[640,128]{1,0:T(8,128)(2,1)S(1)} %add_convert_fusion.2), channel_id=1, source_target_pairs={{0,32},{8,40},{16,48},{24,56},{32,0},{40,8},{48,16},{56,24},{64,96... | collective-permute-start | bytes 491528 | tf_op jit(solution)/shard_map/ppermute | solution.py:648
  199.3 11.2 %collective-permute-start.17 = (bf16[640,128]{1,0:T(8,128)(2,1)S(1)}, bf16[640,128]{1,0:T(8,128)(2,1)S(1)}, u32[]{:S(2)}, u32[]{:S(2)}) collective-permute-start(bf16[640,128]{1,0:T(8,128)(2,1)S(1)} %add_convert_fusion.1), channel_id=1, source_target_pairs={{0,64},{8,72},{16,80},{24,88},{32,96},{40,104},{48,112},{56,120},{... | collective-permute-start | bytes 491528 | tf_op jit(solution)/shard_map/ppermute | solution.py:648
  210.6 20.8 %collective-permute-start.18 = (bf16[640,128]{1,0:T(8,128)(2,1)S(1)}, bf16[640,128]{1,0:T(8,128)(2,1)S(1)}, u32[]{:S(2)}, u32[]{:S(2)}) collective-permute-start(bf16[640,128]{1,0:T(8,128)(2,1)S(1)} %get-tuple-element.38), channel_id=1, source_target_pairs={{0,1},{1,0},{2,3},{3,2},{4,5},{5,4},{6,7},{7,6},{8,9},{9,8},{10,11... | collective-permute-start | bytes 491528 | tf_op jit(solution)/shard_map/ppermute | solution.py:30
  213.1 9.2 %collective-permute-start.2 = (bf16[800,128]{1,0:T(8,128)(2,1)}, bf16[800,128]{1,0:T(8,128)(2,1)S(1)}, u32[]{:S(2)}, u32[]{:S(2)}) collective-permute-start(bf16[800,128]{1,0:T(8,128)(2,1)} %get-tuple-element.26), channel_id=1, source_target_pairs={{0,1},{1,0},{2,3},{3,2},{4,5},{5,4},{6,7},{7,6},{8,9},{9,8},{10,11... | collective-permute-start | bytes 614408 | tf_op jit(solution)/shard_map/ppermute | solution.py:30
  219.0 13.1 %collective-permute-start.8 = (bf16[800,128]{1,0:T(8,128)(2,1)}, bf16[800,128]{1,0:T(8,128)(2,1)S(1)}, u32[]{:S(2)}, u32[]{:S(2)}) collective-permute-start(bf16[800,128]{1,0:T(8,128)(2,1)} %get-tuple-element.30), channel_id=1, source_target_pairs={{0,1},{1,0},{2,3},{3,2},{4,5},{5,4},{6,7},{7,6},{8,9},{9,8},{10,11... | collective-permute-start | bytes 614408 | tf_op jit(solution)/shard_map/ppermute | solution.py:30
  222.3 0.7 copy-start.11
  225.1 16.1 %copy-start.6 = (bf16[800,128]{1,0:T(8,128)(2,1)S(1)}, bf16[800,128]{1,0:T(8,128)(2,1)}, u32[]{:S(2)}) copy-start(bf16[800,128]{1,0:T(8,128)(2,1)} %update.2) | copy-start | bytes 614404
  225.1 11.8 %collective-permute-start.3 = (bf16[800,128]{1,0:T(8,128)(2,1)}, bf16[800,128]{1,0:T(8,128)(2,1)S(1)}, u32[]{:S(2)}, u32[]{:S(2)}) collective-permute-start(bf16[800,128]{1,0:T(8,128)(2,1)} %update.2), channel_id=1, source_target_pairs={{0,2},{2,4},{4,6},{6,0},{1,3},{3,5},{5,7},{7,1},{8,10},{10,12},{12... | collective-permute-start | bytes 614408 | tf_op jit(solution)/shard_map/ppermute | solution.py:30
  226.8 13.5 %collective-permute-start.4 = (bf16[800,128]{1,0:T(8,128)(2,1)}, bf16[800,128]{1,0:T(8,128)(2,1)S(1)}, u32[]{:S(2)}, u32[]{:S(2)}) collective-permute-start(bf16[800,128]{1,0:T(8,128)(2,1)} %update.2), channel_id=1, source_target_pairs={{0,6},{2,0},{4,2},{6,4},{1,7},{3,1},{5,3},{7,5},{8,14},{10,8},{12,... | collective-permute-start | bytes 614408 | tf_op jit(solution)/shard_map/ppermute | solution.py:30
  228.3 12.1 %collective-permute-start.5 = (bf16[800,128]{1,0:T(8,128)(2,1)}, bf16[800,128]{1,0:T(8,128)(2,1)S(1)}, u32[]{:S(2)}, u32[]{:S(2)}) collective-permute-start(bf16[800,128]{1,0:T(8,128)(2,1)} %update.2), channel_id=1, source_target_pairs={{0,4},{2,6},{4,0},{6,2},{1,5},{3,7},{5,1},{7,3},{8,12},{10,14},{12... | collective-permute-start | bytes 614408 | tf_op jit(solution)/shard_map/ppermute | solution.py:30
  230.4 11.8 %copy-start.16 = (s32[8]{0:T(128)}, s32[8]{0:T(128)S(1)}, u32[]{:S(2)}) copy-start(s32[8]{0:T(128)S(1)} %pad_add_fusion.place) | copy-start | bytes 100
  231.5 15.9 %collective-permute-start.19 = (bf16[2,640,128]{2,1,0:T(8,128)(2,1)S(1)}, bf16[2,640,128]{2,1,0:T(8,128)(2,1)}, u32[]{:S(2)}, u32[]{:S(2)}) collective-permute-start(bf16[2,640,128]{2,1,0:T(8,128)(2,1)S(1)} %pad_maximum_fusion.2), channel_id=1, source_target_pairs={{0,2},{2,4},{4,6},{6,0},{1,3},{3,5},{5,7},{7,1},{8,10},{10,12},{12... | collective-permute-start | bytes 983048 | tf_op jit(solution)/shard_map/ppermute | solution.py:30
  232.1 2.7 copy-start.10
  232.1 17.9 %collective-permute-start.20 = (bf16[2,640,128]{2,1,0:T(8,128)(2,1)S(1)}, bf16[2,640,128]{2,1,0:T(8,128)(2,1)}, u32[]{:S(2)}, u32[]{:S(2)}) collective-permute-start(bf16[2,640,128]{2,1,0:T(8,128)(2,1)S(1)} %pad_maximum_fusion.2), channel_id=1, source_target_pairs={{0,6},{2,0},{4,2},{6,4},{1,7},{3,1},{5,3},{7,5},{8,14},{10,8},{12,... | collective-permute-start | bytes 983048 | tf_op jit(solution)/shard_map/ppermute | solution.py:30
  236.9 9.8 %copy-start.7 = (bf16[800,128]{1,0:T(8,128)(2,1)S(1)}, bf16[800,128]{1,0:T(8,128)(2,1)}, u32[]{:S(2)}) copy-start(bf16[800,128]{1,0:T(8,128)(2,1)} %update.3) | copy-start | bytes 614404
  236.9 9.8 %collective-permute-start.9 = (bf16[800,128]{1,0:T(8,128)(2,1)}, bf16[800,128]{1,0:T(8,128)(2,1)S(1)}, u32[]{:S(2)}, u32[]{:S(2)}) collective-permute-start(bf16[800,128]{1,0:T(8,128)(2,1)} %update.3), channel_id=1, source_target_pairs={{0,1},{1,0},{2,3},{3,2},{4,5},{5,4},{6,7},{7,6},{8,9},{9,8},{10,11... | collective-permute-start | bytes 614408 | tf_op jit(solution)/shard_map/ppermute | solution.py:30
  240.4 0.7 copy-start.8
  240.4 0.7 copy-start.9
  242.3 18.4 %copy-start.2 = (bf16[4,800,128]{2,1,0:T(8,128)(2,1)}, bf16[4,800,128]{2,1,0:T(8,128)(2,1)S(1)}, u32[]{:S(2)}) copy-start(bf16[4,800,128]{2,1,0:T(8,128)(2,1)S(1)} %pad_maximum_fusion.a_ref) | copy-start | bytes 2457604
  242.3 26.5 %collective-permute-start.6 = (bf16[4,800,128]{2,1,0:T(8,128)(2,1)S(1)}, bf16[4,800,128]{2,1,0:T(8,128)(2,1)}, u32[]{:S(2)}, u32[]{:S(2)}) collective-permute-start(bf16[4,800,128]{2,1,0:T(8,128)(2,1)S(1)} %pad_maximum_fusion.a_ref), channel_id=1, source_target_pairs={{0,1},{1,0},{2,3},{3,2},{4,5},{5,4},{6,7},{7,6},{8,9},{9,8},{10,11... | collective-permute-start | bytes 2457608 | tf_op jit(solution)/shard_map/ppermute | solution.py:30
  243.8 12.3 %collective-permute-start.21 = (bf16[2,640,128]{2,1,0:T(8,128)(2,1)S(1)}, bf16[2,640,128]{2,1,0:T(8,128)(2,1)S(1)}, u32[]{:S(2)}, u32[]{:S(2)}) collective-permute-start(bf16[2,640,128]{2,1,0:T(8,128)(2,1)S(1)} %pad_maximum_fusion.2), channel_id=1, source_target_pairs={{0,4},{2,6},{4,0},{6,2},{1,5},{3,7},{5,1},{7,3},{8,12},{10,14},{12... | collective-permute-start | bytes 983048 | tf_op jit(solution)/shard_map/ppermute | solution.py:30
  246.7 14.0 %copy-start.5 = (bf16[2,800,128]{2,1,0:T(8,128)(2,1)}, bf16[2,800,128]{2,1,0:T(8,128)(2,1)S(1)}, u32[]{:S(2)}) copy-start(bf16[2,800,128]{2,1,0:T(8,128)(2,1)S(1)} %pad_maximum_fusion.1.b0_ref) | copy-start | bytes 1228804
  246.7 17.2 %collective-permute-start.10 = (bf16[2,800,128]{2,1,0:T(8,128)(2,1)S(1)}, bf16[2,800,128]{2,1,0:T(8,128)(2,1)}, u32[]{:S(2)}, u32[]{:S(2)}) collective-permute-start(bf16[2,800,128]{2,1,0:T(8,128)(2,1)S(1)} %pad_maximum_fusion.1.b0_ref), channel_id=1, source_target_pairs={{0,2},{2,4},{4,6},{6,0},{1,3},{3,5},{5,7},{7,1},{8,10},{10,12},{12... | collective-permute-start | bytes 1228808 | tf_op jit(solution)/shard_map/ppermute | solution.py:30
  247.3 16.6 %collective-permute-start.11 = (bf16[2,800,128]{2,1,0:T(8,128)(2,1)S(1)}, bf16[2,800,128]{2,1,0:T(8,128)(2,1)}, u32[]{:S(2)}, u32[]{:S(2)}) collective-permute-start(bf16[2,800,128]{2,1,0:T(8,128)(2,1)S(1)} %pad_maximum_fusion.1.b0_ref), channel_id=1, source_target_pairs={{0,6},{2,0},{4,2},{6,4},{1,7},{3,1},{5,3},{7,5},{8,14},{10,8},{12,... | collective-permute-start | bytes 1228808 | tf_op jit(solution)/shard_map/ppermute | solution.py:30
  250.0 18.8 %collective-permute-start.12 = (bf16[2,800,128]{2,1,0:T(8,128)(2,1)S(1)}, bf16[2,800,128]{2,1,0:T(8,128)(2,1)}, u32[]{:S(2)}, u32[]{:S(2)}) collective-permute-start(bf16[2,800,128]{2,1,0:T(8,128)(2,1)S(1)} %pad_maximum_fusion.1.b0_ref), channel_id=1, source_target_pairs={{0,4},{2,6},{4,0},{6,2},{1,5},{3,7},{5,1},{7,3},{8,12},{10,14},{12... | collective-permute-start | bytes 1228808 | tf_op jit(solution)/shard_map/ppermute | solution.py:30
  256.1 1.1 copy-start.4

commit v7 on v6

--- a/solution.py
+++ b/solution.py
@@ -333,10 +333,10 @@
                 )
 
         def looped(step, h, start, stop):
-            @pl.loop(0, (stop - start) // 16)
+            @pl.loop(0, (stop - start) // 32)
             def _(q):
-                at = pl.multiple_of(start + q * 16, 16)
-                step(h, at, pl.multiple_of(at * GROUPS, 64), 16)
+                at = pl.multiple_of(start + q * 32, 32)
+                step(h, at, pl.multiple_of(at * GROUPS, 128), 32)
 
         dense(0, db0)
         add_edges(0, 0, 0, CHUNK)
@@ -418,13 +418,13 @@
         fetch(blk, slot).wait()
         vs = vb.at[slot]
 
-        @pl.loop(0, SPAN // 16)
+        @pl.loop(0, SPAN // 32)
         def _(q):
-            base = pl.multiple_of(q * 16 * GROUPS, 64)
-            for t in range(0, 16, 4):
+            base = pl.multiple_of(q * 32 * GROUPS, 128)
+            for t in range(0, 32, 4):
                 add_rows(
                     [
-                        (accs[i], row_of(src_i[blk * SPAN + q * 16 + t + i]), vs, slot_of(base, t + i))
+                        (accs[i], row_of(src_i[blk * SPAN + q * 32 + t + i]), vs, slot_of(base, t + i))
                         for i in range(4)
                     ]
                 )

time: 279 us -> 278 us (level)
  Pallas kernels: 107 us -> 93.6 us
  starting transfers between devices: 93.6 us -> 102 us
  waiting for transfers between devices: 36.7 us -> 39.8 us
    all_to_all x3, starting transfers between devices: 40.9 us -> 66.4 us  [by_side(): return lax.all_to_all(x.reshape(sides, -1, LANES), 'side', 0, 0, tiled=True)]
    ppermute x18, starting transfers between devices: 41.5 us -> 23 us  [shifted(): return lax.ppermute(x, axis, [(i, (i + by) % count) for i in range(count)])]
    pallas_call x1, Pallas kernels: 54 us -> 44.4 us  [edge_blocks(): pl.pallas_call(functools.partial(block_kernel, nneg), out_shape=(half, ha...]
    ppermute x18, waiting for transfers between devices: 25.8 us -> 32.5 us  [shifted(): return lax.ppermute(x, axis, [(i, (i + by) % count) for i in range(count)])]
  transfers between devices with their start and end apart: 25 -> 25, of which waited for: 11 -> 12; matrix products, arithmetic and copies ran while one was open for 9% -> 9% of each run, Pallas kernels for 17% -> 16%
where the time goes in v7:
time: 278 us; the launch traced here: 273 us
  starting transfers between devices  102 us (37%)
  Pallas kernels  93.6 us (34%)
  waiting for transfers between devices  39.8 us (14%)
  local copies, waits for them, and re-layouts  23.6 us (8%)
  other arithmetic  12.5 us (4%)
    all_to_all x3, starting transfers between devices, by_side(): return lax.all_to_all(x.reshape(sides, -1, LANES), 'side', 0, 0, tiled=True)  66.4 us
    pallas_call x1, Pallas kernels, edge_blocks(): pl.pallas_call(functools.partial(block_kernel, nneg), out_shape=(half, ha...  44.4 us
    ppermute x18, waiting for transfers between devices, shifted(): return lax.ppermute(x, axis, [(i, (i + by) % count) for i in range(count)])  32.5 us
    ppermute x18, starting transfers between devices, shifted(): return lax.ppermute(x, axis, [(i, (i + by) % count) for i in range(count)])  23 us
    unnamed x40, local copies, waits for them, and re-layouts  15.7 us
    pallas_call x1, Pallas kernels, edge_rows(): pl.pallas_call(edge_rows_kernel, out_shape=(shape, shape), in_specs=[smem...  14.9 us
    pallas_call x1, Pallas kernels, source_rows(): pl.pallas_call(source_kernel, out_shape=(half, half), in_specs=[smem()] *...  13.4 us
    ppermute x4, starting transfers between devices, swapped(): return lax.ppermute(x, axis, [(i, i ^ bit) for i in range(count)])  12.6 us
  transfers between devices with their start and end apart: 25, of which 12 were waited for; matrix products, arithmetic and copies ran while one was open for 9% of the time, Pallas kernels for 16%

profile of v7, /device:TPU:96, one launch (start us, length us, event | category | flops | bytes accessed | tf_op | source)
XLA Modules:
  0.0 273.0 jit_solution(17969841241522897677)
XLA Ops:
  0.7 6.2 %copy.14.emb_hbm = bf16[4096,400]{1,0:T(8,128)(2,1)} copy(bf16[4096,400]{0,1:T(8,128)(2,1)} %param.8) | data formatting | bytes 6553600 | tf_op args[0]
  7.6 0.6 broadcast_multiply_fusion.2
  8.2 2.2 copy.15.rel_ref
  10.4 0.6 copy.19
  11.0 0.6 broadcast_multiply_fusion.1
  11.6 14.9 %edge_rows.1 = (f32[8,4096,128]{2,1,0:T(8,128)}, f32[8,4096,128]{2,1,0:T(8,128)}) custom-call(s32[1]{0:T(128)} %bitcast.36.count, s32[8192]{0:T(1024)} %bitcast.47, s32[8192]{0:T(1024)} %bitcast.49, bf16[4096,400]{1,0:T(8,128)(2,1)} %copy.14.emb_hbm, f32[1345,400]{1,0:T(8,128)} %copy.15.rel_ref), custom_call_target="tpu_custom_call" | custom-call | bytes 60000000 | tf_op jit(solution)/shard_map/edge_rows/pallas_call | solution.py:451
  26.5 0.6 broadcast_multiply_fusion
  27.2 10.1 %collective-permute-done = bf16[4096,400]{0,1:T(8,128)(2,1)} collective-permute-done((bf16[4096,400]{0,1:T(8,128)(2,1)}, bf16[4096,400]{0,1:T(8,128)(2,1)}, u32[]{:S(2)}, u32[]{:S(2)}) %collective-permute-start) | collective-permute-done | bytes 3276832 | tf_op jit(solution)/shard_map/ppermute | solution.py:30
  37.2 6.0 %copy.16.dst_hbm = bf16[4096,400]{1,0:T(8,128)(2,1)} copy(bf16[4096,400]{0,1:T(8,128)(2,1)} %collective-permute-done) | data formatting | bytes 6553600 | tf_op jit(solution)/shard_map/ppermute | solution.py:30
  43.2 44.4 %edge_blocks.1 = (bf16[8,800,128]{2,1,0:T(8,128)(2,1)}, bf16[8,800,128]{2,1,0:T(8,128)(2,1)}, bf16[8,640,128]{2,1,0:T(8,128)(2,1)}, f32[8,4096,128]{2,1,0:T(8,128)}) custom-call(s32[1]{0:T(128)} %bitcast.37.count, s32[8192]{0:T(1024)} %bitcast.50, s32[8192]{0:T(1024)} %bitcast.56, s32[8192]{0:T(1024)} %bitcast.55, bf16[4096,400]{1,0:T(8,128)(2,1)} %copy.16.dst_hbm, ...), custom_call_target="tpu_custom_call" | custom-call | tf_op jit(solution)/shard_map/edge_blocks/pallas_call | solution.py:481
  87.8 49.5 %all-to-all-start.2 = ((bf16[4,1280,128]{2,1,0:T(8,128)(2,1)}), bf16[4,1280,128]{2,1,0:T(8,128)(2,1)S(1)}, u32[]{:S(2)}, u32[]{:S(2)}) async-start(bf16[4,1280,128]{2,1,0:T(8,128)(2,1)} %bitcast.42), calls=%async_computation.2 | async-start | bytes 2621440 | tf_op jit(solution)/shard_map/all_to_all | solution.py:635
  137.2 13.4 %source_rows.1 = (bf16[8,800,128]{2,1,0:T(8,128)(2,1)}, bf16[8,800,128]{2,1,0:T(8,128)(2,1)}) custom-call(s32[1]{0:T(128)} %bitcast.38.count, s32[8192]{0:T(1024)} %bitcast.48, f32[8,4096,128]{2,1,0:T(8,128)} %get-tuple-element.22.v_hbm), custom_call_target="tpu_custom_call" | custom-call | bytes 60000000 | tf_op jit(solution)/shard_map/source_rows/pallas_call | solution.py:519
  150.6 3.0 %add.84 = bf16[8,800,128]{2,1,0:T(8,128)(2,1)} add(bf16[8,800,128]{2,1,0:T(8,128)(2,1)} %get-tuple-element.23.after_ref, bf16[8,800,128]{2,1,0:T(8,128)(2,1)S(1)} %collective-permute-done.1) | non-fusion elementwise | flops 819200 | bytes 4915200 | tf_op jit(solution)/shard_map/add | solution.py:692
  153.7 1.1 copy-done.1
  154.8 12.0 %all-to-all-start = ((bf16[4,1600,128]{2,1,0:T(8,128)(2,1)}), bf16[4,1600,128]{2,1,0:T(8,128)(2,1)S(1)}, u32[]{:S(2)}, u32[]{:S(2)}) async-start(bf16[4,1600,128]{2,1,0:T(8,128)(2,1)} %bitcast.40), calls=%async_computation | async-start | bytes 3276800 | tf_op jit(solution)/shard_map/all_to_all | solution.py:635
  166.8 2.2 sum_sides.5
  169.0 7.0 %collective-permute-done.13 = bf16[640,128]{1,0:T(8,128)(2,1)S(1)} collective-permute-done((bf16[640,128]{1,0:T(8,128)(2,1)}, bf16[640,128]{1,0:T(8,128)(2,1)S(1)}, u32[]{:S(2)}, u32[]{:S(2)}) %collective-permute-start.13) | collective-permute-done | bytes 163872 | tf_op jit(solution)/shard_map/ppermute | solution.py:30
  176.0 1.0 add_convert_fusion.4
  177.0 0.1 collective-permute-start.14
  177.1 1.4 collective-permute-done.14
  178.6 0.1 collective-permute-start.15
  178.7 3.5 %add.87 = bf16[8,800,128]{2,1,0:T(8,128)(2,1)} add(bf16[8,800,128]{2,1,0:T(8,128)(2,1)} %get-tuple-element.27, bf16[8,800,128]{2,1,0:T(8,128)(2,1)} %collective-permute-done.7) | non-fusion elementwise | flops 819200 | bytes 4915200 | tf_op jit(solution)/shard_map/add | solution.py:692
  182.2 1.2 copy-done
  183.3 5.0 %all-to-all-start.1 = ((bf16[4,1600,128]{2,1,0:T(8,128)(2,1)}), bf16[4,1600,128]{2,1,0:T(8,128)(2,1)}, u32[]{:S(2)}, u32[]{:S(2)}) async-start(bf16[4,1600,128]{2,1,0:T(8,128)(2,1)} %bitcast.39), calls=%async_computation.1 | async-start | bytes 3276800 | tf_op jit(solution)/shard_map/all_to_all | solution.py:635
  188.4 5.1 %collective-permute-start.16 = (bf16[640,128]{1,0:T(8,128)(2,1)S(1)}, bf16[640,128]{1,0:T(8,128)(2,1)S(1)}, u32[]{:S(2)}, u32[]{:S(2)}) collective-permute-start(bf16[640,128]{1,0:T(8,128)(2,1)S(1)} %add_convert_fusion.2), channel_id=1, source_target_pairs={{0,32},{8,40},{16,48},{24,56},{32,0},{40,8},{48,16},{56,24},{64,96... | collective-permute-start | bytes 491528 | tf_op jit(solution)/shard_map/ppermute | solution.py:648
  193.5 3.9 %collective-permute-done.16 = bf16[640,128]{1,0:T(8,128)(2,1)S(1)} collective-permute-done((bf16[640,128]{1,0:T(8,128)(2,1)S(1)}, bf16[640,128]{1,0:T(8,128)(2,1)S(1)}, u32[]{:S(2)}, u32[]{:S(2)}) %collective-permute-start.16) | collective-permute-done | bytes 163872 | tf_op jit(solution)/shard_map/ppermute | solution.py:648
  197.5 7.3 %collective-permute-start.17 = (bf16[640,128]{1,0:T(8,128)(2,1)S(1)}, bf16[640,128]{1,0:T(8,128)(2,1)S(1)}, u32[]{:S(2)}, u32[]{:S(2)}) collective-permute-start(bf16[640,128]{1,0:T(8,128)(2,1)S(1)} %add_convert_fusion.1), channel_id=1, source_target_pairs={{0,64},{8,72},{16,80},{24,88},{32,96},{40,104},{48,112},{56,120},{... | collective-permute-start | bytes 491528 | tf_op jit(solution)/shard_map/ppermute | solution.py:648
  204.8 0.1 broadcast_add_fusion
  204.9 1.8 dynamic-slice_bitcast_fusion
  206.7 1.9 collective-permute-done.17
  208.7 3.0 %collective-permute-start.18 = (bf16[640,128]{1,0:T(8,128)(2,1)S(1)}, bf16[640,128]{1,0:T(8,128)(2,1)S(1)}, u32[]{:S(2)}, u32[]{:S(2)}) collective-permute-start(bf16[640,128]{1,0:T(8,128)(2,1)S(1)} %get-tuple-element.38), channel_id=1, source_target_pairs={{0,1},{1,0},{2,3},{3,2},{4,5},{5,4},{6,7},{7,6},{8,9},{9,8},{10,11... | collective-permute-start | bytes 491528 | tf_op jit(solution)/shard_map/ppermute | solution.py:30
  211.7 2.4 sum_sides.3
  214.1 0.6 collective-permute-start.2
  214.7 2.4 sum_sides.4
  217.1 2.9 %collective-permute-start.8 = (bf16[800,128]{1,0:T(8,128)(2,1)}, bf16[800,128]{1,0:T(8,128)(2,1)S(1)}, u32[]{:S(2)}, u32[]{:S(2)}) collective-permute-start(bf16[800,128]{1,0:T(8,128)(2,1)} %get-tuple-element.30), channel_id=1, source_target_pairs={{0,1},{1,0},{2,3},{3,2},{4,5},{5,4},{6,7},{7,6},{8,9},{9,8},{10,11... | collective-permute-start | bytes 614408 | tf_op jit(solution)/shard_map/ppermute | solution.py:30
  220.0 3.4 %collective-permute-done.2.b_ref = bf16[800,128]{1,0:T(8,128)(2,1)S(1)} collective-permute-done((bf16[800,128]{1,0:T(8,128)(2,1)}, bf16[800,128]{1,0:T(8,128)(2,1)S(1)}, u32[]{:S(2)}, u32[]{:S(2)}) %collective-permute-start.2) | collective-permute-done | bytes 204832 | tf_op jit(solution)/shard_map/ppermute | solution.py:30
  223.4 0.7 copy-done.11
  224.1 2.1 update.2
  226.2 1.8 collective-permute-start.3
  228.0 1.4 collective-permute-start.4
  229.4 2.1 collective-permute-start.5
  231.6 1.0 sort.17
  232.6 0.6 collective-permute-start.19
  233.2 2.7 collective-permute-start.20
  235.9 2.1 update.3
  238.0 0.5 collective-permute-start.9
  238.5 0.1 collective-permute-done.5
  238.7 0.5 copy-done.8
  239.2 0.1 copy-done.9
  239.3 1.1 pad_maximum_fusion.a_ref
  240.5 3.2 %collective-permute-start.6 = (bf16[4,800,128]{2,1,0:T(8,128)(2,1)S(1)}, bf16[4,800,128]{2,1,0:T(8,128)(2,1)}, u32[]{:S(2)}, u32[]{:S(2)}) collective-permute-start(bf16[4,800,128]{2,1,0:T(8,128)(2,1)S(1)} %pad_maximum_fusion.a_ref), channel_id=1, source_target_pairs={{0,1},{1,0},{2,3},{3,2},{4,5},{5,4},{6,7},{7,6},{8,9},{9,8},{10,11... | collective-permute-start | bytes 2457608 | tf_op jit(solution)/shard_map/ppermute | solution.py:30
  243.7 0.6 fusion.1.order
  244.3 0.6 collective-permute-start.21
  245.0 2.8 %collective-permute-done.9 = bf16[800,128]{1,0:T(8,128)(2,1)S(1)} collective-permute-done((bf16[800,128]{1,0:T(8,128)(2,1)}, bf16[800,128]{1,0:T(8,128)(2,1)S(1)}, u32[]{:S(2)}, u32[]{:S(2)}) %collective-permute-start.9) | collective-permute-done | bytes 204832 | tf_op jit(solution)/shard_map/ppermute | solution.py:30
  247.9 3.2 %collective-permute-start.11 = (bf16[2,800,128]{2,1,0:T(8,128)(2,1)S(1)}, bf16[2,800,128]{2,1,0:T(8,128)(2,1)}, u32[]{:S(2)}, u32[]{:S(2)}) collective-permute-start(bf16[2,800,128]{2,1,0:T(8,128)(2,1)S(1)} %pad_maximum_fusion.1.b0_ref), channel_id=1, source_target_pairs={{0,6},{2,0},{4,2},{6,4},{1,7},{3,1},{5,3},{7,5},{8,14},{10,8},{12,... | collective-permute-start | bytes 1228808 | tf_op jit(solution)/shard_map/ppermute | solution.py:30
  251.2 1.0 constant_dynamic-update-slice_fusion.2
  252.2 1.0 constant_dynamic-update-slice_fusion.1
  253.2 3.4 %collective-permute-done.21 = bf16[2,640,128]{2,1,0:T(8,128)(2,1)S(1)} collective-permute-done((bf16[2,640,128]{2,1,0:T(8,128)(2,1)S(1)}, bf16[2,640,128]{2,1,0:T(8,128)(2,1)S(1)}, u32[]{:S(2)}, u32[]{:S(2)}) %collective-permute-start.21) | collective-permute-done | bytes 327712 | tf_op jit(solution)/shard_map/ppermute | solution.py:30
  256.6 1.0 copy-done.4
  257.7 3.5 %relation_out.1 = f32[400,1345]{1,0:T(8,128)} custom-call(s32[8]{0:T(128)} %fusion.1.order, bf16[8,640,128]{2,1,0:T(8,128)(2,1)} %copy-done.4), custom_call_target="tpu_custom_call" | custom-call | tf_op jit(solution)/shard_map/relation_out/pallas_call | solution.py:624
  261.2 1.2 collective-permute-done.10.b1_ref
  262.4 2.9 %collective-permute-done.11.b2_ref = bf16[2,800,128]{2,1,0:T(8,128)(2,1)} collective-permute-done((bf16[2,800,128]{2,1,0:T(8,128)(2,1)S(1)}, bf16[2,800,128]{2,1,0:T(8,128)(2,1)}, u32[]{:S(2)}, u32[]{:S(2)}) %collective-permute-start.11) | collective-permute-done | bytes 409632 | tf_op jit(solution)/shard_map/ppermute | solution.py:30
  265.3 1.5 collective-permute-done.12.b3_ref
  266.8 6.2 %finish.1 = (bf16[400,4096]{1,0:T(8,128)(2,1)}, bf16[400,4096]{1,0:T(8,128)(2,1)}) custom-call(s32[8]{0:T(128)} %copy-done.16, bf16[4,800,128]{2,1,0:T(8,128)(2,1)} %copy-done.2, bf16[4,800,128]{2,1,0:T(8,128)(2,1)} %collective-permute-done.6.ar_ref, bf16[2,800,128]{2,1,0:T(8,128)(2,1)} %copy-done.5, bf16[2,800,128]{2,1,0:T(8,128)(2,1)} %collective-permute-done.10.b1_ref, ...), custom_call_target="tpu_custom_call" | custom-call | tf_op jit(solution)/shard_map/finish/pallas_call | solution.py:607
  (59 shorter events, 0.7 us)
Async XLA Ops:
  0.6 6.9 %copy-start.12 = (s32[1,1,1,8192]{3,2,1,0:T(1,128)S(1)}, s32[1,1,1,8192]{3,2,1,0:T(1,128)}, u32[]{:S(2)}) copy-start(s32[1,1,1,8192]{3,2,1,0:T(1,128)} %param.10) | copy-start | bytes 98308
  0.6 7.5 %copy-start.3 = (f32[1345,400]{0,1:T(8,128)S(1)}, f32[1345,400]{0,1:T(8,128)}, u32[]{:S(2)}) copy-start(f32[1345,400]{0,1:T(8,128)} %param.9) | copy-start | bytes 6456004
  0.7 36.6 %collective-permute-start = (bf16[4096,400]{0,1:T(8,128)(2,1)}, bf16[4096,400]{0,1:T(8,128)(2,1)}, u32[]{:S(2)}, u32[]{:S(2)}) collective-permute-start(bf16[4096,400]{0,1:T(8,128)(2,1)} %param.8), channel_id=1, source_target_pairs={{0,120},{8,0},{16,8},{24,16},{32,24},{40,32},{48,40},{56,48},{64,5... | collective-permute-start | bytes 9830408 | tf_op jit(solution)/shard_map/ppermute | solution.py:30
  8.2 2.2 copy-start.13
  8.2 2.8 %copy-start.14 = (s32[1,1,1,8192]{3,2,1,0:T(1,128)S(1)}, s32[1,1,1,8192]{3,2,1,0:T(1,128)}, u32[]{:S(2)}) copy-start(s32[1,1,1,8192]{3,2,1,0:T(1,128)} %param.11) | copy-start | bytes 98308
  11.6 14.9 %copy-start.15 = (s32[1,1,1,8192]{3,2,1,0:T(1,128)S(1)}, s32[1,1,1,8192]{3,2,1,0:T(1,128)}, u32[]{:S(2)}) copy-start(s32[1,1,1,8192]{3,2,1,0:T(1,128)} %param.12) | copy-start | bytes 98308
  87.7 63.0 %collective-permute-start.1 = (bf16[8,800,128]{2,1,0:T(8,128)(2,1)}, bf16[8,800,128]{2,1,0:T(8,128)(2,1)S(1)}, u32[]{:S(2)}, u32[]{:S(2)}) collective-permute-start(bf16[8,800,128]{2,1,0:T(8,128)(2,1)} %get-tuple-element.24), channel_id=1, source_target_pairs={{0,8},{8,16},{16,24},{24,32},{32,40},{40,48},{48,56},{56,64},{64,7... | collective-permute-start | bytes 4915208 | tf_op jit(solution)/shard_map/ppermute | solution.py:30
  87.8 65.9 %all-to-all-start.2 = ((bf16[4,1280,128]{2,1,0:T(8,128)(2,1)}), bf16[4,1280,128]{2,1,0:T(8,128)(2,1)S(1)}, u32[]{:S(2)}, u32[]{:S(2)}) async-start(bf16[4,1280,128]{2,1,0:T(8,128)(2,1)} %bitcast.42), calls=%async_computation.2 | async-start | bytes 2621440 | tf_op jit(solution)/shard_map/all_to_all | solution.py:635
  137.2 41.4 %collective-permute-start.7 = (bf16[8,800,128]{2,1,0:T(8,128)(2,1)}, bf16[8,800,128]{2,1,0:T(8,128)(2,1)}, u32[]{:S(2)}, u32[]{:S(2)}) collective-permute-start(bf16[8,800,128]{2,1,0:T(8,128)(2,1)} %get-tuple-element.28), channel_id=1, source_target_pairs={{0,8},{8,16},{16,24},{24,32},{32,40},{40,48},{48,56},{56,64},{64,7... | collective-permute-start | bytes 4915208 | tf_op jit(solution)/shard_map/ppermute | solution.py:30
  153.7 1.1 copy-start.1
  154.8 27.4 %all-to-all-start = ((bf16[4,1600,128]{2,1,0:T(8,128)(2,1)}), bf16[4,1600,128]{2,1,0:T(8,128)(2,1)S(1)}, u32[]{:S(2)}, u32[]{:S(2)}) async-start(bf16[4,1600,128]{2,1,0:T(8,128)(2,1)} %bitcast.40), calls=%async_computation | async-start | bytes 3276800 | tf_op jit(solution)/shard_map/all_to_all | solution.py:635
  169.0 7.0 %collective-permute-start.13 = (bf16[640,128]{1,0:T(8,128)(2,1)}, bf16[640,128]{1,0:T(8,128)(2,1)S(1)}, u32[]{:S(2)}, u32[]{:S(2)}) collective-permute-start(bf16[640,128]{1,0:T(8,128)(2,1)} %get-tuple-element.35), channel_id=1, source_target_pairs={{0,1},{1,0},{2,3},{3,2},{4,5},{5,4},{6,7},{7,6},{8,9},{9,8},{10,11... | collective-permute-start | bytes 491528 | tf_op jit(solution)/shard_map/ppermute | solution.py:30
  177.0 1.5 collective-permute-start.14
  178.6 9.8 %collective-permute-start.15 = (bf16[640,128]{1,0:T(8,128)(2,1)S(1)}, bf16[640,128]{1,0:T(8,128)(2,1)S(1)}, u32[]{:S(2)}, u32[]{:S(2)}) collective-permute-start(bf16[640,128]{1,0:T(8,128)(2,1)S(1)} %add_convert_fusion.3), channel_id=1, source_target_pairs={{0,16},{8,24},{16,0},{24,8},{32,48},{40,56},{48,32},{56,40},{64,80... | collective-permute-start | bytes 491528 | tf_op jit(solution)/shard_map/ppermute | solution.py:648
  182.2 1.2 copy-start
  183.3 31.4 %all-to-all-start.1 = ((bf16[4,1600,128]{2,1,0:T(8,128)(2,1)}), bf16[4,1600,128]{2,1,0:T(8,128)(2,1)}, u32[]{:S(2)}, u32[]{:S(2)}) async-start(bf16[4,1600,128]{2,1,0:T(8,128)(2,1)} %bitcast.39), calls=%async_computation.1 | async-start | bytes 3276800 | tf_op jit(solution)/shard_map/all_to_all | solution.py:635
  188.4 9.1 %collective-permute-start.16 = (bf16[640,128]{1,0:T(8,128)(2,1)S(1)}, bf16[640,128]{1,0:T(8,128)(2,1)S(1)}, u32[]{:S(2)}, u32[]{:S(2)}) collective-permute-start(bf16[640,128]{1,0:T(8,128)(2,1)S(1)} %add_convert_fusion.2), channel_id=1, source_target_pairs={{0,32},{8,40},{16,48},{24,56},{32,0},{40,8},{48,16},{56,24},{64,96... | collective-permute-start | bytes 491528 | tf_op jit(solution)/shard_map/ppermute | solution.py:648
  197.5 11.2 %collective-permute-start.17 = (bf16[640,128]{1,0:T(8,128)(2,1)S(1)}, bf16[640,128]{1,0:T(8,128)(2,1)S(1)}, u32[]{:S(2)}, u32[]{:S(2)}) collective-permute-start(bf16[640,128]{1,0:T(8,128)(2,1)S(1)} %add_convert_fusion.1), channel_id=1, source_target_pairs={{0,64},{8,72},{16,80},{24,88},{32,96},{40,104},{48,112},{56,120},{... | collective-permute-start | bytes 491528 | tf_op jit(solution)/shard_map/ppermute | solution.py:648
  208.7 23.9 %collective-permute-start.18 = (bf16[640,128]{1,0:T(8,128)(2,1)S(1)}, bf16[640,128]{1,0:T(8,128)(2,1)S(1)}, u32[]{:S(2)}, u32[]{:S(2)}) collective-permute-start(bf16[640,128]{1,0:T(8,128)(2,1)S(1)} %get-tuple-element.38), channel_id=1, source_target_pairs={{0,1},{1,0},{2,3},{3,2},{4,5},{5,4},{6,7},{7,6},{8,9},{9,8},{10,11... | collective-permute-start | bytes 491528 | tf_op jit(solution)/shard_map/ppermute | solution.py:30
  214.1 9.3 %collective-permute-start.2 = (bf16[800,128]{1,0:T(8,128)(2,1)}, bf16[800,128]{1,0:T(8,128)(2,1)S(1)}, u32[]{:S(2)}, u32[]{:S(2)}) collective-permute-start(bf16[800,128]{1,0:T(8,128)(2,1)} %get-tuple-element.26), channel_id=1, source_target_pairs={{0,1},{1,0},{2,3},{3,2},{4,5},{5,4},{6,7},{7,6},{8,9},{9,8},{10,11... | collective-permute-start | bytes 614408 | tf_op jit(solution)/shard_map/ppermute | solution.py:30
  217.1 16.2 %collective-permute-start.8 = (bf16[800,128]{1,0:T(8,128)(2,1)}, bf16[800,128]{1,0:T(8,128)(2,1)S(1)}, u32[]{:S(2)}, u32[]{:S(2)}) collective-permute-start(bf16[800,128]{1,0:T(8,128)(2,1)} %get-tuple-element.30), channel_id=1, source_target_pairs={{0,1},{1,0},{2,3},{3,2},{4,5},{5,4},{6,7},{7,6},{8,9},{9,8},{10,11... | collective-permute-start | bytes 614408 | tf_op jit(solution)/shard_map/ppermute | solution.py:30
  223.4 0.7 copy-start.11
  226.2 13.2 %copy-start.6 = (bf16[800,128]{1,0:T(8,128)(2,1)S(1)}, bf16[800,128]{1,0:T(8,128)(2,1)}, u32[]{:S(2)}) copy-start(bf16[800,128]{1,0:T(8,128)(2,1)} %update.2) | copy-start | bytes 614404
  226.2 11.8 %collective-permute-start.3 = (bf16[800,128]{1,0:T(8,128)(2,1)}, bf16[800,128]{1,0:T(8,128)(2,1)S(1)}, u32[]{:S(2)}, u32[]{:S(2)}) collective-permute-start(bf16[800,128]{1,0:T(8,128)(2,1)} %update.2), channel_id=1, source_target_pairs={{0,2},{2,4},{4,6},{6,0},{1,3},{3,5},{5,7},{7,1},{8,10},{10,12},{12... | collective-permute-start | bytes 614408 | tf_op jit(solution)/shard_map/ppermute | solution.py:30
  228.0 10.5 %collective-permute-start.4 = (bf16[800,128]{1,0:T(8,128)(2,1)}, bf16[800,128]{1,0:T(8,128)(2,1)S(1)}, u32[]{:S(2)}, u32[]{:S(2)}) collective-permute-start(bf16[800,128]{1,0:T(8,128)(2,1)} %update.2), channel_id=1, source_target_pairs={{0,6},{2,0},{4,2},{6,4},{1,7},{3,1},{5,3},{7,5},{8,14},{10,8},{12,... | collective-permute-start | bytes 614408 | tf_op jit(solution)/shard_map/ppermute | solution.py:30
  229.4 9.2 %collective-permute-start.5 = (bf16[800,128]{1,0:T(8,128)(2,1)}, bf16[800,128]{1,0:T(8,128)(2,1)S(1)}, u32[]{:S(2)}, u32[]{:S(2)}) collective-permute-start(bf16[800,128]{1,0:T(8,128)(2,1)} %update.2), channel_id=1, source_target_pairs={{0,4},{2,6},{4,0},{6,2},{1,5},{3,7},{5,1},{7,3},{8,12},{10,14},{12... | collective-permute-start | bytes 614408 | tf_op jit(solution)/shard_map/ppermute | solution.py:30
  231.6 8.9 %copy-start.16 = (s32[8]{0:T(128)}, s32[8]{0:T(128)S(1)}, u32[]{:S(2)}) copy-start(s32[8]{0:T(128)S(1)} %pad_add_fusion.place) | copy-start | bytes 100
  232.6 15.3 %collective-permute-start.19 = (bf16[2,640,128]{2,1,0:T(8,128)(2,1)S(1)}, bf16[2,640,128]{2,1,0:T(8,128)(2,1)}, u32[]{:S(2)}, u32[]{:S(2)}) collective-permute-start(bf16[2,640,128]{2,1,0:T(8,128)(2,1)S(1)} %pad_maximum_fusion.2), channel_id=1, source_target_pairs={{0,2},{2,4},{4,6},{6,0},{1,3},{3,5},{5,7},{7,1},{8,10},{10,12},{12... | collective-permute-start | bytes 983048 | tf_op jit(solution)/shard_map/ppermute | solution.py:30
  233.2 2.7 copy-start.10
  233.2 17.9 %collective-permute-start.20 = (bf16[2,640,128]{2,1,0:T(8,128)(2,1)S(1)}, bf16[2,640,128]{2,1,0:T(8,128)(2,1)}, u32[]{:S(2)}, u32[]{:S(2)}) collective-permute-start(bf16[2,640,128]{2,1,0:T(8,128)(2,1)S(1)} %pad_maximum_fusion.2), channel_id=1, source_target_pairs={{0,6},{2,0},{4,2},{6,4},{1,7},{3,1},{5,3},{7,5},{8,14},{10,8},{12,... | collective-permute-start | bytes 983048 | tf_op jit(solution)/shard_map/ppermute | solution.py:30
  238.0 9.7 %copy-start.7 = (bf16[800,128]{1,0:T(8,128)(2,1)S(1)}, bf16[800,128]{1,0:T(8,128)(2,1)}, u32[]{:S(2)}) copy-start(bf16[800,128]{1,0:T(8,128)(2,1)} %update.3) | copy-start | bytes 614404
  238.0 9.7 %collective-permute-start.9 = (bf16[800,128]{1,0:T(8,128)(2,1)}, bf16[800,128]{1,0:T(8,128)(2,1)S(1)}, u32[]{:S(2)}, u32[]{:S(2)}) collective-permute-start(bf16[800,128]{1,0:T(8,128)(2,1)} %update.3), channel_id=1, source_target_pairs={{0,1},{1,0},{2,3},{3,2},{4,5},{5,4},{6,7},{7,6},{8,9},{9,8},{10,11... | collective-permute-start | bytes 614408 | tf_op jit(solution)/shard_map/ppermute | solution.py:30
  238.5 0.7 copy-start.8
  238.7 0.7 copy-start.9
  240.5 20.7 %copy-start.2 = (bf16[4,800,128]{2,1,0:T(8,128)(2,1)}, bf16[4,800,128]{2,1,0:T(8,128)(2,1)S(1)}, u32[]{:S(2)}) copy-start(bf16[4,800,128]{2,1,0:T(8,128)(2,1)S(1)} %pad_maximum_fusion.a_ref) | copy-start | bytes 2457604
  240.5 26.3 %collective-permute-start.6 = (bf16[4,800,128]{2,1,0:T(8,128)(2,1)S(1)}, bf16[4,800,128]{2,1,0:T(8,128)(2,1)}, u32[]{:S(2)}, u32[]{:S(2)}) collective-permute-start(bf16[4,800,128]{2,1,0:T(8,128)(2,1)S(1)} %pad_maximum_fusion.a_ref), channel_id=1, source_target_pairs={{0,1},{1,0},{2,3},{3,2},{4,5},{5,4},{6,7},{7,6},{8,9},{9,8},{10,11... | collective-permute-start | bytes 2457608 | tf_op jit(solution)/shard_map/ppermute | solution.py:30
  244.3 12.3 %collective-permute-start.21 = (bf16[2,640,128]{2,1,0:T(8,128)(2,1)S(1)}, bf16[2,640,128]{2,1,0:T(8,128)(2,1)S(1)}, u32[]{:S(2)}, u32[]{:S(2)}) collective-permute-start(bf16[2,640,128]{2,1,0:T(8,128)(2,1)S(1)} %pad_maximum_fusion.2), channel_id=1, source_target_pairs={{0,4},{2,6},{4,0},{6,2},{1,5},{3,7},{5,1},{7,3},{8,12},{10,14},{12... | collective-permute-start | bytes 983048 | tf_op jit(solution)/shard_map/ppermute | solution.py:30
  247.8 13.4 %copy-start.5 = (bf16[2,800,128]{2,1,0:T(8,128)(2,1)}, bf16[2,800,128]{2,1,0:T(8,128)(2,1)S(1)}, u32[]{:S(2)}) copy-start(bf16[2,800,128]{2,1,0:T(8,128)(2,1)S(1)} %pad_maximum_fusion.1.b0_ref) | copy-start | bytes 1228804
  247.8 14.6 %collective-permute-start.10 = (bf16[2,800,128]{2,1,0:T(8,128)(2,1)S(1)}, bf16[2,800,128]{2,1,0:T(8,128)(2,1)}, u32[]{:S(2)}, u32[]{:S(2)}) collective-permute-start(bf16[2,800,128]{2,1,0:T(8,128)(2,1)S(1)} %pad_maximum_fusion.1.b0_ref), channel_id=1, source_target_pairs={{0,2},{2,4},{4,6},{6,0},{1,3},{3,5},{5,7},{7,1},{8,10},{10,12},{12... | collective-permute-start | bytes 1228808 | tf_op jit(solution)/shard_map/ppermute | solution.py:30
  247.9 17.4 %collective-permute-start.11 = (bf16[2,800,128]{2,1,0:T(8,128)(2,1)S(1)}, bf16[2,800,128]{2,1,0:T(8,128)(2,1)}, u32[]{:S(2)}, u32[]{:S(2)}) collective-permute-start(bf16[2,800,128]{2,1,0:T(8,128)(2,1)S(1)} %pad_maximum_fusion.1.b0_ref), channel_id=1, source_target_pairs={{0,6},{2,0},{4,2},{6,4},{1,7},{3,1},{5,3},{7,5},{8,14},{10,8},{12,... | collective-permute-start | bytes 1228808 | tf_op jit(solution)/shard_map/ppermute | solution.py:30
  251.1 15.7 %collective-permute-start.12 = (bf16[2,800,128]{2,1,0:T(8,128)(2,1)S(1)}, bf16[2,800,128]{2,1,0:T(8,128)(2,1)}, u32[]{:S(2)}, u32[]{:S(2)}) collective-permute-start(bf16[2,800,128]{2,1,0:T(8,128)(2,1)S(1)} %pad_maximum_fusion.1.b0_ref), channel_id=1, source_target_pairs={{0,4},{2,6},{4,0},{6,2},{1,5},{3,7},{5,1},{7,3},{8,12},{10,14},{12... | collective-permute-start | bytes 1228808 | tf_op jit(solution)/shard_map/ppermute | solution.py:30
  256.6 1.1 copy-start.4
